TPU v7x, 128 devices: a whole 4x4x4 slice. The times are simulated.
128 devices in a mesh: dp: 64 (over z, x_lo, y, core), rep: 2 (over x_hi).
Axes of the slice: x: 4 (x_hi: 2, x_lo: 2; x = x_hi * 2 + x_lo), y: 4, z: 4, core: 2. Of those that a mesh axis runs over, the one named last changes fastest.
Arguments:
- states: bfloat16 [2, 128, 256, 768], P(None, ('dp', 'rep')), may hold values from -24 to 24
- qkv_weight: bfloat16 [768, 2304], P('dp'), may hold values from -0.21875 to 0.21875
- query_bias: bfloat16 [768], P('dp'), may hold values from -3 to 3
- value_bias: bfloat16 [768], P('dp'), may hold values from -3 to 3
- out_weight: bfloat16 [768, 768], P('dp'), may hold values from -0.625 to 0.625
- out_bias: bfloat16 [768], P('dp'), may hold values from -3 to 3
- attn_gain: bfloat16 [768], P('dp'), may hold values from 0.099609375 to 1.8984375
- attn_shift: bfloat16 [768], P('dp'), may hold values from -3 to 3
- up_weight: bfloat16 [768, 3072], P('dp'), may hold values from -0.21875 to 0.21875
- up_bias: bfloat16 [3072], P('dp'), may hold values from -3 to 3
- down_weight: bfloat16 [3072, 768], P('dp'), may hold values from -0.109375 to 0.109375
- down_bias: bfloat16 [768], P('dp'), may hold values from -3 to 3
- ffn_gain: bfloat16 [768], P('dp'), may hold values from 0.099609375 to 1.8984375
- ffn_shift: bfloat16 [768], P('dp'), may hold values from -3 to 3
- out_grad: bfloat16 [2, 128, 256, 768], P(None, ('dp', 'rep')), may hold values from -6 to 6
- lengths: int32 [2, 128], P(None, ('dp', 'rep')), may hold values from 64 to 256, as said below
Outputs:
- encoded: bfloat16 [2, 128, 256, 768], P(None, ('dp', 'rep'))
- states_grad: float32 [2, 128, 256, 768], P(None, ('dp', 'rep'))
- grad_qkv_weight: float32 [768, 2304], P('dp')
- grad_query_bias: float32 [768], P('dp')
- grad_value_bias: float32 [768], P('dp')
- grad_out_weight: float32 [768, 768], P('dp')
- grad_out_bias: float32 [768], P('dp')
- grad_attn_gain: float32 [768], P('dp')
- grad_attn_shift: float32 [768], P('dp')
- grad_up_weight: float32 [768, 3072], P('dp')
- grad_up_bias: float32 [3072], P('dp')
- grad_down_weight: float32 [3072, 768], P('dp')
- grad_down_bias: float32 [768], P('dp')
- grad_ffn_gain: float32 [768], P('dp')
- grad_ffn_shift: float32 [768], P('dp')
Inputs may be any that keep to these rules, and one draw needn't show every extreme that they name: Slot [m, s] holds one sequence of lengths[m, s] tokens at its start; later key slots are padding. In every draw some slot is full (256) and some holds 64.
All inputs are finite; a program needn't handle non-finite values.
Results may differ from a plain program's by a relative error of at most 0.013.
The roundings to bfloat16 on the way count: a program that leaves them out, or rounds other values in their place, can miss the bound.
Values may be sent and summed in bfloat16 or wider, within the bound.
A program may use at most 128 MiB of HBM per device.

v0:
```python
import math

import jax
import jax.numpy as jnp
from jax import lax
from jax.sharding import PartitionSpec as P

HD = 64


epsilon = 1e-05


def layer_norm(hidden, gain, shift):
    center = hidden - jnp.mean(hidden, -1, keepdims=True)
    variance = jnp.mean(center * center, -1, keepdims=True)
    return center * lax.rsqrt(variance + epsilon) * gain + shift


def gelu_exact(value):
    return 0.5 * value * (1.0 + lax.erf(value * (1.0 / math.sqrt(2.0))))


def contract_rows(left, right):
    return lax.dot_general(
        left, right, (((0,), (0,)), ((), ())), preferred_element_type=jnp.float32
    )


def times_transposed(left, right):
    return lax.dot_general(
        left, right, (((1,), (1,)), ((), ())), preferred_element_type=jnp.float32
    )


def masked_scores(queries, key_rows, valid_keys):
    scores = jnp.einsum("bqhd,bkhd->bhqk", queries, key_rows, preferred_element_type=jnp.float32)
    scores = scores * (1.0 / math.sqrt(HD))
    return jnp.where(valid_keys[:, None, None, :], scores, -1000000000.0)


def column_sum(matrix):
    return jnp.sum(matrix.astype(jnp.float32), 0)


def forward(weights, states, valid_keys):
    (
        qkv_weight,
        query_bias,
        value_bias,
        out_weight,
        out_bias,
        attn_gain,
        attn_shift,
        up_weight,
        up_bias,
        down_weight,
        down_bias,
        ffn_gain,
        ffn_shift,
    ) = weights
    seq_count, length, width = states.shape
    head_count = width // HD
    shaped = (seq_count, length, head_count, HD)
    flat_rows = states.reshape(seq_count * length, width)
    joint_proj = jnp.dot(flat_rows, qkv_weight, preferred_element_type=jnp.float32)
    queries = (joint_proj[:, :width] + query_bias.astype(jnp.float32)).astype(jnp.bfloat16)
    key_rows = joint_proj[:, width : 2 * width].astype(jnp.bfloat16)
    values = (joint_proj[:, 2 * width :] + value_bias.astype(jnp.float32)).astype(jnp.bfloat16)
    scores = masked_scores(queries.reshape(shaped), key_rows.reshape(shaped), valid_keys)
    row_peak = jnp.max(scores, -1, keepdims=True)
    exponent = jnp.exp(scores - row_peak)
    row_total = jnp.sum(exponent, -1, keepdims=True)
    attention = (exponent / row_total).astype(jnp.bfloat16)
    log_total = row_peak + jnp.log(row_total)
    mixed_heads = jnp.einsum(
        "bhqk,bkhd->bqhd", attention, values.reshape(shaped), preferred_element_type=jnp.float32
    )
    mixed_heads = mixed_heads.reshape(seq_count * length, width).astype(jnp.bfloat16)
    branch = jnp.dot(mixed_heads, out_weight, preferred_element_type=jnp.float32) + out_bias.astype(
        jnp.float32
    )
    residual = flat_rows.astype(jnp.float32) + branch
    normed = layer_norm(residual, attn_gain.astype(jnp.float32), attn_shift.astype(jnp.float32))
    normed_low = normed.astype(jnp.bfloat16)
    pre_act = jnp.dot(normed_low, up_weight, preferred_element_type=jnp.float32) + up_bias.astype(
        jnp.float32
    )
    activation = gelu_exact(pre_act).astype(jnp.bfloat16)
    update = jnp.dot(
        activation, down_weight, preferred_element_type=jnp.float32
    ) + down_bias.astype(jnp.float32)
    second = normed + update
    encoded = layer_norm(second, ffn_gain.astype(jnp.float32), ffn_shift.astype(jnp.float32))
    saved_state = (
        flat_rows,
        queries,
        key_rows,
        values,
        log_total,
        mixed_heads,
        residual,
        normed_low,
        pre_act,
        activation,
        second,
        valid_keys,
    )
    return (encoded, saved_state)


def backward(weights, saved_state, cotangent):
    (
        qkv_weight,
        query_bias,
        value_bias,
        out_weight,
        out_bias,
        attn_gain,
        attn_shift,
        up_weight,
        up_bias,
        down_weight,
        down_bias,
        ffn_gain,
        ffn_shift,
    ) = weights
    (
        flat_rows,
        queries,
        key_rows,
        values,
        log_total,
        mixed_heads,
        residual,
        normed_low,
        pre_act,
        activation,
        second,
        valid_keys,
    ) = saved_state
    row_count, width = flat_rows.shape
    seq_count, length = valid_keys.shape
    shaped = (seq_count, length, width // HD, HD)
    scale = 1.0 / math.sqrt(HD)
    ignored, ffn_pull = jax.vjp(
        layer_norm, second, ffn_gain.astype(jnp.float32), ffn_shift.astype(jnp.float32)
    )
    grad_second, grad_ffn_gain, grad_ffn_shift = ffn_pull(cotangent)
    grad_update = grad_second.astype(jnp.bfloat16)
    grad_down = contract_rows(activation, grad_update)
    grad_down_bias = column_sum(grad_update)
    grad_activation = times_transposed(grad_update, down_weight)
    ignored, gelu_pull = jax.vjp(gelu_exact, pre_act)
    grad_pre = gelu_pull(grad_activation)[0].astype(jnp.bfloat16)
    grad_up = contract_rows(normed_low, grad_pre)
    grad_up_bias = column_sum(grad_pre)
    grad_normed = grad_second + times_transposed(grad_pre, up_weight)
    ignored, attn_pull = jax.vjp(
        layer_norm, residual, attn_gain.astype(jnp.float32), attn_shift.astype(jnp.float32)
    )
    grad_residual, grad_attn_gain, grad_attn_shift = attn_pull(grad_normed)
    grad_branch = grad_residual.astype(jnp.bfloat16)
    grad_out = contract_rows(mixed_heads, grad_branch)
    grad_out_bias = column_sum(grad_branch)
    grad_mixed = times_transposed(grad_branch, out_weight).astype(jnp.bfloat16).reshape(shaped)
    query_heads = queries.reshape(shaped)
    key_heads = key_rows.reshape(shaped)
    value_heads = values.reshape(shaped)
    scores = masked_scores(query_heads, key_heads, valid_keys)
    attention_full = jnp.exp(scores - log_total)
    attention_low = attention_full.astype(jnp.bfloat16)
    grad_attention = jnp.einsum(
        "bqhd,bkhd->bhqk", grad_mixed, value_heads, preferred_element_type=jnp.float32
    )
    grad_values = jnp.einsum(
        "bhqk,bqhd->bkhd", attention_low, grad_mixed, preferred_element_type=jnp.float32
    )
    grad_values = grad_values.reshape(row_count, width).astype(jnp.bfloat16)
    grad_scores = attention_full * (
        grad_attention - jnp.sum(attention_full * grad_attention, -1, keepdims=True)
    )
    grad_scores = grad_scores.astype(jnp.bfloat16)
    grad_queries = (
        jnp.einsum("bhqk,bkhd->bqhd", grad_scores, key_heads, preferred_element_type=jnp.float32)
        * scale
    )
    grad_queries = grad_queries.reshape(row_count, width).astype(jnp.bfloat16)
    grad_keys = (
        jnp.einsum("bhqk,bqhd->bkhd", grad_scores, query_heads, preferred_element_type=jnp.float32)
        * scale
    )
    grad_keys = grad_keys.reshape(row_count, width).astype(jnp.bfloat16)
    grad_joint = jnp.concatenate([grad_queries, grad_keys, grad_values], axis=1)
    grad_qkv = contract_rows(flat_rows, grad_joint)
    grad_query_bias = column_sum(grad_queries)
    grad_value_bias = column_sum(grad_values)
    input_grad = grad_residual + times_transposed(grad_joint, qkv_weight)
    gradients = (
        grad_qkv,
        grad_query_bias,
        grad_value_bias,
        grad_out,
        grad_out_bias,
        grad_attn_gain,
        grad_attn_shift,
        grad_up,
        grad_up_bias,
        grad_down,
        grad_down_bias,
        grad_ffn_gain,
        grad_ffn_shift,
    )
    return (gradients, input_grad)


def add_tuples(left, right):
    return tuple((left_item + right_item for left_item, right_item in zip(left, right)))


def local(
    states,
    qkv_weight,
    query_bias,
    value_bias,
    out_weight,
    out_bias,
    attn_gain,
    attn_shift,
    up_weight,
    up_bias,
    down_weight,
    down_bias,
    ffn_gain,
    ffn_shift,
    out_grad,
    lengths,
):
    shards = (
        qkv_weight,
        query_bias,
        value_bias,
        out_weight,
        out_bias,
        attn_gain,
        attn_shift,
        up_weight,
        up_bias,
        down_weight,
        down_bias,
        ffn_gain,
        ffn_shift,
    )
    micro_count, seq_count, length, width = states.shape
    positions = jnp.arange(length, dtype=jnp.int32)
    valid_all = positions[None, None, :] < lengths[:, :, None]
    encoded_list = []
    input_list = []
    totals = None
    for step_index in range(micro_count):
        gathered = (
            lax.all_gather(shards[0], "dp", axis=0, tiled=True),
            lax.all_gather(shards[1], "dp", axis=0, tiled=True),
            lax.all_gather(shards[2], "dp", axis=0, tiled=True),
            lax.all_gather(shards[3], "dp", axis=0, tiled=True),
            lax.all_gather(shards[4], "dp", axis=0, tiled=True),
            lax.all_gather(shards[5], "dp", axis=0, tiled=True),
            lax.all_gather(shards[6], "dp", axis=0, tiled=True),
            lax.all_gather(shards[7], "dp", axis=0, tiled=True),
            lax.all_gather(shards[8], "dp", axis=0, tiled=True),
            lax.all_gather(shards[9], "dp", axis=0, tiled=True),
            lax.all_gather(shards[10], "dp", axis=0, tiled=True),
            lax.all_gather(shards[11], "dp", axis=0, tiled=True),
            lax.all_gather(shards[12], "dp", axis=0, tiled=True),
        )
        encoded, saved_state = forward(gathered, states[step_index], valid_all[step_index])
        gathered = (
            lax.all_gather(shards[0], "dp", axis=0, tiled=True),
            lax.all_gather(shards[1], "dp", axis=0, tiled=True),
            lax.all_gather(shards[2], "dp", axis=0, tiled=True),
            lax.all_gather(shards[3], "dp", axis=0, tiled=True),
            lax.all_gather(shards[4], "dp", axis=0, tiled=True),
            lax.all_gather(shards[5], "dp", axis=0, tiled=True),
            lax.all_gather(shards[6], "dp", axis=0, tiled=True),
            lax.all_gather(shards[7], "dp", axis=0, tiled=True),
            lax.all_gather(shards[8], "dp", axis=0, tiled=True),
            lax.all_gather(shards[9], "dp", axis=0, tiled=True),
            lax.all_gather(shards[10], "dp", axis=0, tiled=True),
            lax.all_gather(shards[11], "dp", axis=0, tiled=True),
            lax.all_gather(shards[12], "dp", axis=0, tiled=True),
        )
        cotangent = out_grad[step_index].reshape(seq_count * length, width).astype(jnp.float32)
        gradients, input_grad = backward(gathered, saved_state, cotangent)
        encoded_list.append(encoded.reshape(seq_count, length, width).astype(jnp.bfloat16))
        input_list.append(input_grad.reshape(seq_count, length, width))
        owned = (
            lax.psum_scatter(gradients[0], "dp", scatter_dimension=0, tiled=True),
            lax.psum_scatter(gradients[1], "dp", scatter_dimension=0, tiled=True),
            lax.psum_scatter(gradients[2], "dp", scatter_dimension=0, tiled=True),
            lax.psum_scatter(gradients[3], "dp", scatter_dimension=0, tiled=True),
            lax.psum_scatter(gradients[4], "dp", scatter_dimension=0, tiled=True),
            lax.psum_scatter(gradients[5], "dp", scatter_dimension=0, tiled=True),
            lax.psum_scatter(gradients[6], "dp", scatter_dimension=0, tiled=True),
            lax.psum_scatter(gradients[7], "dp", scatter_dimension=0, tiled=True),
            lax.psum_scatter(gradients[8], "dp", scatter_dimension=0, tiled=True),
            lax.psum_scatter(gradients[9], "dp", scatter_dimension=0, tiled=True),
            lax.psum_scatter(gradients[10], "dp", scatter_dimension=0, tiled=True),
            lax.psum_scatter(gradients[11], "dp", scatter_dimension=0, tiled=True),
            lax.psum_scatter(gradients[12], "dp", scatter_dimension=0, tiled=True),
        )
        totals = owned if totals is None else add_tuples(totals, owned)
    final = lax.psum(totals, "rep")
    return (jnp.stack(encoded_list), jnp.stack(input_list)) + tuple(final)


def solution(mesh):
    return jax.shard_map(
        local,
        mesh=mesh,
        in_specs=(
            P(None, ("dp", "rep"), None, None),
            P("dp", None),
            P("dp"),
            P("dp"),
            P("dp", None),
            P("dp"),
            P("dp"),
            P("dp"),
            P("dp", None),
            P("dp"),
            P("dp", None),
            P("dp"),
            P("dp"),
            P("dp"),
            P(None, ("dp", "rep"), None, None),
            P(None, ("dp", "rep")),
        ),
        out_specs=(
            P(None, ("dp", "rep"), None, None),
            P(None, ("dp", "rep"), None, None),
            P("dp", None),
            P("dp"),
            P("dp"),
            P("dp", None),
            P("dp"),
            P("dp"),
            P("dp"),
            P("dp", None),
            P("dp"),
            P("dp", None),
            P("dp"),
            P("dp"),
            P("dp"),
        ),
        check_vma=False,
    )
```

profile of v0, /device:TPU:1, one launch (start us, length us, event | category | flops | bytes accessed | tf_op | source)
XLA Modules:
  0.0 1698.1 jit_solution(5767361236564778088)
XLA Ops:
  20.3 277.1 %all-reduce.26 = (bf16[768]{0:T(1024)(128)(2,1)S(1)}, bf16[768]{0:T(1024)(128)(2,1)S(1)}, bf16[768]{0:T(1024)(128)(2,1)S(1)}, bf16[768]{0:T(1024)(128)(2,1)S(1)}...) all-reduce(bf16[768]{0:T(1024)(128)(2,1)S(1)} %dynamic-update-slice, ...), channel_id=1, replica_groups=mesh['dp'=64,'rep'=2] {'dp'}, use_global_device_ids=true, to_apply=%add | all-reduce | flops 9216 | bytes 36864
  301.6 3.1 reshape.469
  304.7 4.9 reshape.467
  309.7 2.4 fusion.54
  316.3 2.1 fusion.57
  320.0 2.1 fusion.44
  337.7 8.0 reshape.471
  345.7 5.7 convolution_add_fusion.2
  351.4 90.1 %all-gather.8.cloned.1.call-done = bf16[3072,768]{1,0:T(8,128)(2,1)} async-done(((bf16[48,768]{1,0:T(8,128)(2,1)}), bf16[3072,768]{1,0:T(8,128)(2,1)}) %all-gather.8.cloned.1.call-update) | async-done | bytes 4718608 | tf_op jit(solution)/shard_map/all_gather | solution.py:271
  441.5 5.2 fusion.87
  454.5 3.4 convert_reduce_fusion
  460.1 3.4 convert_reduce_fusion.1
  463.5 2.4 multiply_reduce_fusion.3
  466.0 2.0 fusion.77
  473.6 3.5 convert_reduce_fusion.8
  486.7 2.4 convert_reduce_fusion.9
  494.0 3.9 add_bitcast_fusion
  498.9 2.9 fusion.89
  501.9 4.8 convolution_add_fusion
  512.1 5.3 convolution_add_fusion.1
  517.4 166.3 %fusion.76 = (f32[16,3072]{1,0:T(8,128)}, f32[16,768]{1,0:T(8,128)}) fusion(f32[768,3072]{1,0:T(8,128)} %convolution_add_fusion.1, f32[768,768]{1,0:T(8,128)} %convolution_add_fusion.4), kind=kCustom, calls=%all-reduce-scatter.2 | all-reduce-scatter fusion | flops 3932161 | bytes 12042752
  684.6 2.0 collective-permute-start.31
  686.6 2.0 collective-permute-start.30
  694.4 12.6 collective-permute-done.31
  710.5 2.0 collective-permute-start.25
  716.4 6.4 collective-permute-start.22
  722.9 3.6 collective-permute-start.21
  730.2 9.0 collective-permute-start.20
  739.2 4.8 collective-permute-start.19
  745.9 2.7 collective-permute-start.17
  748.6 2.4 collective-permute-start.16
  751.1 3.5 fusion.16
  756.0 5.4 collective-permute-start.14
  761.4 5.2 collective-permute-start.13
  766.6 2.2 collective-permute-start.12
  768.8 3.1 collective-permute-start.11
  773.8 43.9 %concatenate.9 = f32[268,3072]{1,0:T(8,128)} concatenate(f32[12,3072]{1,0:T(8,128)} %collective-permute-done.31, f32[16,3072]{1,0:T(8,128)} %collective-permute-done.30, f32[16,3072]{1,0:T(8,128)} %collective-permute-done.29, f32[16,3072]{1,0:T(8,128)} %collective-permute-done.28, f32[16,3072]{1,0:T(8,128)} %collective-permute-done.27, f32[16,3072]{1,0:T(8,128)} %collective-permute-done.26, ...), dimensions={0} | concatenate | bytes 6586368
  819.4 3.6 collective-permute-start.10
  823.0 245.2 %all-reduce.31.cloned.1.call-done = f32[768,2304]{0,1:T(8,128)} async-done(((f32[768,2304]{0,1:T(8,128)}), f32[768,2304]{0,1:T(8,128)}) %all-reduce.31.cloned.1.call-update) | async-done | bytes 7077904
  1068.2 3.1 constant_dynamic-slice_fusion.2
  1071.3 294.7 %reduce-scatter.7.cloned.1.call-done = f32[48,768]{1,0:T(8,128)} async-done(((f32[3072,768]{1,0:T(8,128)}), f32[48,768]{1,0:T(8,128)}) %reduce-scatter.7.cloned.1.call-update) | async-done | bytes 147472 | tf_op jit(solution)/shard_map/reduce_scatter | solution.py:306
  1372.9 2.6 fusion.17
  1377.2 7.3 collective-permute-start.3
  1385.9 4.0 collective-permute-start.1
  1393.5 269.2 %all-reduce.23 = (f32[768]{0:T(1024)S(1)}, f32[768]{0:T(1024)S(1)}, f32[768]{0:T(1024)S(1)}, f32[768]{0:T(1024)S(1)}, f32[768]{0:T(1024)S(1)}, /*index=5*/f32[30...) all-reduce(f32[768]{0:T(1024)S(1)} %reshape.437, ...), channel_id=16, replica_groups=mesh['dp'=64,'rep'=2] {'dp'}, use_global_device_ids=true, to_apply=%region_26.27.clone | all-reduce | flops 9216 | bytes 73728
  1663.3 11.1 concatenate.8
  1675.4 10.0 all-reduce.24
  1685.3 2.3 copy.89
  (403 shorter events, 114.3 us)
Async XLA Ops:
  7.2 294.4 %all-gather.12.cloned.1.call-start = ((), (), s32[]{:S(2)}) async-start(), calls=%async_computation.4 | async-start | bytes 1597440 | tf_op jit(solution)/shard_map/all_gather | solution.py:265
  7.9 296.8 %all-gather.10.cloned.1.call-start = ((), (), s32[]{:S(2)}) async-start(), calls=%async_computation.3 | async-start | bytes 4792320 | tf_op jit(solution)/shard_map/all_gather | solution.py:262
  8.7 329.0 %all-gather.14.cloned.1.call-start = ((), (), s32[]{:S(2)}) async-start(), calls=%async_computation.5 | async-start | bytes 6389760 | tf_op jit(solution)/shard_map/all_gather | solution.py:269
  9.4 432.0 %all-gather.8.cloned.1.call-start = ((), (), s32[]{:S(2)}) async-start(), calls=%async_computation.1 | async-start | bytes 4792320 | tf_op jit(solution)/shard_map/all_gather | solution.py:271
  10.0 1058.3 %all-reduce.31.cloned.1.call-start = ((), (), s32[]{:S(2)}) async-start(), calls=%async_computation.6 | async-start | bytes 14155776
  330.2 135.8 %copy-start.70 = (f32[256]{0:T(256)}, f32[256]{0:T(256)S(1)}, u32[]{:S(2)}) copy-start(f32[256]{0:T(256)S(1)} %broadcast_multiply_fusion.3) | copy-start | bytes 3076
  498.0 868.0 %reduce-scatter.7.cloned.1.call-start = ((), (), s32[]{:S(2)}) async-start(), calls=%async_computation.2 | async-start | bytes 9584640 | tf_op jit(solution)/shard_map/reduce_scatter | solution.py:306
  506.7 1178.6 %all-reduce.33.cloned.1.call-start = ((), (), s32[]{:S(2)}) async-start(), calls=%async_computation.7 | async-start | bytes 3047424 | tf_op jit(solution)/shard_map/psum | solution.py:312
  517.4 233.7 %copy-start.3 = (bf16[768,2304]{1,0:T(8,128)(2,1)S(1)}, bf16[768,2304]{1,0:T(8,128)(2,1)}, u32[]{:S(2)}) copy-start(bf16[768,2304]{1,0:T(8,128)(2,1)} %copy-done.2) | copy-start | bytes 10616836
  684.6 22.5 %collective-permute-start.31 = (f32[12,3072]{1,0:T(8,128)S(1)}, f32[12,3072]{1,0:T(8,128)}, u32[]{:S(2)}, u32[]{:S(2)}) collective-permute-start(f32[12,3072]{1,0:T(8,128)S(1)} %slice.59), channel_id=1, source_target_pairs={{0,32},{2,34},{4,36},{6,38},{8,40},{10,42},{12,44},{14,46},{16,48}... | collective-permute-start | bytes 442376
  686.6 24.0 %collective-permute-start.30 = (f32[16,3072]{1,0:T(8,128)}, f32[16,3072]{1,0:T(8,128)}, u32[]{:S(2)}, u32[]{:S(2)}) collective-permute-start(f32[16,3072]{1,0:T(8,128)} %get-tuple-element.109), channel_id=1, source_target_pairs={{0,30},{2,32},{4,34},{6,36},{8,38},{10,40},{12,42},{14,44},{16,46}... | collective-permute-start | bytes 589832
  688.6 24.0 %collective-permute-start.29 = (f32[16,3072]{1,0:T(8,128)}, f32[16,3072]{1,0:T(8,128)}, u32[]{:S(2)}, u32[]{:S(2)}) collective-permute-start(f32[16,3072]{1,0:T(8,128)} %get-tuple-element.109), channel_id=1, source_target_pairs={{0,28},{2,30},{4,32},{6,34},{8,36},{10,38},{12,40},{14,42},{16,44}... | collective-permute-start | bytes 589832
  690.5 24.0 %collective-permute-start.28 = (f32[16,3072]{1,0:T(8,128)}, f32[16,3072]{1,0:T(8,128)}, u32[]{:S(2)}, u32[]{:S(2)}) collective-permute-start(f32[16,3072]{1,0:T(8,128)} %get-tuple-element.109), channel_id=1, source_target_pairs={{0,26},{2,28},{4,30},{6,32},{8,34},{10,36},{12,38},{14,40},{16,42}... | collective-permute-start | bytes 589832
  692.5 24.0 %collective-permute-start.27 = (f32[16,3072]{1,0:T(8,128)}, f32[16,3072]{1,0:T(8,128)}, u32[]{:S(2)}, u32[]{:S(2)}) collective-permute-start(f32[16,3072]{1,0:T(8,128)} %get-tuple-element.109), channel_id=1, source_target_pairs={{0,24},{2,26},{4,28},{6,30},{8,32},{10,34},{12,36},{14,38},{16,40}... | collective-permute-start | bytes 589832
  707.1 15.8 collective-permute-start.26
  710.5 19.7 %collective-permute-start.25 = (f32[16,3072]{1,0:T(8,128)}, f32[16,3072]{1,0:T(8,128)}, u32[]{:S(2)}, u32[]{:S(2)}) collective-permute-start(f32[16,3072]{1,0:T(8,128)} %get-tuple-element.109), channel_id=1, source_target_pairs={{0,20},{2,22},{4,24},{6,26},{8,28},{10,30},{12,32},{14,34},{16,36}... | collective-permute-start | bytes 589832
  712.5 26.7 %collective-permute-start.24 = (f32[16,3072]{1,0:T(8,128)}, f32[16,3072]{1,0:T(8,128)}, u32[]{:S(2)}, u32[]{:S(2)}) collective-permute-start(f32[16,3072]{1,0:T(8,128)} %get-tuple-element.109), channel_id=1, source_target_pairs={{0,18},{2,20},{4,22},{6,24},{8,26},{10,28},{12,30},{14,32},{16,34}... | collective-permute-start | bytes 589832
  714.5 29.5 %collective-permute-start.23 = (f32[16,3072]{1,0:T(8,128)}, f32[16,3072]{1,0:T(8,128)}, u32[]{:S(2)}, u32[]{:S(2)}) collective-permute-start(f32[16,3072]{1,0:T(8,128)} %get-tuple-element.109), channel_id=1, source_target_pairs={{0,16},{2,18},{4,20},{6,22},{8,24},{10,26},{12,28},{14,30},{16,32}... | collective-permute-start | bytes 589832
  716.4 29.5 %collective-permute-start.22 = (f32[16,3072]{1,0:T(8,128)}, f32[16,3072]{1,0:T(8,128)}, u32[]{:S(2)}, u32[]{:S(2)}) collective-permute-start(f32[16,3072]{1,0:T(8,128)} %get-tuple-element.109), channel_id=1, source_target_pairs={{0,14},{2,16},{4,18},{6,20},{8,22},{10,24},{12,26},{14,28},{16,30}... | collective-permute-start | bytes 589832
  722.9 25.8 %collective-permute-start.21 = (f32[16,3072]{1,0:T(8,128)}, f32[16,3072]{1,0:T(8,128)}, u32[]{:S(2)}, u32[]{:S(2)}) collective-permute-start(f32[16,3072]{1,0:T(8,128)} %get-tuple-element.109), channel_id=1, source_target_pairs={{0,12},{2,14},{4,16},{6,18},{8,20},{10,22},{12,24},{14,26},{16,28}... | collective-permute-start | bytes 589832
  730.2 25.8 %collective-permute-start.20 = (f32[16,3072]{1,0:T(8,128)}, f32[16,3072]{1,0:T(8,128)}, u32[]{:S(2)}, u32[]{:S(2)}) collective-permute-start(f32[16,3072]{1,0:T(8,128)} %get-tuple-element.109), channel_id=1, source_target_pairs={{0,10},{2,12},{4,14},{6,16},{8,18},{10,20},{12,22},{14,24},{16,26}... | collective-permute-start | bytes 589832
  739.2 22.2 %collective-permute-start.19 = (f32[16,3072]{1,0:T(8,128)}, f32[16,3072]{1,0:T(8,128)}, u32[]{:S(2)}, u32[]{:S(2)}) collective-permute-start(f32[16,3072]{1,0:T(8,128)} %get-tuple-element.109), channel_id=1, source_target_pairs={{0,8},{2,10},{4,12},{6,14},{8,16},{10,18},{12,20},{14,22},{16,24},... | collective-permute-start | bytes 589832
  744.0 22.7 %collective-permute-start.18 = (f32[16,3072]{1,0:T(8,128)}, f32[16,3072]{1,0:T(8,128)}, u32[]{:S(2)}, u32[]{:S(2)}) collective-permute-start(f32[16,3072]{1,0:T(8,128)} %get-tuple-element.109), channel_id=1, source_target_pairs={{0,6},{2,8},{4,10},{6,12},{8,14},{10,16},{12,18},{14,20},{16,22},{... | collective-permute-start | bytes 589832
  745.9 22.9 %collective-permute-start.17 = (f32[16,3072]{1,0:T(8,128)}, f32[16,3072]{1,0:T(8,128)}, u32[]{:S(2)}, u32[]{:S(2)}) collective-permute-start(f32[16,3072]{1,0:T(8,128)} %get-tuple-element.109), channel_id=1, source_target_pairs={{0,4},{2,6},{4,8},{6,10},{8,12},{10,14},{12,16},{14,18},{16,20},{1... | collective-permute-start | bytes 589832
  748.6 23.3 %collective-permute-start.16 = (f32[16,3072]{1,0:T(8,128)}, f32[16,3072]{1,0:T(8,128)}, u32[]{:S(2)}, u32[]{:S(2)}) collective-permute-start(f32[16,3072]{1,0:T(8,128)} %get-tuple-element.109), channel_id=1, source_target_pairs={{0,2},{2,4},{4,6},{6,8},{8,10},{10,12},{12,14},{14,16},{16,18},{18... | collective-permute-start | bytes 589832
  756.0 610.0 %collective-permute-start.14 = (f32[16,768]{1,0:T(8,128)}, f32[16,768]{1,0:T(8,128)}, u32[]{:S(2)}, u32[]{:S(2)}) collective-permute-start(f32[16,768]{1,0:T(8,128)} %get-tuple-element.110), channel_id=1, source_target_pairs={{0,30},{2,32},{4,34},{6,36},{8,38},{10,40},{12,42},{14,44},{16,46}... | collective-permute-start | bytes 147464
  761.4 606.0 %collective-permute-start.13 = (f32[16,768]{1,0:T(8,128)}, f32[16,768]{1,0:T(8,128)}, u32[]{:S(2)}, u32[]{:S(2)}) collective-permute-start(f32[16,768]{1,0:T(8,128)} %get-tuple-element.110), channel_id=1, source_target_pairs={{0,28},{2,30},{4,32},{6,34},{8,36},{10,38},{12,40},{14,42},{16,44}... | collective-permute-start | bytes 147464
  766.6 602.1 %collective-permute-start.12 = (f32[16,768]{1,0:T(8,128)}, f32[16,768]{1,0:T(8,128)}, u32[]{:S(2)}, u32[]{:S(2)}) collective-permute-start(f32[16,768]{1,0:T(8,128)} %get-tuple-element.110), channel_id=1, source_target_pairs={{0,26},{2,28},{4,30},{6,32},{8,34},{10,36},{12,38},{14,40},{16,42}... | collective-permute-start | bytes 147464
  768.8 601.2 %collective-permute-start.11 = (f32[16,768]{1,0:T(8,128)}, f32[16,768]{1,0:T(8,128)}, u32[]{:S(2)}, u32[]{:S(2)}) collective-permute-start(f32[16,768]{1,0:T(8,128)} %get-tuple-element.110), channel_id=1, source_target_pairs={{0,24},{2,26},{4,28},{6,30},{8,32},{10,34},{12,36},{14,38},{16,40}... | collective-permute-start | bytes 147464
  771.9 47.5 %collective-permute-start.15 = (f32[12,768]{1,0:T(8,128)}, f32[12,768]{1,0:T(8,128)}, u32[]{:S(2)}, u32[]{:S(2)}) collective-permute-start(f32[12,768]{1,0:T(8,128)} %slice.58), channel_id=1, source_target_pairs={{0,32},{2,34},{4,36},{6,38},{8,40},{10,42},{12,44},{14,46},{16,48}... | collective-permute-start | bytes 110600
  817.7 555.2 %copy-start.101 = (f32[256]{0:T(256)S(1)}, f32[256]{0:T(256)}, u32[]{:S(2)}) copy-start(f32[256]{0:T(256)} %copy-done.100) | copy-start | bytes 3076
  819.4 552.0 %collective-permute-start.10 = (f32[16,768]{1,0:T(8,128)}, f32[16,768]{1,0:T(8,128)}, u32[]{:S(2)}, u32[]{:S(2)}) collective-permute-start(f32[16,768]{1,0:T(8,128)} %get-tuple-element.110), channel_id=1, source_target_pairs={{0,22},{2,24},{4,26},{6,28},{8,30},{10,32},{12,34},{14,36},{16,38}... | collective-permute-start | bytes 147464
  1366.0 25.9 %copy-start.55 = (f32[1,1,256,768]{3,2,1,0:T(8,128)S(1)}, f32[1,1,256,768]{3,2,1,0:T(8,128)}, u32[]{:S(2)}) copy-start(f32[1,1,256,768]{3,2,1,0:T(8,128)} %fusion.16) | copy-start | bytes 2359300
  1366.0 9.8 collective-permute-start.9
  1367.4 9.8 collective-permute-start.8
  1368.7 15.8 collective-permute-start.7
  1370.1 15.8 collective-permute-start.6
  1371.4 18.5 %collective-permute-start.5 = (f32[16,768]{1,0:T(8,128)}, f32[16,768]{1,0:T(8,128)S(1)}, u32[]{:S(2)}, u32[]{:S(2)}) collective-permute-start(f32[16,768]{1,0:T(8,128)} %get-tuple-element.110), channel_id=1, source_target_pairs={{0,12},{2,14},{4,16},{6,18},{8,20},{10,22},{12,24},{14,26},{16,28}... | collective-permute-start | bytes 147464
  1375.7 17.7 %copy-start.79 = (f32[768]{0:T(1024)S(1)}, f32[768]{0:T(1024)}, u32[]{:S(2)}) copy-start(f32[768]{0:T(1024)} %get-tuple-element.119) | copy-start | bytes 9220
  1375.7 17.7 %copy-start.80 = (f32[768]{0:T(1024)S(1)}, f32[768]{0:T(1024)}, u32[]{:S(2)}) copy-start(f32[768]{0:T(1024)} %get-tuple-element.121) | copy-start | bytes 9220
  1375.7 17.7 %copy-start.82 = (f32[768]{0:T(1024)S(1)}, f32[768]{0:T(1024)}, u32[]{:S(2)}) copy-start(f32[768]{0:T(1024)} %add.369) | copy-start | bytes 9220
  1375.7 298.7 %copy-start.40 = (bf16[1,1,256,768]{3,2,1,0:T(8,128)(2,1)S(1)}, bf16[1,1,256,768]{3,2,1,0:T(8,128)(2,1)}, u32[]{:S(2)}) copy-start(bf16[1,1,256,768]{3,2,1,0:T(8,128)(2,1)} %get-tuple-element.136) | copy-start | bytes 1179652
  1375.7 298.7 %copy-start.41 = (bf16[1,1,256,768]{3,2,1,0:T(8,128)(2,1)S(1)}, bf16[1,1,256,768]{3,2,1,0:T(8,128)(2,1)}, u32[]{:S(2)}) copy-start(bf16[1,1,256,768]{3,2,1,0:T(8,128)(2,1)} %get-tuple-element.137) | copy-start | bytes 1179652
  1375.8 287.5 %collective-permute-start.4 = (f32[16,768]{1,0:T(8,128)}, f32[16,768]{1,0:T(8,128)S(1)}, u32[]{:S(2)}, u32[]{:S(2)}) collective-permute-start(f32[16,768]{1,0:T(8,128)} %get-tuple-element.110), channel_id=1, source_target_pairs={{0,10},{2,12},{4,14},{6,16},{8,18},{10,20},{12,22},{14,24},{16,26}... | collective-permute-start | bytes 147464
  1377.2 286.1 %collective-permute-start.3 = (f32[16,768]{1,0:T(8,128)}, f32[16,768]{1,0:T(8,128)S(1)}, u32[]{:S(2)}, u32[]{:S(2)}) collective-permute-start(f32[16,768]{1,0:T(8,128)} %get-tuple-element.110), channel_id=1, source_target_pairs={{0,8},{2,10},{4,12},{6,14},{8,16},{10,18},{12,20},{14,22},{16,24},... | collective-permute-start | bytes 147464
  1384.6 278.7 %collective-permute-start.2 = (f32[16,768]{1,0:T(8,128)}, f32[16,768]{1,0:T(8,128)S(1)}, u32[]{:S(2)}, u32[]{:S(2)}) collective-permute-start(f32[16,768]{1,0:T(8,128)} %get-tuple-element.110), channel_id=1, source_target_pairs={{0,6},{2,8},{4,10},{6,12},{8,14},{10,16},{12,18},{14,20},{16,22},{... | collective-permute-start | bytes 147464
  1385.9 277.4 %collective-permute-start.1 = (f32[16,768]{1,0:T(8,128)}, f32[16,768]{1,0:T(8,128)S(1)}, u32[]{:S(2)}, u32[]{:S(2)}) collective-permute-start(f32[16,768]{1,0:T(8,128)} %get-tuple-element.110), channel_id=1, source_target_pairs={{0,4},{2,6},{4,8},{6,10},{8,12},{10,14},{12,16},{14,18},{16,20},{1... | collective-permute-start | bytes 147464
  1389.9 273.4 %collective-permute-start = (f32[16,768]{1,0:T(8,128)}, f32[16,768]{1,0:T(8,128)S(1)}, u32[]{:S(2)}, u32[]{:S(2)}) collective-permute-start(f32[16,768]{1,0:T(8,128)} %get-tuple-element.110), channel_id=1, source_target_pairs={{0,2},{2,4},{4,6},{6,8},{8,10},{10,12},{12,14},{14,16},{16,18},{18... | collective-permute-start | bytes 147464
  (99 other events, 473.5 us)
Sparse Core Ops, SparseCore 0:
  9.7 106.5 all-gather.11
  118.0 106.0 all-gather.9
  225.8 107.9 all-gather.13
  335.3 106.1 all-gather.7
  498.1 570.1 all-reduce.30
  1070.6 295.2 reduce-scatter.6
  1369.3 66.5 all-reduce.32
where the time goes:
time: 1720 us; the launch traced here: 1700 us
  blocking collectives  722 us (42%)
  waiting for transfers between devices  647 us (38%)
  local copies, waits for them, and re-layouts  116 us (7%)
  starting transfers between devices  93.1 us (5%)
  matrix products  77.4 us (5%)
  other arithmetic  23.3 us (1%)
  between operations  19.2 us (1%)
    unnamed x3, blocking collectives  713 us
    reduce_scatter x1, waiting for transfers between devices, local(): lax.psum_scatter(gradients[9], 'dp', scatter_dimension=0, tiled=True)  295 us
    unnamed x40, waiting for transfers between devices  262 us
    unnamed x257, local copies, waits for them, and re-layouts  105 us
    unnamed x33, starting transfers between devices  92.7 us
    all_gather x1, waiting for transfers between devices, local(): lax.all_gather(shards[9], 'dp', axis=0, tiled=True)  90.1 us
  transfers between devices with their start and end apart: 39, of which 5 were waited for; matrix products, arithmetic and copies ran while one was open for 18% of the time, Pallas kernels for 0%

commit v1 on v0

--- a/solution.py
+++ b/solution.py
@@ -1,9 +1,377 @@
+import functools
+import itertools
 import math
 
 import jax
 import jax.numpy as jnp
 from jax import lax
+from jax.experimental import pallas as pl
+from jax.experimental.pallas import tpu as pltpu
 from jax.sharding import PartitionSpec as P
+
+MESH = pl.DeviceIdType.MESH
+BF = jnp.bfloat16
+F32 = jnp.float32
+WIDTH = 768
+UNIT = 48
+LANES = 128
+PARTS = 6
+
+ORDERS = (
+    ("z1", "z3", "y1", "y3", "x1"),
+    ("y1", "y3", "z1", "z3", "x3"),
+    ("y3", "z1", "z3", "x1", "y1"),
+    ("y1", "z3", "x1", "z1", "y3"),
+    ("y1", "z3", "x3", "y3", "z1"),
+    ("z1", "y3", "x3", "y1", "z3"),
+)
+
+
+def position():
+    dp = lax.axis_index("dp")
+    rep = lax.axis_index("rep")
+    return {"core": dp % 2, "y": (dp // 2) % 4, "z": dp // 16, "x": rep * 2 + (dp // 8) % 2}
+
+
+def device_of(place):
+    dp = ((place["z"] * 2 + place["x"] % 2) * 4 + place["y"]) * 2 + place["core"]
+    return (dp, place["x"] // 2)
+
+
+def hop(place, link):
+    moved = dict(place)
+    if link == "core":
+        moved["core"] = 1 - place["core"]
+    elif link[1] == "1":
+        p = place[link[0]]
+        moved[link[0]] = p + 1 - 2 * (p % 2)
+    elif link[1] == "3":
+        moved[link[0]] = 3 - place[link[0]]
+    else:
+        moved[link[0]] = (place[link[0]] + 2) % 4
+    return moved
+
+
+def boxes(place, links):
+    y, z, x = place["y"], place["z"], place["x"] % 2
+    if "y1" in links and "y3" in links:
+        ys = [((0, 2), (0, 2))]
+    elif "y1" in links:
+        ys = [((0, 2), (y // 2, 1))]
+    elif "y3" in links:
+        ys = [((y % 2, 1), (y // 2, 1)), ((1 - y % 2, 1), (1 - y // 2, 1))]
+    else:
+        ys = [((y % 2, 1), (y // 2, 1))]
+    if "z1" in links and "z3" in links:
+        zs = [(0, 4)]
+    elif "z1" in links:
+        zs = [((z // 2) * 2, 2)]
+    elif "z3" in links:
+        zs = [(z, 1), (3 - z, 1)]
+    else:
+        zs = [(z, 1)]
+    xs = (0, 2) if "x1" in links or "x3" in links else (x, 1)
+    return [(ylow, zz, xs, yhigh) for (ylow, yhigh) in ys for zz in zs]
+
+
+def slices(phase, core, box, part):
+    ylow, z, x, yhigh = (pl.ds(*s) for s in box)
+    cols = pl.ds(part * LANES, LANES)
+    if phase < 2:
+        return (ylow, pl.ds(core, 1), z, x, yhigh, slice(None), cols)
+    return (z, x, yhigh, ylow, pl.ds(core, 1), slice(None), cols)
+
+
+SHAPES = (
+    (2, 2, 4, 2, 2, UNIT, WIDTH),
+    (2, 2, 4, 2, 2, UNIT, WIDTH),
+    (4, 2, 2, 2, 2, UNIT, WIDTH),
+)
+
+
+def size_box(count):
+    sizes = {1: (1, 1, 1, 1), 2: (1, 1, 1, 2), 4: (1, 1, 2, 2), 8: (1, 2, 2, 2), 16: (1, 4, 2, 2), 32: (2, 4, 2, 2)}[count]
+    return tuple((0, n) for n in sizes)
+
+
+def wait_units(ref, phase, count, part, sem):
+    view = ref.at[slices(phase, 0, size_box(count), part)]
+    pltpu.make_async_copy(view, view, sem).wait()
+
+
+def remote(src, dst, send_sem, recv_sem, place):
+    return pltpu.make_async_remote_copy(
+        src_ref=src, dst_ref=dst, send_sem=send_sem, recv_sem=recv_sem,
+        device_id=device_of(place), device_id_type=MESH,
+    )
+
+
+def greet(places):
+    barrier = pltpu.get_barrier_semaphore()
+    for place in places:
+        pl.semaphore_signal(barrier, inc=1, device_id=device_of(place), device_id_type=MESH)
+    pl.semaphore_wait(barrier, len(places))
+
+
+def member_of(place):
+    return (place["y"] % 2) * 2 + place["core"]
+
+
+def mates(here):
+    return [hop(here, "core"), hop(here, "y1"), hop(hop(here, "core"), "y1")]
+
+
+def own_box(here):
+    return boxes(here, ())[0]
+def ag_kernel(first_ref, up_ref, down_ref, wa, wb, wc, stage, landed, tall, unit, local_sem, mate_send, mate_recv, send, recv, sib_send, sib_recv):
+    here = position()
+    me = member_of(here)
+    sibling = hop(here, "core")
+    greet([hop(here, l) for l in ("y1", "y3", "z1", "z3", "x1", "x3", "core")] + [mates(here)[2]])
+    weights = (wa, wb, wc)
+    copies = []
+    for which, src in enumerate((first_ref, up_ref)):
+        for i in range(4):
+            stage[which, i, 0:12, :] = src[:, i * WIDTH:(i + 1) * WIDTH].astype(F32)
+    for which in range(2):
+        for k, mate in enumerate(mates(here)):
+            cp = remote(stage.at[which, member_of(mate)], landed.at[which, me], mate_send.at[which, k], mate_recv.at[which, k], mate)
+            cp.start()
+            copies.append(cp)
+    for cp in copies:
+        cp.wait()
+    for which in range(2):
+        for i in range(4):
+            @pl.when(me == i)
+            def _():
+                tall[which, 12 * i:12 * i + 12, :] = stage[which, i, 0:12, :]
+            @pl.when(me != i)
+            def _():
+                tall[which, 12 * i:12 * i + 12, :] = landed[which, i, 0:12, :]
+        unit[which] = tall[which].astype(BF)
+    unit[2] = down_ref[...]
+    own = own_box(here)
+    cps = []
+    for phase in range(3):
+        w = weights[phase]
+        ylow, z, x, yhigh = (s for s, n in own)
+        at = (ylow, here["core"], z, x, yhigh) if phase < 2 else (z, x, yhigh, ylow, here["core"])
+        cp = pltpu.make_async_copy(unit.at[phase], w.at[at], local_sem.at[phase])
+        cp.start()
+        cps.append(cp)
+    for cp in cps:
+        cp.wait()
+    for step in range(6):
+        for phase in range(3):
+            w = weights[phase]
+            for part in range(PARTS):
+                order = ORDERS[part]
+                if step > 0:
+                    wait_units(w, phase, 1 << (step - 1), part, recv.at[phase, part, step - 1])
+                if step < 5:
+                    there = hop(here, order[step])
+                    for box in boxes(here, order[:step]):
+                        view = w.at[slices(phase, here["core"], box, part)]
+                        remote(view, view, send.at[phase, part, step], recv.at[phase, part, step], there).start()
+                if step >= 4:
+                    new = boxes(here, order[:4]) if step == 4 else boxes(hop(here, order[4]), order[:4])
+                    for box in new:
+                        view = w.at[slices(phase, here["core"], box, part)]
+                        remote(view, view, sib_send.at[phase, part], sib_recv.at[phase, part], sibling).start()
+    for phase in range(3):
+        w = weights[phase]
+        for part in range(PARTS):
+            wait_units(w, phase, 32, part, sib_recv.at[phase, part])
+            wait_units(w, phase, 32, part, sib_send.at[phase, part])
+            for s in range(5):
+                wait_units(w, phase, 1 << s, part, send.at[phase, part, s])
+
+def gather_weights(first, up, down, cid=1, space=pl.ANY):
+    vm = pl.BlockSpec(memory_space=pltpu.VMEM)
+    return pl.pallas_call(
+        ag_kernel,
+        out_shape=[jax.ShapeDtypeStruct(s, BF) for s in SHAPES],
+        in_specs=[vm]*3,
+        out_specs=[pl.BlockSpec(memory_space=space)]*3,
+        scratch_shapes=[
+            pltpu.VMEM((2, 4, 16, WIDTH), F32), pltpu.VMEM((2, 4, 16, WIDTH), F32), pltpu.VMEM((2, UNIT, WIDTH), F32), pltpu.VMEM((3, UNIT, WIDTH), BF),
+            pltpu.SemaphoreType.DMA((3,)),
+            pltpu.SemaphoreType.DMA((2, 3)), pltpu.SemaphoreType.DMA((2, 3)),
+            pltpu.SemaphoreType.DMA((3, PARTS, 5)), pltpu.SemaphoreType.DMA((3, PARTS, 5)),
+            pltpu.SemaphoreType.DMA((3, PARTS)), pltpu.SemaphoreType.DMA((3, PARTS)),
+        ],
+        compiler_params=pltpu.CompilerParams(collective_id=cid, has_side_effects=True, vmem_limit_bytes=60 * 2**20),
+    )(first, up, down)
+
+
+START = {16: 0, 8: 16, 4: 24, 2: 28, 1: 30}
+VLINKS = ("core", "y1", "y3", "x1", "z1", "z3")
+
+
+def box_count(box):
+    return box[0][1] * box[1][1] * box[2][1] * box[3][1]
+
+
+def rs_kernel(ga, gb, gc, gv, oqkv, oout, oup, odown, ovec, rda, rdb, rdc, rk, rx, tall, stage, landed, rv,
+              sib_send, sib_recv, send, recv, rep_send, rep_recv, mate_send, mate_recv, vsend, vrecv):
+    here = position()
+    me = member_of(here)
+    sibling = hop(here, "core")
+    twin = hop(here, "x2")
+    greet([hop(here, l) for l in ("y1", "y3", "z1", "z3", "x1", "x3", "core", "x2")] + [mates(here)[2]])
+    grads = (ga, gb, gc)
+    rds = (rda, rdb, rdc)
+    every = ((0, 2), (0, 4), (0, 2), (0, 2))
+    dp = ((here["z"] * 2 + here["x"] % 2) * 4 + here["y"]) * 2 + here["core"]
+
+    def vec_start(r):
+        if r < 6:
+            n = 32 >> r
+            there = hop(here, VLINKS[5 - r])
+            to = ((there["z"] * 2 + there["x"] % 2) * 4 + there["y"]) * 2 + there["core"]
+            src = gv.at[pl.ds(to // n * n, n)]
+            dst = rv.at[pl.ds(64 - 2 * n, n)]
+        else:
+            n, there, src, dst = 1, twin, gv.at[pl.ds(dp, 1)], rv.at[pl.ds(63, 1)]
+        cp = remote(src, dst, vsend.at[r], vrecv.at[r], there)
+        cp.start()
+        return cp
+
+    def vec_add(r, cp):
+        cp.wait()
+        n = 32 >> r if r < 6 else 1
+        lo = 64 - 2 * n if r < 6 else 63
+        mine = pl.ds(dp // n * n, n)
+        gv[mine] = gv[mine] + rv[lo:lo + n]
+
+    def sib_slices(phase, part):
+        cols = pl.ds(part * LANES, LANES)
+        if phase < 2:
+            return (slice(None), pl.ds(0, 1), slice(None), slice(None), slice(None), slice(None), cols)
+        return (slice(None), slice(None), slice(None), slice(None), pl.ds(0, 1), slice(None), cols)
+
+    def sib_copy(phase, part):
+        return remote(grads[phase].at[slices(phase, 1 - here["core"], every, part)], rds[phase].at[sib_slices(phase, part)],
+                      sib_send.at[phase, part], sib_recv.at[phase, part], sibling)
+
+    def sib_add(phase, part):
+        sib_copy(phase, part).wait()
+        for z in range(4):
+            box = ((0, 2), (z, 1), (0, 2), (0, 2))
+            at = slices(phase, here["core"], box, part)
+            g = grads[phase]
+            g[at] = (g[at].astype(F32) + rds[phase][slices(phase, 0, box, part)].astype(F32)).astype(BF)
+
+    def hop_start(phase, part, step):
+        order = ORDERS[part]
+        there = hop(here, order[step])
+        at = START[1 << step]
+        for box in boxes(there, order[:step]):
+            n = box_count(box)
+            src = grads[phase].at[slices(phase, here["core"], box, part)]
+            shape = src.shape[:5]
+            dst = rk.at[phase, pl.ds(at, n)].reshape(shape + (UNIT, WIDTH)).at[:, :, :, :, :, :, pl.ds(part * LANES, LANES)]
+            remote(src, dst, send.at[phase, part, step], recv.at[phase, part, step], there).start()
+            at += n
+
+    def hop_add(phase, part, step):
+        order = ORDERS[part]
+        n = 1 << step
+        at = START[n]
+        cols = pl.ds(part * LANES, LANES)
+        view = rk.at[phase, pl.ds(at, n), :, cols]
+        pltpu.make_async_copy(view, view, recv.at[phase, part, step]).wait()
+        for box in boxes(here, order[:step]):
+            m = box_count(box)
+            g = grads[phase]
+            where = slices(phase, here["core"], box, part)
+            old = g[where]
+            g[where] = (old.astype(F32) + rk[phase, at:at + m, :, part * LANES:(part + 1) * LANES].reshape(old.shape).astype(F32)).astype(BF)
+            at += m
+
+    def hop_sent(phase, part, step):
+        n = 1 << step
+        view = rk.at[phase, pl.ds(START[n], n), :, pl.ds(part * LANES, LANES)]
+        pltpu.make_async_copy(view, view, send.at[phase, part, step]).wait()
+
+    for phase in range(3):
+        for part in range(PARTS):
+            sib_copy(phase, part).start()
+    v = vec_start(0)
+    for phase in range(3):
+        for part in range(PARTS):
+            sib_add(phase, part)
+            hop_start(phase, part, 4)
+    vec_add(0, v)
+    for step in range(4, -1, -1):
+        v = vec_start(5 - step)
+        for phase in range(3):
+            for part in range(PARTS):
+                hop_add(phase, part, step)
+                if step > 0:
+                    hop_start(phase, part, step - 1)
+            if step == 0:
+                ylow, z, x, yhigh = (s for s, n in own_box(here))
+                at = (ylow, here["core"], z, x, yhigh) if phase < 2 else (z, x, yhigh, ylow, here["core"])
+                remote(grads[phase].at[at], rx.at[phase], rep_send.at[phase], rep_recv.at[phase], twin).start()
+        vec_add(5 - step, v)
+    v = vec_start(6)
+    ylow, z, x, yhigh = (s for s, n in own_box(here))
+    swaps = []
+    for phase in range(3):
+        at = (ylow, here["core"], z, x, yhigh) if phase < 2 else (z, x, yhigh, ylow, here["core"])
+        remote(grads[phase].at[at], rx.at[phase], rep_send.at[phase], rep_recv.at[phase], twin).wait()
+        total = grads[phase][at].astype(F32) + rx[phase].astype(F32)
+        if phase == 2:
+            odown[...] = total
+        else:
+            tall[phase] = total
+            for i in range(4):
+                stage[phase, i, 0:12, :] = tall[phase, 12 * i:12 * i + 12, :]
+            for k, mate in enumerate(mates(here)):
+                cp = remote(stage.at[phase, member_of(mate)], landed.at[phase, me], mate_send.at[phase, k], mate_recv.at[phase, k], mate)
+                cp.start()
+                swaps.append(cp)
+    vec_add(6, v)
+    ovec[...] = gv[dp]
+    for cp in swaps:
+        cp.wait()
+    for phase in range(2):
+        for i in range(4):
+            dst = oup.at[:, pl.ds(i * WIDTH, WIDTH)] if phase else (oqkv.at[:, pl.ds(i * WIDTH, WIDTH)] if i < 3 else oout)
+
+            @pl.when(me == i)
+            def _():
+                dst[...] = stage[phase, i, 0:12, :]
+
+            @pl.when(me != i)
+            def _():
+                dst[...] = landed[phase, i, 0:12, :]
+    for phase in range(3):
+        for part in range(PARTS):
+            for step in range(5):
+                hop_sent(phase, part, step)
+
+
+def scatter_grads(ga, gb, gc, gv, cid=2):
+    vm = pl.BlockSpec(memory_space=pltpu.VMEM)
+    dma = pltpu.SemaphoreType.DMA
+    return pl.pallas_call(
+        rs_kernel,
+        out_shape=[jax.ShapeDtypeStruct((12, 3 * WIDTH), F32), jax.ShapeDtypeStruct((12, WIDTH), F32), jax.ShapeDtypeStruct((12, 4 * WIDTH), F32),
+                   jax.ShapeDtypeStruct((UNIT, WIDTH), F32), jax.ShapeDtypeStruct((8, LANES), F32)],
+        in_specs=[vm] * 4,
+        out_specs=[vm] * 5,
+        scratch_shapes=[
+            pltpu.VMEM((2, 1, 4, 2, 2, UNIT, WIDTH), BF), pltpu.VMEM((2, 1, 4, 2, 2, UNIT, WIDTH), BF), pltpu.VMEM((4, 2, 2, 2, 1, UNIT, WIDTH), BF),
+            pltpu.VMEM((3, 31, UNIT, WIDTH), BF), pltpu.VMEM((3, UNIT, WIDTH), BF),
+            pltpu.VMEM((2, UNIT, WIDTH), F32), pltpu.VMEM((2, 4, 16, WIDTH), F32), pltpu.VMEM((2, 4, 16, WIDTH), F32), pltpu.VMEM((64, 8, LANES), F32),
+            dma((3, PARTS)), dma((3, PARTS)), dma((3, PARTS, 5)), dma((3, PARTS, 5)), dma((3,)), dma((3,)), dma((2, 3)), dma((2, 3)), dma((7,)), dma((7,)),
+        ],
+        input_output_aliases={},
+        compiler_params=pltpu.CompilerParams(collective_id=cid, has_side_effects=True, vmem_limit_bytes=60 * 2**20),
+    )(ga, gb, gc, gv)
+
 
 HD = 64
 
@@ -214,103 +582,39 @@
     return (gradients, input_grad)
 
 
-def add_tuples(left, right):
-    return tuple((left_item + right_item for left_item, right_item in zip(left, right)))
-
-
-def local(
-    states,
-    qkv_weight,
-    query_bias,
-    value_bias,
-    out_weight,
-    out_bias,
-    attn_gain,
-    attn_shift,
-    up_weight,
-    up_bias,
-    down_weight,
-    down_bias,
-    ffn_gain,
-    ffn_shift,
-    out_grad,
-    lengths,
-):
-    shards = (
-        qkv_weight,
-        query_bias,
-        value_bias,
-        out_weight,
-        out_bias,
-        attn_gain,
-        attn_shift,
-        up_weight,
-        up_bias,
-        down_weight,
-        down_bias,
-        ffn_gain,
-        ffn_shift,
-    )
+def spread(vector):
+    return vector.reshape(64, -1)
+
+
+def local(states, qkv_weight, query_bias, value_bias, out_weight, out_bias, attn_gain, attn_shift, up_weight, up_bias,
+          down_weight, down_bias, ffn_gain, ffn_shift, out_grad, lengths):
     micro_count, seq_count, length, width = states.shape
     positions = jnp.arange(length, dtype=jnp.int32)
-    valid_all = positions[None, None, :] < lengths[:, :, None]
-    encoded_list = []
-    input_list = []
-    totals = None
-    for step_index in range(micro_count):
-        gathered = (
-            lax.all_gather(shards[0], "dp", axis=0, tiled=True),
-            lax.all_gather(shards[1], "dp", axis=0, tiled=True),
-            lax.all_gather(shards[2], "dp", axis=0, tiled=True),
-            lax.all_gather(shards[3], "dp", axis=0, tiled=True),
-            lax.all_gather(shards[4], "dp", axis=0, tiled=True),
-            lax.all_gather(shards[5], "dp", axis=0, tiled=True),
-            lax.all_gather(shards[6], "dp", axis=0, tiled=True),
-            lax.all_gather(shards[7], "dp", axis=0, tiled=True),
-            lax.all_gather(shards[8], "dp", axis=0, tiled=True),
-            lax.all_gather(shards[9], "dp", axis=0, tiled=True),
-            lax.all_gather(shards[10], "dp", axis=0, tiled=True),
-            lax.all_gather(shards[11], "dp", axis=0, tiled=True),
-            lax.all_gather(shards[12], "dp", axis=0, tiled=True),
-        )
-        encoded, saved_state = forward(gathered, states[step_index], valid_all[step_index])
-        gathered = (
-            lax.all_gather(shards[0], "dp", axis=0, tiled=True),
-            lax.all_gather(shards[1], "dp", axis=0, tiled=True),
-            lax.all_gather(shards[2], "dp", axis=0, tiled=True),
-            lax.all_gather(shards[3], "dp", axis=0, tiled=True),
-            lax.all_gather(shards[4], "dp", axis=0, tiled=True),
-            lax.all_gather(shards[5], "dp", axis=0, tiled=True),
-            lax.all_gather(shards[6], "dp", axis=0, tiled=True),
-            lax.all_gather(shards[7], "dp", axis=0, tiled=True),
-            lax.all_gather(shards[8], "dp", axis=0, tiled=True),
-            lax.all_gather(shards[9], "dp", axis=0, tiled=True),
-            lax.all_gather(shards[10], "dp", axis=0, tiled=True),
-            lax.all_gather(shards[11], "dp", axis=0, tiled=True),
-            lax.all_gather(shards[12], "dp", axis=0, tiled=True),
-        )
-        cotangent = out_grad[step_index].reshape(seq_count * length, width).astype(jnp.float32)
-        gradients, input_grad = backward(gathered, saved_state, cotangent)
-        encoded_list.append(encoded.reshape(seq_count, length, width).astype(jnp.bfloat16))
-        input_list.append(input_grad.reshape(seq_count, length, width))
-        owned = (
-            lax.psum_scatter(gradients[0], "dp", scatter_dimension=0, tiled=True),
-            lax.psum_scatter(gradients[1], "dp", scatter_dimension=0, tiled=True),
-            lax.psum_scatter(gradients[2], "dp", scatter_dimension=0, tiled=True),
-            lax.psum_scatter(gradients[3], "dp", scatter_dimension=0, tiled=True),
-            lax.psum_scatter(gradients[4], "dp", scatter_dimension=0, tiled=True),
-            lax.psum_scatter(gradients[5], "dp", scatter_dimension=0, tiled=True),
-            lax.psum_scatter(gradients[6], "dp", scatter_dimension=0, tiled=True),
-            lax.psum_scatter(gradients[7], "dp", scatter_dimension=0, tiled=True),
-            lax.psum_scatter(gradients[8], "dp", scatter_dimension=0, tiled=True),
-            lax.psum_scatter(gradients[9], "dp", scatter_dimension=0, tiled=True),
-            lax.psum_scatter(gradients[10], "dp", scatter_dimension=0, tiled=True),
-            lax.psum_scatter(gradients[11], "dp", scatter_dimension=0, tiled=True),
-            lax.psum_scatter(gradients[12], "dp", scatter_dimension=0, tiled=True),
-        )
-        totals = owned if totals is None else add_tuples(totals, owned)
-    final = lax.psum(totals, "rep")
-    return (jnp.stack(encoded_list), jnp.stack(input_list)) + tuple(final)
+    valid = (positions[None, None, :] < lengths[:, :, None]).reshape(micro_count * seq_count, length)
+    short = (query_bias, value_bias, out_bias, attn_gain, attn_shift, down_bias, ffn_gain, ffn_shift)
+    packed = lax.all_gather(jnp.concatenate(short + (up_bias,)), "dp", axis=0)
+    qb, vb, ob, ag, ash, db, fg, fs = (packed[:, 12 * i:12 * i + 12].reshape(width) for i in range(8))
+    ub = packed[:, 96:].reshape(4 * width)
+    wa, wb, wc = gather_weights(jnp.concatenate([qkv_weight, out_weight], 1), up_weight, down_weight)
+    wa = wa.reshape(4, width, width)
+    wb = wb.reshape(4, width, width)
+    full = (jnp.concatenate([wa[0], wa[1], wa[2]], 1), qb, vb, wa[3], ob, ag, ash,
+            jnp.concatenate([wb[i] for i in range(4)], 1), ub, wc.reshape(4 * width, width), db, fg, fs)
+    x = states.reshape(micro_count * seq_count, length, width)
+    encoded, saved = forward(full, x, valid)
+    grads, input_grad = backward(full, saved, out_grad.reshape(-1, width).astype(F32))
+    gqkv, gqb, gvb, gow, gob, gag, gash, gup, gub, gdn, gdb, gfg, gfs = grads
+    low = lambda a: a.astype(BF)
+    ga = jnp.stack([low(gqkv[:, i * width:(i + 1) * width]) for i in range(3)] + [low(gow)]).reshape(SHAPES[0])
+    gb = jnp.stack([low(gup[:, i * width:(i + 1) * width]) for i in range(4)]).reshape(SHAPES[1])
+    gc = low(gdn).reshape(SHAPES[2])
+    row = jnp.concatenate([spread(v) for v in (gqb, gvb, gob, gag, gash, gdb, gfg, gfs)], 1)
+    row = jnp.pad(row, ((0, 0), (0, 32)))
+    gv = jnp.concatenate([row[:, None], jnp.pad(spread(gub), ((0, 0), (0, 80)))[:, None], jnp.zeros((64, 6, 128), F32)], 1)
+    oqkv, oout, oup, odown, ovec = scatter_grads(ga, gb, gc, gv)
+    o = [ovec[0, 12 * i:12 * i + 12] for i in range(8)]
+    return (encoded.reshape(states.shape).astype(BF), input_grad.reshape(states.shape), oqkv, o[0], o[1], oout, o[2], o[3], o[4],
+            oup, ovec[1, :48], odown, o[5], o[6], o[7])
 
 
 def solution(mesh):

time: 1720 us -> 527 us (0.31)
  waiting for transfers between devices: 647 us -> 0 us
  blocking collectives: 722 us -> 277 us
  Pallas kernels: 0 us -> 115 us
  starting transfers between devices: 93.1 us -> 0 us
  local copies, waits for them, and re-layouts: 116 us -> 50.1 us
  matrix products: 77.4 us -> 58.6 us
    unnamed x3 -> x1, blocking collectives: 713 us -> 277 us
    reduce_scatter x1 -> x0, waiting for transfers between devices: 295 us -> none  [local(): lax.psum_scatter(gradients[9], 'dp', scatter_dimension=0, tiled=True)]
    unnamed x40 -> x0, waiting for transfers between devices: 262 us -> none
    pallas_call x0 -> x2, Pallas kernels: none -> 115 us  [the longest x1 60.1 us: scatter_grads(): pl.pallas_call(rs_kernel, out_shape=[jax.ShapeDtypeStruct((12, 3 * WIDTH)...]
    unnamed x33 -> x0, starting transfers between devices: 92.7 us -> none
    all_gather x4 -> x0, waiting for transfers between devices: 90.1 us -> none  [the longest x1 90.1 us: local(): lax.all_gather(shards[9], 'dp', axis=0, tiled=True)]
    unnamed x257 -> x119, local copies, waits for them, and re-layouts: 105 us -> 19.9 us
  transfers between devices with their start and end apart: 39 -> 0, of which waited for: 5 -> 0; matrix products, arithmetic and copies ran while one was open for 18% -> 0% of each run, Pallas kernels for 0% -> 0%
where the time goes in v1:
time: 527 us; the launch traced here: 521 us
  blocking collectives  277 us (53%)
  Pallas kernels  115 us (22%)
  matrix products  58.6 us (11%)
  local copies, waits for them, and re-layouts  50.1 us (10%)
  other arithmetic  17.7 us (3%)
    unnamed x1, blocking collectives  277 us
    pallas_call x1, Pallas kernels, scatter_grads(): pl.pallas_call(rs_kernel, out_shape=[jax.ShapeDtypeStruct((12, 3 * WIDTH)...  60.1 us
    pallas_call x1, Pallas kernels, gather_weights(): pl.pallas_call(ag_kernel, out_shape=[jax.ShapeDtypeStruct(s, BF) for s in...  55 us
    unnamed x119, local copies, waits for them, and re-layouts  19.9 us
    dot_general x4, matrix products, times_transposed(): lax.dot_general(left, right, (((1,), (1,)), ((), ())), preferred_element_...  15.3 us
    dot_general x4, matrix products, contract_rows(): lax.dot_general(left, right, (((0,), (0,)), ((), ())), preferred_element_...  10.8 us

profile of v1, /device:TPU:1, one launch (start us, length us, event | category | flops | bytes accessed | tf_op | source)
XLA Modules:
  0.0 520.8 jit_solution(13479790767101043794)
XLA Ops:
  0.6 6.1 %concatenate.23 = bf16[144]{0:T(256)(128)(2,1)S(1)} concatenate(bf16[12]{0:T(256)(128)(2,1)} %param.18, bf16[12]{0:T(256)(128)(2,1)} %param.19, bf16[12]{0:T(256)(128)(2,1)} %param.21, bf16[12]{0:T(256)(128)(2,1)} %param.22, bf16[12]{0:T(256)(128)(2,1)} %param.23, bf16[12]{0:T(256)(128)(2,1)} %param.27, bf16[12]{0:T(256)(128)(2,1)} %param.28, bf16[12]{0:T(256)(128)(2,1)} %param.29, ...), dimensions={0} | concatenate | bytes 576 | tf_op jit(solution)/shard_map/concatenate | solution.py:595
  6.8 1.2 dynamic-slice
  8.9 276.8 %all-reduce.2 = bf16[9216]{0:T(1024)(128)(2,1)S(1)} all-reduce(bf16[9216]{0:T(1024)(128)(2,1)S(1)} %dynamic-update-slice), channel_id=2, replica_groups=mesh['dp'=64,'rep'=2] {'dp'}, use_global_device_ids=true, to_apply=%add.2 | all-reduce | flops 9216 | bytes 36864
  288.0 1.6 pad_maximum_fusion.10.first_ref
  289.5 55.0 %shard_map.271 = (bf16[2,2,4,2,2,48,768]{6,5,4,3,2,1,0:T(8,128)(2,1)}, bf16[2,2,4,2,2,48,768]{6,5,4,3,2,1,0:T(8,128)(2,1)}, bf16[4,2,2,2,2,48,768]{6,5,4,3,2,1,0:T(8,128)(2,1)}) custom-call(bf16[12,3072]{1,0:T(8,128)(2,1)} %pad_maximum_fusion.10.first_ref, bf16[12,3072]{1,0:T(8,128)(2,1)} %up_ref.1, bf16[48,768]{1,0:T(8,128)(2,1)} %down_ref.1), custom_call_target="tpu_custom_call" | custom-call | tf_op jit(solution)/shard_map/pallas_call | solution.py:191
  344.5 4.6 slice_bitcast_fusion.10
  349.3 2.3 slice_bitcast_fusion.14
  351.6 2.1 convolution_bitcast_fusion
  353.7 2.1 copy-done.11
  356.3 2.2 fusion.8
  358.8 2.0 fusion.42
  360.8 1.1 fusion
  361.9 1.6 copy-done
  363.6 4.2 fusion.19
  369.0 2.4 fusion.43
  371.5 1.5 reshape.314
  372.9 0.9 reshape.313
  374.2 8.4 %multiply_convert_fusion.1 = (bf16[512,3072]{1,0:T(8,128)(2,1)S(1)}, f32[512,3072]{1,0:T(8,128)}) fusion(f32[3072]{0:T(1024)} %reshape.315, bf16[768,768]{1,0:T(8,128)(2,1)} %get-tuple-element.86, bf16[768,768]{1,0:T(8,128)(2,1)} %get-tuple-element.87, bf16[768,768]{1,0:T(8,128)(2,1)} %get-tuple-element.88, bf16[768,768]{1,0:T(8,128)(2,1)S(1)} %copy-done.13, ...), kind=kOutput, calls=%fused_computation.5 | convolution fusion | flops 2446196736 | bytes 15751168 | tf_op jit(solution)/shard_map/dot_general | solution.py:454
  382.6 5.3 %fusion.44 = (f32[512]{0:T(512)S(1)}, f32[512,768]{1,0:T(8,128)S(1)}) fusion(f32[768]{0:T(1024)S(1)} %copy-done.39, bf16[512,3072]{1,0:T(8,128)(2,1)S(1)} %get-tuple-element.113, bf16[3072,768]{1,0:T(8,128)(2,1)S(1)} %bitcast.167, f32[768]{0:T(1024)S(1)} %copy-done.37, f32[768]{0:T(1024)S(1)} %reshape.313, f32[512]{0:T(512)S(1)} %fusion.32, ...), kind=kOutput, calls=%fused_computation.133 | convolution fusion | flops 2418671104 | bytes 11025408 | tf_op jit(solution)/shard_map/dot_general | solution.py:458
  389.3 1.6 fusion.41
  391.1 1.5 copy-done.48
  392.7 6.9 %convert_reduce_fusion = (f32[3072]{0:T(1024)S(1)}, bf16[512,3072]{1,0:T(8,128)(2,1)S(1)}) fusion(f32[512,3072]{1,0:T(8,128)S(1)} %copy-done.48, f32[3072]{0:T(1024)S(1)} %copy-done.36, bf16[512,768]{1,0:T(8,128)(2,1)S(1)} %get-tuple-element.67, bf16[3072,768]{1,0:T(8,128)(2,1)} %bitcast.164), kind=kOutput, calls=%fused_computation | convolution fusion | flops 2441081856 | bytes 14966784 | tf_op jit(solution)/shard_map/dot_general | solution.py:399
  399.7 3.1 multiply_reduce_fusion.1
  403.6 1.0 copy-done.9
  404.8 0.9 copy-done.28
  405.7 2.1 convolution_convert_fusion.4
  407.8 1.2 copy.50
  408.9 3.4 reshape.296
  412.4 5.0 multiply_reduce_fusion
  417.5 1.6 multiply_convert_fusion
  421.0 1.1 fusion.20
  422.1 0.8 copy.58
  423.3 1.2 convert_reduce_fusion.4
  426.6 3.2 add_add_fusion.4
  430.9 2.3 fusion.2
  433.5 2.7 pad_maximum_fusion.1
  436.2 1.3 copy-done.45
  437.6 3.4 convolution_convert_fusion.1
  441.3 2.7 pad_maximum_fusion.2
  444.0 1.1 copy-done.47
  445.1 4.4 convolution_convert_fusion
  451.5 60.1 %shard_map.272 = (f32[12,2304]{1,0:T(8,128)}, f32[12,768]{1,0:T(8,128)}, f32[12,3072]{1,0:T(8,128)}, f32[48,768]{1,0:T(8,128)}, f32[8,128]{1,0:T(8,128)}) custom-call(bf16[2,2,4,2,2,48,768]{6,5,4,3,2,1,0:T(8,128)(2,1)} %bitcast.143, bf16[2,2,4,2,2,48,768]{6,5,4,3,2,1,0:T(8,128)(2,1)} %bitcast.144, bf16[4,2,2,2,2,48,768]{6,5,4,3,2,1,0:T(8,128)(2,1)} %bitcast.145, ...), custom_call_target="tpu_custom_call" | custom-call | tf_op jit(solution)/shard_map/pallas_call | solution.py:359
  511.6 1.6 slice_bitcast_fusion.17
  513.2 1.2 slice_bitcast_fusion.20
  514.4 1.6 copy.107
  516.0 1.4 copy.108
  517.4 1.6 copy.109
  519.0 1.6 copy.110
  (163 shorter events, 15.4 us)
Async XLA Ops:
  349.3 2.3 copy-start.40
  351.6 2.1 copy-start.18
  351.6 2.1 copy-start.20
  351.6 2.1 copy-start.22
  353.7 2.1 copy-start.11
  356.3 2.4 copy-start.43
  358.7 2.1 copy-start.1
  360.8 2.7 copy-start
  360.8 2.8 copy-start.30
  363.4 4.5 copy-start.32
  363.6 4.3 copy-start.12
  367.9 1.1 copy-start.41
  368.9 2.5 copy-start.24
  369.0 5.1 copy-start.13
  371.4 11.1 %copy-start.6 = (f32[512,768]{1,0:T(8,128)}, f32[512,768]{1,0:T(8,128)S(1)}, u32[]{:S(2)}) copy-start(f32[512,768]{1,0:T(8,128)S(1)} %get-tuple-element.112) | copy-start | bytes 4718596
  373.8 8.8 %slice-start.2 = ((s8[4718592]{0:T(1024)(128)(4,1)}), s8[4194304]{0:T(1024)(128)(4,1)S(1)}, s32[]{:S(2)}) async-start(s8[4718592]{0:T(1024)(128)(4,1)} %bitcast.165), calls=%async_computation.2 | async-start | bytes 8388608
  374.1 8.5 %copy-start.37 = (f32[768]{0:T(1024)S(1)}, f32[768]{0:T(1024)}, u32[]{:S(2)}) copy-start(f32[768]{0:T(1024)} %reshape.314) | copy-start | bytes 9220
  374.1 8.5 %copy-start.39 = (f32[768]{0:T(1024)S(1)}, f32[768]{0:T(1024)}, u32[]{:S(2)}) copy-start(f32[768]{0:T(1024)} %reshape.316) | copy-start | bytes 9220
  374.2 8.5 %slice-start.3 = ((s8[4718592]{0:T(1024)(128)(4,1)}), s8[524288]{0:T(1024)(128)(4,1)S(1)}, s32[]{:S(2)}) async-start(s8[4718592]{0:T(1024)(128)(4,1)} %bitcast.165), calls=%async_computation.3 | async-start | bytes 1048576
  382.6 5.4 %copy-start.46 = (bf16[512,3072]{1,0:T(8,128)(2,1)}, bf16[512,3072]{1,0:T(8,128)(2,1)S(1)}, u32[]{:S(2)}) copy-start(bf16[512,3072]{1,0:T(8,128)(2,1)S(1)} %get-tuple-element.113) | copy-start | bytes 9437188
  382.6 5.7 %copy-start.35 = (f32[64,12]{1,0:T(8,128)S(1)}, f32[64,12]{1,0:T(8,128)}, u32[]{:S(2)}) copy-start(f32[64,12]{1,0:T(8,128)} %get-tuple-element.93) | copy-start | bytes 9220
  382.6 5.8 %copy-start.4 = (bf16[2,1,256,768]{3,2,1,0:T(8,128)(2,1)S(1)}, bf16[2,1,256,768]{3,2,1,0:T(8,128)(2,1)}, u32[]{:S(2)}) copy-start(bf16[2,1,256,768]{3,2,1,0:T(8,128)(2,1)} %param.30) | copy-start | bytes 2359300
  387.9 1.2 copy-start.34
  389.3 3.4 copy-start.48
  390.9 1.8 copy-start.36
  391.1 8.5 %copy-start.26 = (bf16[512,768]{1,0:T(8,128)(2,1)}, bf16[512,768]{1,0:T(8,128)(2,1)S(1)}, u32[]{:S(2)}) copy-start(bf16[512,768]{1,0:T(8,128)(2,1)S(1)} %get-tuple-element.67) | copy-start | bytes 2359300
  392.6 7.0 %copy-start.7 = (f32[512,768]{1,0:T(8,128)S(1)}, f32[512,768]{1,0:T(8,128)}, u32[]{:S(2)}) copy-start(f32[512,768]{1,0:T(8,128)} %copy-done.6) | copy-start | bytes 4718596
  392.6 7.0 %copy-start.14 = (bf16[768,768]{1,0:T(8,128)(2,1)S(1)}, bf16[768,768]{1,0:T(8,128)(2,1)}, u32[]{:S(2)}) copy-start(bf16[768,768]{1,0:T(8,128)(2,1)} %get-tuple-element.85) | copy-start | bytes 3538948
  392.6 7.0 %copy-start.15 = (bf16[768,768]{1,0:T(8,128)(2,1)S(1)}, bf16[768,768]{1,0:T(8,128)(2,1)}, u32[]{:S(2)}) copy-start(bf16[768,768]{1,0:T(8,128)(2,1)} %get-tuple-element.86) | copy-start | bytes 3538948
  392.6 7.0 %copy-start.16 = (bf16[768,768]{1,0:T(8,128)(2,1)S(1)}, bf16[768,768]{1,0:T(8,128)(2,1)}, u32[]{:S(2)}) copy-start(bf16[768,768]{1,0:T(8,128)(2,1)} %get-tuple-element.87) | copy-start | bytes 3538948
  392.6 7.0 %copy-start.17 = (bf16[768,768]{1,0:T(8,128)(2,1)S(1)}, bf16[768,768]{1,0:T(8,128)(2,1)}, u32[]{:S(2)}) copy-start(bf16[768,768]{1,0:T(8,128)(2,1)} %get-tuple-element.88) | copy-start | bytes 3538948
  399.6 3.2 copy-start.44
  403.4 1.1 copy-start.9
  408.9 8.5 %slice-start = ((s8[6291456]{0:T(1024)(128)(4,1)}), s8[2097152]{0:T(1024)(128)(4,1)S(1)}, s32[]{:S(2)}) async-start(s8[6291456]{0:T(1024)(128)(4,1)} %bitcast.141), calls=%async_computation | async-start | bytes 4194304
  412.4 5.1 slice-start.1
  422.1 1.1 copy-start.3
  423.3 2.3 copy-start.23
  424.4 1.4 copy-start.10
  424.4 1.8 copy-start.19
  424.5 2.1 copy-start.21
  426.6 3.2 copy-start.25
  426.6 3.2 copy-start.29
  433.5 2.8 copy-start.8
  433.5 2.7 copy-start.38
  433.5 4.1 copy-start.45
  441.3 2.7 copy-start.27
  441.3 3.8 copy-start.47
  445.1 5.1 copy-start.5
  (5 other events, 4.7 us)

commit v2 on v0

v2 whole, which is shorter than its diff:
```python
import collections
import math
import types

import jax
import jax.numpy as jnp
from jax import lax
from jax.experimental import pallas as pl
from jax.experimental.pallas import tpu as pltpu
from jax.sharding import PartitionSpec as P

Place = collections.namedtuple("Place", "core y z x")
MESH = pl.DeviceIdType.MESH
BF = jnp.bfloat16
F32 = jnp.float32
WIDTH = 768
UNIT = 48
LANES = 128
PARTS = 6

CORE, Y1, Y3, Z1, Z3, X1, X2, X3 = (0, 0), (1, 1), (1, 3), (2, 1), (2, 3), (3, 1), (3, 2), (3, 3)

ORDERS = (
    (Z1, Z3, Y1, Y3, X1),
    (Y1, Y3, Z1, Z3, X3),
    (Y3, Z1, Z3, X1, Y1),
    (Y1, Z3, X1, Z1, Y3),
    (Y1, Z3, X3, Y3, Z1),
    (Z1, Y3, X3, Y1, Z3),
)


def position():
    dp = lax.axis_index("dp")
    rep = lax.axis_index("rep")
    return Place(dp % 2, (dp // 2) % 4, dp // 16, rep * 2 + (dp // 8) % 2)


def device_of(place):
    dp = ((place.z * 2 + place.x % 2) * 4 + place.y) * 2 + place.core
    return (dp, place.x // 2)


def hop(place, link):
    axis, how = link
    p = place[axis]
    moved = (1 - p, p + 1 - 2 * (p % 2), (p + 2) % 4, 3 - p)[how]
    return Place(*(moved if i == axis else q for i, q in enumerate(place)))


def boxes(place, links):
    y, z, x = place.y, place.z, place.x % 2
    if Y1 in links and Y3 in links:
        ys = [((0, 2), (0, 2))]
    elif Y1 in links:
        ys = [((0, 2), (y // 2, 1))]
    elif Y3 in links:
        ys = [((y % 2, 1), (y // 2, 1)), ((1 - y % 2, 1), (1 - y // 2, 1))]
    else:
        ys = [((y % 2, 1), (y // 2, 1))]
    if Z1 in links and Z3 in links:
        zs = [(0, 4)]
    elif Z1 in links:
        zs = [((z // 2) * 2, 2)]
    elif Z3 in links:
        zs = [(z, 1), (3 - z, 1)]
    else:
        zs = [(z, 1)]
    xs = (0, 2) if X1 in links or X3 in links else (x, 1)
    return [(ylow, zz, xs, yhigh) for (ylow, yhigh) in ys for zz in zs]


def slices(phase, core, box, part):
    ylow, z, x, yhigh = (pl.ds(*s) for s in box)
    cols = pl.ds(part * LANES, LANES)
    if phase < 2:
        return (ylow, pl.ds(core, 1), z, x, yhigh, slice(None), cols)
    return (z, x, yhigh, ylow, pl.ds(core, 1), slice(None), cols)


SHAPES = (
    (2, 2, 4, 2, 2, UNIT, WIDTH),
    (2, 2, 4, 2, 2, UNIT, WIDTH),
    (4, 2, 2, 2, 2, UNIT, WIDTH),
)


def size_box(count):
    sizes = {1: (1, 1, 1, 1), 2: (1, 1, 1, 2), 4: (1, 1, 2, 2), 8: (1, 2, 2, 2), 16: (1, 4, 2, 2), 32: (2, 4, 2, 2)}[count]
    return tuple((0, n) for n in sizes)


def wait_units(ref, phase, count, part, sem):
    view = ref.at[slices(phase, 0, size_box(count), part)]
    pltpu.make_async_copy(view, view, sem).wait()


def remote(src, dst, send_sem, recv_sem, place):
    return pltpu.make_async_remote_copy(
        src_ref=src, dst_ref=dst, send_sem=send_sem, recv_sem=recv_sem,
        device_id=device_of(place), device_id_type=MESH,
    )


def greet(places):
    barrier = pltpu.get_barrier_semaphore()
    for place in places:
        pl.semaphore_signal(barrier, inc=1, device_id=device_of(place), device_id_type=MESH)
    pl.semaphore_wait(barrier, len(places))


def member_of(place):
    return (place.y % 2) * 2 + place.core


def mates(here):
    return [hop(here, CORE), hop(here, Y1), hop(hop(here, CORE), Y1)]


def own_box(here):
    return boxes(here, ())[0]


HALF = 256
SEQ = 256
TOKENS = 512
epsilon = 1e-05
NT = (((1,), (1,)), ((), ()))
TN = (((0,), (0,)), ((), ()))
VQ, VV, VO, VAG, VAS, VD, VFG, VFS, VUP = range(9)


def mm(left, right):
    return jnp.dot(left, right, preferred_element_type=F32)


def mm_nt(left, right):
    return lax.dot_general(left, right, NT, preferred_element_type=F32)


def mm_tn(left, right):
    return lax.dot_general(left, right, TN, preferred_element_type=F32)


def normalise(value):
    center = value - jnp.mean(value, -1, keepdims=True)
    scale = lax.rsqrt(jnp.mean(center * center, -1, keepdims=True) + epsilon)
    return center * scale, scale


def norm_back(cot, gain, n, scale):
    e = cot * gain
    return scale * (e - jnp.mean(e, -1, keepdims=True) - n * jnp.mean(e * n, -1, keepdims=True))


def half_masks():
    lane = lax.broadcasted_iota(jnp.int32, (1, LANES), 1)
    low = (lane < 64).astype(F32).astype(BF)
    return low, (1.0 - low.astype(F32)).astype(BF)


def column_total(ref_rows):
    return jnp.sum(ref_rows.astype(F32), 0, keepdims=True)


class Layer:
    def __init__(self, slabs, grads, vec, lengths, x, og, enc, gvec, b):
        self.slabs, self.grads, self.vec, self.lengths, self.x, self.og = slabs, grads, vec, lengths, x, og
        self.enc, self.gvec, self.b = enc, gvec, b

    def v(self, row):
        return self.vec[row:row + 1, :]

    def project(self):
        b = self.b
        for j, (dst, row) in enumerate(((b.q, VQ), (b.k, None), (b.v, VV))):
            for n in range(3):
                cols = slice(n * 256, n * 256 + 256)
                acc = mm(self.x[...], self.slabs[0].at[j][:, cols])
                if row is not None:
                    acc = acc + self.vec[row:row + 1, cols]
                low = acc.astype(BF)
                if j == 0:
                    low = (low.astype(F32) * 0.125).astype(BF)
                dst[:, cols] = low

    def attend(self):
        b = self.b
        masks = half_masks()

        def body(i, _):
            s, p = i // 6, i % 6
            rows = pl.ds(pl.multiple_of(s * SEQ, SEQ), SEQ)
            cols = pl.ds(pl.multiple_of(p * LANES, LANES), LANES)
            q, k, v = b.q[rows, cols], b.k[rows, cols], b.v[rows, cols]
            length = self.lengths[s, 0]
            key = lax.broadcasted_iota(jnp.int32, (SEQ, SEQ), 0)
            out = None
            for a in range(2):
                st = mm_nt(k * masks[a], q)
                st = jnp.where(key < length, st, -1e9)
                e = jnp.exp(st - jnp.max(st, 0, keepdims=True))
                att = e * (1.0 / jnp.sum(e, 0, keepdims=True))
                b.p[i * 2 + a] = att
                o = mm_tn(v * masks[a], att.astype(BF))
                out = o if out is None else out + o
            b.mixed[rows, cols] = out.T.astype(BF)
            return 0

        lax.fori_loop(0, 12, body, 0)

    def attn_out(self):
        b = self.b
        for n in range(3):
            cols = slice(n * 256, n * 256 + 256)
            acc = mm(b.mixed[...], self.slabs[0].at[3][:, cols]) + self.vec[VO:VO + 1, cols]
            b.n1[:, cols] = self.x[:, cols].astype(F32) + acc

        def body(r, _):
            rows = pl.ds(pl.multiple_of(r * 32, 32), 32)
            n, scale = normalise(b.n1[rows, :])
            b.n1[rows, :] = n
            b.r1[rows, :] = jnp.broadcast_to(scale, (32, LANES))
            b.nl[rows, :] = (n * self.v(VAG) + self.v(VAS)).astype(BF)
            return 0

        lax.fori_loop(0, TOKENS // 32, body, 0)

    def feed(self):
        b = self.b

        def body(j, _):
            w = self.slabs[1].at[j]
            for n in range(3):
                cols = slice(n * 256, n * 256 + 256)
                bias = self.vec[pl.ds(VUP + j, 1), cols]
                for h in range(2):
                    rows = slice(h * 256, h * 256 + 256)
                    pre = mm(b.nl[rows, :], w[:, cols]) + bias
                    cdf = 0.5 * (1.0 + lax.erf(pre * (1.0 / math.sqrt(2.0))))
                    pdf = jnp.exp(pre * pre * -0.5) * (1.0 / math.sqrt(2.0 * math.pi))
                    b.act[j, rows, cols] = (pre * cdf).astype(BF)
                    b.gp[j, rows, cols] = cdf + pre * pdf
            return 0

        lax.fori_loop(0, 4, body, 0)

    def feed_out(self):
        b = self.b
        for n in range(3):
            cols = slice(n * 256, n * 256 + 256)
            acc = self.b.n1[:, cols] * self.vec[VAG:VAG + 1, cols] + self.vec[VAS:VAS + 1, cols] + self.vec[VD:VD + 1, cols]
            for j in range(4):
                acc = acc + mm(b.act[j], self.slabs[2].at[j][:, cols])
            b.second[:, cols] = acc

        def body(r, sums):
            rows = pl.ds(pl.multiple_of(r * 32, 32), 32)
            n, scale = normalise(b.second[rows, :])
            c = self.og[rows, :].astype(F32)
            self.enc[rows, :] = (n * self.v(VFG) + self.v(VFS)).astype(BF)
            g = norm_back(c, self.v(VFG), n, scale)
            b.second[rows, :] = g
            low = g.astype(BF)
            b.nl[rows, :] = low
            return sums[0] + column_total(c * n), sums[1] + column_total(c), sums[2] + column_total(low)

        zero = jnp.zeros((1, WIDTH), F32)
        sums = lax.fori_loop(0, TOKENS // 32, body, (zero, zero, zero))
        self.gvec[VFG:VFG + 1, :], self.gvec[VFS:VFS + 1, :], self.gvec[VD:VD + 1, :] = sums

    def down_grads(self):
        b = self.b

        def body(j, _):
            for n in range(3):
                cols = slice(n * 256, n * 256 + 256)
                self.grads[2][j, :, cols] = mm_tn(b.act[j], b.nl[:, cols]).astype(BF)
            return 0

        lax.fori_loop(0, 4, body, 0)

    def feed_back(self):
        b = self.b

        def body(j, _):
            w = self.slabs[2].at[j]
            for n in range(3):
                cols = slice(n * 256, n * 256 + 256)
                total = jnp.zeros((1, 256), F32)
                for h in range(2):
                    rows = slice(h * 256, h * 256 + 256)
                    acc = mm_nt(b.nl[rows, :], w[cols, :])
                    low = (acc * b.gp[j, rows, cols]).astype(BF)
                    b.gpre[j, rows, cols] = low
                    total = total + column_total(low)
                self.gvec[pl.ds(VUP + j, 1), cols] = total
            return 0

        lax.fori_loop(0, 4, body, 0)

    def up_grads(self):
        b = self.b

        def body(j, _):
            for n in range(3):
                cols = slice(n * 256, n * 256 + 256)
                self.grads[1][j, :, cols] = mm(b.nlt[...], b.gpre[j, :, cols]).astype(BF)
            return 0

        lax.fori_loop(0, 4, body, 0)

    def norm1_back(self):
        b = self.b
        for n in range(3):
            cols = slice(n * 256, n * 256 + 256)
            acc = b.second[:, cols]
            for j in range(4):
                acc = acc + mm_nt(b.gpre[j], self.slabs[1].at[j][cols, :])
            b.second[:, cols] = acc

    def norm1_rows(self):
        b = self.b

        def body(r, sums):
            rows = pl.ds(pl.multiple_of(r * 32, 32), 32)
            c = b.second[rows, :]
            n = b.n1[rows, :]
            g = norm_back(c, self.v(VAG), n, b.r1[rows, 0:1])
            b.second[rows, :] = g
            low = g.astype(BF)
            b.nl[rows, :] = low
            return sums[0] + column_total(c * n), sums[1] + column_total(c), sums[2] + column_total(low)

        zero = jnp.zeros((1, WIDTH), F32)
        sums = lax.fori_loop(0, TOKENS // 32, body, (zero, zero, zero))
        self.gvec[VAG:VAG + 1, :], self.gvec[VAS:VAS + 1, :], self.gvec[VO:VO + 1, :] = sums

    def out_grads(self):
        b = self.b
        for n in range(3):
            cols = slice(n * 256, n * 256 + 256)
            self.grads[0][3, :, cols] = mm_tn(b.mixed[...], b.nl[:, cols]).astype(BF)
        for n in range(3):
            cols = slice(n * 256, n * 256 + 256)
            b.mixed[:, cols] = mm_nt(b.nl[...], self.slabs[0].at[3][cols, :]).astype(BF)

    def attend_back(self, p):
        b = self.b
        masks = half_masks()
        cols = slice(p * LANES, p * LANES + LANES)

        def body(s, _):
            rows = pl.ds(pl.multiple_of(s * SEQ, SEQ), SEQ)
            q, k, v, do = b.q[rows, cols], b.k[rows, cols], b.v[rows, cols], b.mixed[rows, cols]
            dq = dk = dv = 0.0
            for a in range(2):
                att = b.p[s * 12 + p * 2 + a]
                do_a = do * masks[a]
                dv = dv + mm(att.astype(BF), do_a)
                dp = mm_nt(v, do_a)
                ds = (att * (dp - jnp.sum(att * dp, 0, keepdims=True))).astype(BF)
                dk = dk + mm(ds, q * masks[a])
                dq = dq + mm_tn(k * masks[a], ds)
            b.gpre[0, rows, cols] = (dq.T * 0.125).astype(BF)
            b.gpre[1, rows, cols] = dk.astype(BF)
            b.gpre[2, rows, cols] = dv.astype(BF)
            return 0

        lax.fori_loop(0, 2, body, 0)
        both = mm(b.xt[...], jnp.concatenate([b.gpre[0, :, cols], b.gpre[1, :, cols]], 1))
        self.grads[0][0, :, cols] = both[:, :LANES].astype(BF)
        self.grads[0][1, :, cols] = both[:, LANES:].astype(BF)
        self.grads[0][2, :, cols] = mm(b.xt[...], b.gpre[2, :, cols]).astype(BF)

    def qkv_totals(self):
        b = self.b
        self.gvec[VQ:VQ + 1, :] = column_total(b.gpre[0])
        self.gvec[VV:VV + 1, :] = column_total(b.gpre[2])

    def input_grad(self, n):
        b = self.b
        cols = slice(n * 256, n * 256 + 256)
        acc = b.second[:, cols]
        for j in range(3):
            acc = acc + mm_nt(b.gpre[j], self.slabs[0].at[j][cols, :])
        b.second[:, cols] = acc


BUFFERS = dict(
    q=((TOKENS, WIDTH), BF), k=((TOKENS, WIDTH), BF), v=((TOKENS, WIDTH), BF), p=((24, SEQ, SEQ), F32),
    mixed=((TOKENS, WIDTH), BF), n1=((TOKENS, WIDTH), F32), r1=((TOKENS, LANES), F32), nl=((TOKENS, WIDTH), BF),
    act=((4, TOKENS, WIDTH), BF), gp=((4, TOKENS, WIDTH), F32), second=((TOKENS, WIDTH), F32),
    gpre=((4, TOKENS, WIDTH), BF), xt=((WIDTH, TOKENS), BF), nlt=((WIDTH, TOKENS), BF),
)


START = {16: 0, 8: 16, 4: 24, 2: 28, 1: 30}
VLINKS = (CORE, Y1, Y3, X1, Z1, Z3)
EVERY = ((0, 2), (0, 4), (0, 2), (0, 2))
SCRATCH = dict(
    wa=(SHAPES[0], BF), wb=(SHAPES[1], BF), wc=(SHAPES[2], BF), ga=(SHAPES[0], BF),
    rdb=((2, 1, 4, 2, 2, UNIT, WIDTH), BF), rdc=((4, 2, 2, 2, 1, UNIT, WIDTH), BF),
    rk=((3, 31, UNIT, WIDTH), BF), rx=((3, UNIT, WIDTH), BF), tall=((2, UNIT, WIDTH), F32),
    stage=((2, 4, 16, WIDTH), F32), landed=((2, 4, 16, WIDTH), F32),
    vt=((64, 8, LANES), F32), gv=((64, 8, LANES), F32), rv=((64, 8, LANES), F32),
    vec=((16, WIDTH), F32), gvec=((16, WIDTH), F32),
    x=((TOKENS, WIDTH), BF),
)
SEMS = dict(
    loads=(4,), mate_send=(2, 3), mate_recv=(2, 3), send=(3, PARTS, 5), recv=(3, PARTS, 5),
    sib_send=(3, PARTS), sib_recv=(3, PARTS), vsend=(6,), vrecv=(6,),
    gsib_send=(3, PARTS), gsib_recv=(3, PARTS), gsend=(3, PARTS, 5), grecv=(3, PARTS, 5),
    rep_send=(3,), rep_recv=(3,), gmate_send=(2, 3), gmate_recv=(2, 3), gvsend=(7,), gvrecv=(7,),
)


def box_count(box):
    return box[0][1] * box[1][1] * box[2][1] * box[3][1]


def split3(value):
    high = value.astype(BF)
    rest = value - high.astype(F32)
    mid = rest.astype(BF)
    return high, mid, (rest - mid.astype(F32)).astype(BF)


def owner_masks(block):
    d = lax.broadcasted_iota(jnp.int32, (64, WIDTH), 0)
    c = lax.broadcasted_iota(jnp.int32, (64, WIDTH), 1)
    if block is None:
        return d == (c * 43691) >> 19
    return d == 16 * block + ((c * 43691) >> 21)


def lane_picks(row):
    c = lax.broadcasted_iota(jnp.int32, (WIDTH, LANES), 0)
    lane = lax.broadcasted_iota(jnp.int32, (WIDTH, LANES), 1)
    if row is None:
        return (lane == c - 48 * ((c * 43691) >> 21)).astype(F32).astype(BF)
    return (lane == 12 * row + c - 12 * ((c * 43691) >> 19)).astype(F32).astype(BF)


def mega_kernel(lengths, vec_in, qkv_in, out_in, up_in, down_in, x_in, og_in,
                enc_out, sgrad_out, oqkv, oout, oup, odown, ovec, *scratch):
    r = b = types.SimpleNamespace(**dict(zip([*SCRATCH, *BUFFERS, *SEMS], scratch)))
    here = position()
    me = member_of(here)
    sibling = hop(here, CORE)
    twin = hop(here, X2)
    dp = device_of(here)[0]
    weights = (r.wa, r.wb, r.wc)
    grads = (r.ga, r.wb, r.wc)
    rds = (r.act.at[pl.ds(0, 3)].reshape((2, 1, 4, 2, 2, UNIT, WIDTH)), r.rdb, r.rdc)
    slabs = [w.reshape(4, WIDTH, WIDTH) for w in weights]
    gslabs = [w.reshape(4, WIDTH, WIDTH) for w in grads]
    layer = Layer(slabs, gslabs, r.vec, lengths, r.x, r.x, r.x, r.gvec, b)

    def own_at(phase):
        ylow, z, x, yhigh = (s for s, n in own_box(here))
        return (ylow, here.core, z, x, yhigh) if phase < 2 else (z, x, yhigh, ylow, here.core)

    def mate_copy(which, k):
        mate = mates(here)[k]
        return remote(r.stage.at[which, member_of(mate)], r.landed.at[which, me],
                      r.mate_send.at[which, k], r.mate_recv.at[which, k], mate)

    def assemble(which):
        for k in range(3):
            mate_copy(which, k).wait()
        for i in range(4):
            @pl.when(me == i)
            def _():
                r.tall[which, 12 * i:12 * i + 12, :] = r.stage[which, i, 0:12, :]

            @pl.when(me != i)
            def _():
                r.tall[which, 12 * i:12 * i + 12, :] = r.landed[which, i, 0:12, :]
        weights[which][own_at(which)] = r.tall[which].astype(BF)

    def gather(phase, step):
        w = weights[phase]
        for part in range(PARTS):
            order = ORDERS[part]
            if step > 0:
                wait_units(w, phase, 1 << (step - 1), part, r.recv.at[phase, part, step - 1])
            if step < 5:
                there = hop(here, order[step])
                for box in boxes(here, order[:step]):
                    view = w.at[slices(phase, here.core, box, part)]
                    remote(view, view, r.send.at[phase, part, step], r.recv.at[phase, part, step], there).start()
            if step >= 4:
                new = boxes(here, order[:4]) if step == 4 else boxes(hop(here, order[4]), order[:4])
                for box in new:
                    view = w.at[slices(phase, here.core, box, part)]
                    remote(view, view, r.sib_send.at[phase, part], r.sib_recv.at[phase, part], sibling).start()

    def gathered(phase):
        for part in range(PARTS):
            wait_units(weights[phase], phase, 32, part, r.sib_recv.at[phase, part])

    def gather_sent(phase):
        for part in range(PARTS):
            wait_units(weights[phase], phase, 32, part, r.sib_send.at[phase, part])
            for s in range(5):
                wait_units(weights[phase], phase, 1 << s, part, r.send.at[phase, part, s])

    def vec_copy(k):
        n = 1 << k
        view = r.vt.at[pl.ds(dp // n * n, n)]
        return remote(view, view, r.vsend.at[k], r.vrecv.at[k], hop(here, VLINKS[k]))

    def vec_next(k):
        vec_copy(k - 1).wait()
        if k < 6:
            vec_copy(k).start()

    def expand():
        first = r.vt[:, 0, :].astype(BF)
        second = r.vt[:, 1, :].astype(BF)
        mask = owner_masks(None)
        for row in range(8):
            t = mm_nt(first, lane_picks(row))
            r.vec[row:row + 1, :] = jnp.sum(jnp.where(mask, t, 0.0), 0, keepdims=True)
        t = mm_nt(second, lane_picks(None))
        for j in range(4):
            r.vec[8 + j:9 + j, :] = jnp.sum(jnp.where(owner_masks(j), t, 0.0), 0, keepdims=True)

    def sib_slices(phase, part):
        cols = pl.ds(part * LANES, LANES)
        if phase < 2:
            return (slice(None), pl.ds(0, 1), slice(None), slice(None), slice(None), slice(None), cols)
        return (slice(None), slice(None), slice(None), slice(None), pl.ds(0, 1), slice(None), cols)

    def sib_copy(phase, part):
        return remote(grads[phase].at[slices(phase, 1 - here.core, EVERY, part)], rds[phase].at[sib_slices(phase, part)],
                      r.gsib_send.at[phase, part], r.gsib_recv.at[phase, part], sibling)

    def sib_add(phase, part):
        sib_copy(phase, part).wait()
        for z in range(4):
            box = ((0, 2), (z, 1), (0, 2), (0, 2))
            at = slices(phase, here.core, box, part)
            g = grads[phase]
            g[at] = g[at] + rds[phase][slices(phase, 0, box, part)]

    def hop_start(phase, part, step):
        order = ORDERS[part]
        there = hop(here, order[step])
        at = START[1 << step]
        for box in boxes(there, order[:step]):
            n = box_count(box)
            src = grads[phase].at[slices(phase, here.core, box, part)]
            dst = r.rk.at[phase, pl.ds(at, n)].reshape(src.shape[:5] + (UNIT, WIDTH)).at[:, :, :, :, :, :, pl.ds(part * LANES, LANES)]
            remote(src, dst, r.gsend.at[phase, part, step], r.grecv.at[phase, part, step], there).start()
            at += n

    def hop_add(phase, part, step):
        n = 1 << step
        at = START[n]
        cols = pl.ds(part * LANES, LANES)
        view = r.rk.at[phase, pl.ds(at, n), :, cols]
        pltpu.make_async_copy(view, view, r.grecv.at[phase, part, step]).wait()
        for box in boxes(here, ORDERS[part][:step]):
            m = box_count(box)
            g = grads[phase]
            where = slices(phase, here.core, box, part)
            old = g[where]
            g[where] = old + r.rk[phase, at:at + m, :, part * LANES:(part + 1) * LANES].reshape(old.shape)
            at += m

    def rep_copy(phase):
        return remote(grads[phase].at[own_at(phase)], r.rx.at[phase], r.rep_send.at[phase], r.rep_recv.at[phase], twin)

    def reduce_sib(phase):
        for part in range(PARTS):
            sib_copy(phase, part).start()

    def reduce_first(phase, parts=range(PARTS)):
        for part in parts:
            sib_add(phase, part)
            hop_start(phase, part, 4)

    def reduce(phase, step):
        for part in range(PARTS):
            hop_add(phase, part, step)
            if step > 0:
                hop_start(phase, part, step - 1)
        if step == 0:
            rep_copy(phase).start()

    def gmate_copy(which, k):
        mate = mates(here)[k]
        return remote(r.stage.at[which, member_of(mate)], r.landed.at[which, me],
                      r.gmate_send.at[which, k], r.gmate_recv.at[which, k], mate)

    def reduce_last(phase):
        rep_copy(phase).wait()
        total = grads[phase][own_at(phase)].astype(F32) + r.rx[phase].astype(F32)
        if phase == 2:
            odown[...] = total
            return
        r.tall[phase] = total
        for i in range(4):
            r.stage[phase, i, 0:12, :] = r.tall[phase, 12 * i:12 * i + 12, :]
        for k in range(3):
            gmate_copy(phase, k).start()

    def deliver(phase):
        for k in range(3):
            gmate_copy(phase, k).wait()
        for i in range(4):
            cols = pl.ds(i * WIDTH, WIDTH)
            dst = oup.at[:, cols] if phase else (oqkv.at[:, cols] if i < 3 else oout)

            @pl.when(me == i)
            def _():
                dst[...] = r.stage[phase, i, 0:12, :]

            @pl.when(me != i)
            def _():
                dst[...] = r.landed[phase, i, 0:12, :]

    def reduce_sent(phase):
        for part in range(PARTS):
            for step in range(5):
                n = 1 << step
                view = r.rk.at[phase, pl.ds(START[n], n), :, pl.ds(part * LANES, LANES)]
                pltpu.make_async_copy(view, view, r.gsend.at[phase, part, step]).wait()

    def pack_rows(rows):
        mask = owner_masks(None)
        first = jnp.zeros((64, LANES), F32)
        for row in rows:
            value = jnp.where(mask, jnp.broadcast_to(r.gvec[row:row + 1, :], (64, WIDTH)), 0.0)
            picks = lane_picks(row)
            for piece in split3(value):
                first = first + mm(piece, picks)
        return first

    def pack():
        second = jnp.zeros((64, LANES), F32)
        picks = lane_picks(None)
        for j in range(4):
            value = jnp.where(owner_masks(j), jnp.broadcast_to(r.gvec[8 + j:9 + j, :], (64, WIDTH)), 0.0)
            for piece in split3(value):
                second = second + mm(piece, picks)
        r.gv[:, 0, :] = pack_rows((VO, VAG, VAS, VD, VFG, VFS))
        r.gv[:, 1, :] = second

    def gvec_copy(k):
        if k < 6:
            n = 32 >> k
            there = hop(here, VLINKS[5 - k])
            to = device_of(there)[0]
            src, dst = r.gv.at[pl.ds(to // n * n, n)], r.rv.at[pl.ds(64 - 2 * n, n)]
        else:
            there, src, dst = twin, r.gv.at[pl.ds(dp, 1)], r.rv.at[pl.ds(63, 1)]
        return remote(src, dst, r.gvsend.at[k], r.gvrecv.at[k], there)

    def gvec_next(k):
        gvec_copy(k).wait()
        n = 32 >> k if k < 6 else 1
        lo = 64 - 2 * n if k < 6 else 63
        mine = pl.ds(dp // n * n, n)
        r.gv[mine] = r.gv[mine] + r.rv[lo:lo + n]
        if k < 6:
            gvec_copy(k + 1).start()

    x_load = pltpu.make_async_copy(x_in, r.x, r.loads.at[0])
    og_load = pltpu.make_async_copy(og_in, r.x, r.loads.at[1])
    x_load.start()
    near = [hop(here, link) for link in (Y1, Y3, Z1, Z3, X1, X3, CORE, X2)] + [mates(here)[2]]
    barrier = pltpu.get_barrier_semaphore()
    for place in near:
        pl.semaphore_signal(barrier, inc=1, device_id=device_of(place), device_id_type=MESH)
    for i in range(4):
        r.stage[0, i, 0:12, :] = (qkv_in[:, i * WIDTH:(i + 1) * WIDTH] if i < 3 else out_in[...]).astype(F32)
        r.stage[1, i, 0:12, :] = up_in[:, i * WIDTH:(i + 1) * WIDTH].astype(F32)
    r.vt[dp] = vec_in[...]
    weights[2][own_at(2)] = down_in[...]
    pl.semaphore_wait(barrier, len(near))
    for which in range(2):
        for k in range(3):
            mate_copy(which, k).start()
    vec_copy(0).start()
    assemble(0)
    gather(0, 0)
    assemble(1)
    gather(1, 0)
    vec_next(1)
    gather(2, 0)
    gather(0, 1)
    vec_next(2)
    gather(1, 1)
    gather(0, 2)
    vec_next(3)
    gather(2, 1)
    gather(0, 3)
    vec_next(4)
    gather(1, 2)
    gather(2, 2)
    gather(0, 4)
    vec_next(5)
    x_load.wait()
    b.xt[...] = r.x[...].T
    gather(1, 3)
    vec_next(6)
    expand()
    gather(0, 5)
    gathered(0)
    gather(1, 4)
    gather(2, 3)
    layer.project()
    gather(2, 4)
    layer.attend()
    gather(1, 5)
    layer.attn_out()
    og_load.start()
    b.nlt[...] = b.nl[...].T
    gather(2, 5)
    gathered(1)
    layer.feed()
    og_load.wait()
    gathered(2)
    layer.feed_out()
    enc_store = pltpu.make_async_copy(r.x, enc_out, r.loads.at[2])
    enc_store.start()
    layer.feed_back()
    gather_sent(2)
    layer.down_grads()
    reduce_sib(2)
    layer.norm1_back()
    reduce_first(2)
    layer.norm1_rows()
    gather_sent(1)
    layer.up_grads()
    reduce_sib(1)
    reduce(2, 4)
    layer.out_grads()
    reduce_first(1)
    reduce(2, 3)
    pack()
    for p in range(PARTS):
        layer.attend_back(p)
        sib_copy(0, p).start()
        if p > 0:
            reduce_first(0, (p - 1,))
        if p < 3:
            reduce(2, 2 - p)
        elif p == 3:
            reduce_last(2)
        if p < 5:
            reduce(1, 4 - p)
        else:
            reduce_last(1)
    layer.qkv_totals()
    r.gv[:, 0, :] = r.gv[:, 0, :] + pack_rows((VQ, VV))
    gvec_copy(0).start()
    layer.input_grad(0)
    reduce_first(0, (5,))
    layer.input_grad(1)
    gvec_next(0)
    layer.input_grad(2)
    sgrad_store = pltpu.make_async_copy(b.second, sgrad_out, r.loads.at[3])
    sgrad_store.start()
    for step in range(4, -1, -1):
        reduce(0, step)
        gvec_next(5 - step)
    deliver(1)
    reduce_last(0)
    gvec_next(6)
    ovec[...] = r.gv[dp]
    deliver(0)
    for phase in range(3):
        reduce_sent(phase)
    gather_sent(0)
    enc_store.wait()
    sgrad_store.wait()


def run_layer(lengths, vec_in, qkv, out, up, down, x, og):
    vm = pl.BlockSpec(memory_space=pltpu.VMEM)
    hb = pl.BlockSpec(memory_space=pl.ANY)
    return pl.pallas_call(
        mega_kernel,
        out_shape=[
            jax.ShapeDtypeStruct((TOKENS, WIDTH), BF), jax.ShapeDtypeStruct((TOKENS, WIDTH), F32),
            jax.ShapeDtypeStruct((12, 3 * WIDTH), F32), jax.ShapeDtypeStruct((12, WIDTH), F32),
            jax.ShapeDtypeStruct((12, 4 * WIDTH), F32), jax.ShapeDtypeStruct((UNIT, WIDTH), F32), jax.ShapeDtypeStruct((8, LANES), F32),
        ],
        in_specs=[pl.BlockSpec(memory_space=pltpu.SMEM)] + [vm] * 5 + [hb] * 2,
        out_specs=[hb, hb] + [vm] * 5,
        scratch_shapes=[pltpu.VMEM(s, d) for s, d in SCRATCH.values()] + [pltpu.VMEM(s, d) for s, d in BUFFERS.values()]
        + [pltpu.SemaphoreType.DMA(s) for s in SEMS.values()],
        compiler_params=pltpu.CompilerParams(collective_id=1, has_side_effects=True, vmem_limit_bytes=63 * 2**20),
    )(lengths, vec_in, qkv, out, up, down, x, og)


def local(states, qkv_weight, query_bias, value_bias, out_weight, out_bias, attn_gain, attn_shift, up_weight, up_bias,
          down_weight, down_bias, ffn_gain, ffn_shift, out_grad, lengths):
    short = (query_bias, value_bias, out_bias, attn_gain, attn_shift, down_bias, ffn_gain, ffn_shift)
    rows = jnp.stack([jnp.pad(jnp.concatenate(short), (0, 32)), jnp.pad(up_bias, (0, 80))])
    vec_in = jnp.pad(rows, ((0, 6), (0, 0))).astype(F32)
    enc, sgrad, oqkv, oout, oup, odown, ovec = run_layer(
        lengths, vec_in, qkv_weight, out_weight, up_weight, down_weight,
        states.reshape(TOKENS, WIDTH), out_grad.reshape(TOKENS, WIDTH))
    o = [ovec[0, 12 * i:12 * i + 12] for i in range(8)]
    return (enc.reshape(states.shape), sgrad.reshape(states.shape), oqkv, o[0], o[1], oout, o[2], o[3], o[4],
            oup, ovec[1, :48], odown, o[5], o[6], o[7])


def solution(mesh):
    return jax.shard_map(
        local,
        mesh=mesh,
        in_specs=(
            P(None, ("dp", "rep"), None, None),
            P("dp", None),
            P("dp"),
            P("dp"),
            P("dp", None),
            P("dp"),
            P("dp"),
            P("dp"),
            P("dp", None),
            P("dp"),
            P("dp", None),
            P("dp"),
            P("dp"),
            P("dp"),
            P(None, ("dp", "rep"), None, None),
            P(None, ("dp", "rep")),
        ),
        out_specs=(
            P(None, ("dp", "rep"), None, None),
            P(None, ("dp", "rep"), None, None),
            P("dp", None),
            P("dp"),
            P("dp"),
            P("dp", None),
            P("dp"),
            P("dp"),
            P("dp"),
            P("dp", None),
            P("dp"),
            P("dp", None),
            P("dp"),
            P("dp"),
            P("dp"),
        ),
        check_vma=False,
    )
```

time: 1720 us -> 180 us (0.10); the launches traced: 1700 us -> 180 us
  blocking collectives: 722 us -> 0 us
  waiting for transfers between devices: 647 us -> 0 us
  Pallas kernels: 0 us -> 163 us
  local copies, waits for them, and re-layouts: 116 us -> 16.1 us
  starting transfers between devices: 93.1 us -> 0 us
  matrix products: 77.4 us -> 0 us
  other arithmetic: 23.3 us -> 0.6 us
  between operations: 19.2 us -> 0.69 us
    unnamed x3 -> x0, blocking collectives: 713 us -> none
    reduce_scatter x1 -> x0, waiting for transfers between devices: 295 us -> none  [local(): lax.psum_scatter(gradients[9], 'dp', scatter_dimension=0, tiled=True)]
    unnamed x40 -> x0, waiting for transfers between devices: 262 us -> none
    pallas_call x0 -> x1, Pallas kernels: none -> 163 us  [run_layer(): pl.pallas_call(mega_kernel, out_shape=[jax.ShapeDtypeStruct((TOKENS, WIDT...]
    unnamed x257 -> x17, local copies, waits for them, and re-layouts: 105 us -> 7.14 us
    unnamed x33 -> x0, starting transfers between devices: 92.7 us -> none
    all_gather x4 -> x0, waiting for transfers between devices: 90.1 us -> none  [the longest x1 90.1 us: local(): lax.all_gather(shards[9], 'dp', axis=0, tiled=True)]
    dot_general x36 -> x0, matrix products: 77.4 us -> none  [the longest x8 21.9 us: contract_rows(): lax.dot_general(left, right, (((0,), (0,)), ((), ())), preferred_element_...]
  transfers between devices with their start and end apart: 39 -> 0, of which waited for: 5 -> 0; matrix products, arithmetic and copies ran while one was open for 18% -> 0% of each run, Pallas kernels for 0% -> 0%
where the time goes in v2:
time: 180 us
  Pallas kernels  163 us (91%)
  local copies, waits for them, and re-layouts  16.1 us (9%)
    pallas_call x1, Pallas kernels, run_layer(): pl.pallas_call(mega_kernel, out_shape=[jax.ShapeDtypeStruct((TOKENS, WIDT...  163 us
    unnamed x17, local copies, waits for them, and re-layouts  7.14 us
    concatenate x1, local copies, waits for them, and re-layouts, local(): jnp.concatenate(short)  5.43 us

profile of v2, /device:TPU:1, one launch (start us, length us, event | category | flops | bytes accessed | tf_op | source)
XLA Modules:
  0.0 180.0 jit_solution(8758375861735123649)
XLA Ops:
  0.6 5.4 %concatenate.3 = bf16[96]{0:T(256)(128)(2,1)S(1)} concatenate(bf16[12]{0:T(256)(128)(2,1)} %param.18, bf16[12]{0:T(256)(128)(2,1)} %param.19, bf16[12]{0:T(256)(128)(2,1)} %param.21, bf16[12]{0:T(256)(128)(2,1)} %param.22, bf16[12]{0:T(256)(128)(2,1)} %param.23, bf16[12]{0:T(256)(128)(2,1)} %param.27, bf16[12]{0:T(256)(128)(2,1)} %param.28, bf16[12]{0:T(256)(128)(2,1)} %param.29), dimensions={0} | concatenate | bytes 384 | tf_op jit(solution)/shard_map/concatenate | solution.py:804
  6.1 0.7 pad_bitcast_fusion
  6.7 1.3 copy.31.lengths
  8.0 0.6 fusion.3.vec_in
  8.6 162.6 %shard_map.271 = (bf16[512,768]{1,0:T(8,128)(2,1)}, f32[512,768]{1,0:T(8,128)}, f32[12,2304]{1,0:T(8,128)}, f32[12,768]{1,0:T(8,128)}, f32[12,3072]{1,0:T(8,128)}, /*index=5*/f32[48,768]{1,0:T(8,128)}, f32[8,128]{1,0:T(8,128)}) custom-call(s32[2,1]{1,0:T(2,128)} %copy.31.lengths, f32[8,128]{1,0:T(8,128)} %fusion.3.vec_in, bf16[12,2304]{1,0:T(8,128)(2,1)} %qkv_in.1, ...), custom_call_target="tpu_custom_call" | custom-call | tf_op jit(solution)/shard_map/pallas_call | solution.py:786
  171.2 0.0 copy-start
  171.3 1.3 slice_bitcast_fusion.3
  172.6 1.6 slice_bitcast_fusion
  174.1 2.1 %copy.40 = bf16[2,1,256,768]{3,2,1,0:T(8,128)(2,1)} copy(bf16[2,1,256,768]{3,2,1,0:T(8,128)(2,1)} %bitcast.33) | data formatting | bytes 1572864
  176.2 0.0 copy-done
  176.2 0.0 copy-start.3
  176.2 0.0 copy-start.4
  176.2 0.0 copy-start.1
  176.2 0.0 copy-start.2
  176.2 1.1 copy.41
  177.4 0.0 copy-done.3
  177.4 0.7 copy.42
  178.0 0.0 copy-done.4
  178.0 0.6 copy.43
  178.7 0.0 copy-done.1
  178.7 0.7 copy.44
  179.3 0.0 copy-done.2
  179.3 0.7 copy.45
Async XLA Ops:
  171.2 5.0 %copy-start = (f32[512,768]{1,0:T(8,128)S(1)}, f32[512,768]{1,0:T(8,128)}, u32[]{:S(2)}) copy-start(f32[512,768]{1,0:T(8,128)} %get-tuple-element.23) | copy-start | bytes 4718596
  176.2 1.2 copy-start.3
  176.2 1.8 %copy-start.4 = (f32[12,768]{1,0:T(8,128)S(1)}, f32[12,768]{1,0:T(8,128)}, u32[]{:S(2)}) copy-start(f32[12,768]{1,0:T(8,128)} %get-tuple-element.74) | copy-start | bytes 110596
  176.2 2.5 %copy-start.1 = (f32[12,3072]{1,0:T(8,128)S(1)}, f32[12,3072]{1,0:T(8,128)}, u32[]{:S(2)}) copy-start(f32[12,3072]{1,0:T(8,128)} %get-tuple-element.78) | copy-start | bytes 442372
  176.2 3.1 %copy-start.2 = (f32[48,768]{1,0:T(8,128)S(1)}, f32[48,768]{1,0:T(8,128)}, u32[]{:S(2)}) copy-start(f32[48,768]{1,0:T(8,128)} %get-tuple-element.80) | copy-start | bytes 442372

commit v3 on v2

--- a/solution.py
+++ b/solution.py
@@ -19,6 +19,7 @@
 PARTS = 6
 
 CORE, Y1, Y3, Z1, Z3, X1, X2, X3 = (0, 0), (1, 1), (1, 3), (2, 1), (2, 3), (3, 1), (3, 2), (3, 3)
+Y2, Z2 = (1, 2), (2, 2)
 
 ORDERS = (
     (Z1, Z3, Y1, Y3, X1),
@@ -121,6 +122,18 @@
     return boxes(here, ())[0]
 
 
+def trio(place, order):
+    a, b = hop(place, order[0]), hop(place, order[1])
+    return a, b, hop(a, order[1])
+
+
+def halves(found):
+    if len(found) == 2:
+        return [found[:1], found[1:]]
+    ylow, (start, n), x, yhigh = found[0]
+    return [[(ylow, (start, n // 2), x, yhigh)], [(ylow, (start + n // 2, n // 2), x, yhigh)]]
+
+
 HALF = 256
 SEQ = 256
 TOKENS = 512
@@ -171,18 +184,18 @@
     def v(self, row):
         return self.vec[row:row + 1, :]
 
-    def project(self):
-        b = self.b
-        for j, (dst, row) in enumerate(((b.q, VQ), (b.k, None), (b.v, VV))):
-            for n in range(3):
-                cols = slice(n * 256, n * 256 + 256)
-                acc = mm(self.x[...], self.slabs[0].at[j][:, cols])
-                if row is not None:
-                    acc = acc + self.vec[row:row + 1, cols]
-                low = acc.astype(BF)
-                if j == 0:
-                    low = (low.astype(F32) * 0.125).astype(BF)
-                dst[:, cols] = low
+    def project(self, j):
+        b = self.b
+        dst, row = ((b.q, VQ), (b.k, None), (b.v, VV))[j]
+        for n in range(3):
+            cols = slice(n * 256, n * 256 + 256)
+            acc = mm(self.x[...], self.slabs[0].at[j][:, cols])
+            if row is not None:
+                acc = acc + self.vec[row:row + 1, cols]
+            low = acc.astype(BF)
+            if j == 0:
+                low = (low.astype(F32) * 0.125).astype(BF)
+            dst[:, cols] = low
 
     def attend(self):
         b = self.b
@@ -193,7 +206,7 @@
             rows = pl.ds(pl.multiple_of(s * SEQ, SEQ), SEQ)
             cols = pl.ds(pl.multiple_of(p * LANES, LANES), LANES)
             q, k, v = b.q[rows, cols], b.k[rows, cols], b.v[rows, cols]
-            length = self.lengths[s, 0]
+            length = self.lengths[0, s]
             key = lax.broadcasted_iota(jnp.int32, (SEQ, SEQ), 0)
             out = None
             for a in range(2):
@@ -269,55 +282,39 @@
         sums = lax.fori_loop(0, TOKENS // 32, body, (zero, zero, zero))
         self.gvec[VFG:VFG + 1, :], self.gvec[VFS:VFS + 1, :], self.gvec[VD:VD + 1, :] = sums
 
-    def down_grads(self):
-        b = self.b
-
-        def body(j, _):
-            for n in range(3):
-                cols = slice(n * 256, n * 256 + 256)
-                self.grads[2][j, :, cols] = mm_tn(b.act[j], b.nl[:, cols]).astype(BF)
-            return 0
-
-        lax.fori_loop(0, 4, body, 0)
-
-    def feed_back(self):
-        b = self.b
-
-        def body(j, _):
-            w = self.slabs[2].at[j]
-            for n in range(3):
-                cols = slice(n * 256, n * 256 + 256)
-                total = jnp.zeros((1, 256), F32)
-                for h in range(2):
-                    rows = slice(h * 256, h * 256 + 256)
-                    acc = mm_nt(b.nl[rows, :], w[cols, :])
-                    low = (acc * b.gp[j, rows, cols]).astype(BF)
-                    b.gpre[j, rows, cols] = low
-                    total = total + column_total(low)
-                self.gvec[pl.ds(VUP + j, 1), cols] = total
-            return 0
-
-        lax.fori_loop(0, 4, body, 0)
-
-    def up_grads(self):
-        b = self.b
-
-        def body(j, _):
-            for n in range(3):
-                cols = slice(n * 256, n * 256 + 256)
-                self.grads[1][j, :, cols] = mm(b.nlt[...], b.gpre[j, :, cols]).astype(BF)
-            return 0
-
-        lax.fori_loop(0, 4, body, 0)
-
-    def norm1_back(self):
+    def down_grads(self, j):
         b = self.b
         for n in range(3):
             cols = slice(n * 256, n * 256 + 256)
-            acc = b.second[:, cols]
-            for j in range(4):
-                acc = acc + mm_nt(b.gpre[j], self.slabs[1].at[j][cols, :])
-            b.second[:, cols] = acc
+            self.grads[2][j, :, cols] = mm_tn(b.act[j], b.nl[:, cols]).astype(BF)
+
+    def feed_back(self, j):
+        b = self.b
+        w = self.slabs[2].at[j]
+        for n in range(3):
+            cols = slice(n * 256, n * 256 + 256)
+            total = jnp.zeros((1, 256), F32)
+            for h in range(2):
+                rows = slice(h * 256, h * 256 + 256)
+                acc = mm_nt(b.nl[rows, :], w[cols, :])
+                low = (acc * b.gp[j, rows, cols]).astype(BF)
+                b.gpre[j, rows, cols] = low
+                total = total + column_total(low)
+            self.gvec[pl.ds(VUP + j, 1), cols] = total
+
+    def up_grads(self, j):
+        b = self.b
+        for n in range(3):
+            cols = slice(n * 256, n * 256 + 256)
+            self.grads[1][j, :, cols] = mm(b.nlt[...], b.gpre[j, :, cols]).astype(BF)
+
+    def norm1_back(self, n):
+        b = self.b
+        cols = slice(n * 256, n * 256 + 256)
+        acc = b.second[:, cols]
+        for j in range(4):
+            acc = acc + mm_nt(b.gpre[j], self.slabs[1].at[j][cols, :])
+        b.second[:, cols] = acc
 
     def norm1_rows(self):
         b = self.b
@@ -341,6 +338,9 @@
         for n in range(3):
             cols = slice(n * 256, n * 256 + 256)
             self.grads[0][3, :, cols] = mm_tn(b.mixed[...], b.nl[:, cols]).astype(BF)
+
+    def out_back(self):
+        b = self.b
         for n in range(3):
             cols = slice(n * 256, n * 256 + 256)
             b.mixed[:, cols] = mm_nt(b.nl[...], self.slabs[0].at[3][cols, :]).astype(BF)
@@ -372,11 +372,8 @@
         self.grads[0][0, :, cols] = both[:, :LANES].astype(BF)
         self.grads[0][1, :, cols] = both[:, LANES:].astype(BF)
         self.grads[0][2, :, cols] = mm(b.xt[...], b.gpre[2, :, cols]).astype(BF)
-
-    def qkv_totals(self):
-        b = self.b
-        self.gvec[VQ:VQ + 1, :] = column_total(b.gpre[0])
-        self.gvec[VV:VV + 1, :] = column_total(b.gpre[2])
+        self.gvec[VQ:VQ + 1, cols] = column_total(b.gpre[0, :, cols])
+        self.gvec[VV:VV + 1, cols] = column_total(b.gpre[2, :, cols])
 
     def input_grad(self, n):
         b = self.b
@@ -395,7 +392,7 @@
 )
 
 
-START = {16: 0, 8: 16, 4: 24, 2: 28, 1: 30}
+START = {16: 0, 8: 16, 4: 24}
 VLINKS = (CORE, Y1, Y3, X1, Z1, Z3)
 EVERY = ((0, 2), (0, 4), (0, 2), (0, 2))
 SCRATCH = dict(
@@ -403,14 +400,14 @@
     rdb=((2, 1, 4, 2, 2, UNIT, WIDTH), BF), rdc=((4, 2, 2, 2, 1, UNIT, WIDTH), BF),
     rk=((3, 31, UNIT, WIDTH), BF), rx=((3, UNIT, WIDTH), BF), tall=((2, UNIT, WIDTH), F32),
     stage=((2, 4, 16, WIDTH), F32), landed=((2, 4, 16, WIDTH), F32),
-    vt=((64, 8, LANES), F32), gv=((64, 8, LANES), F32), rv=((64, 8, LANES), F32),
+    vt=((64, 2, LANES), F32), gv=((64, 2, LANES), F32), rv=((64, 2, LANES), F32),
     vec=((16, WIDTH), F32), gvec=((16, WIDTH), F32),
-    x=((TOKENS, WIDTH), BF),
+    x=((TOKENS, WIDTH), BF), qkv_in=((12, 3 * WIDTH), BF), out_in=((12, WIDTH), BF), up_in=((12, 4 * WIDTH), BF),
 )
 SEMS = dict(
-    loads=(4,), mate_send=(2, 3), mate_recv=(2, 3), send=(3, PARTS, 5), recv=(3, PARTS, 5),
+    loads=(8,), mate_send=(2, 3), mate_recv=(2, 3), send=(3, PARTS, 7), recv=(3, PARTS, 7),
     sib_send=(3, PARTS), sib_recv=(3, PARTS), vsend=(6,), vrecv=(6,),
-    gsib_send=(3, PARTS), gsib_recv=(3, PARTS), gsend=(3, PARTS, 5), grecv=(3, PARTS, 5),
+    gsib_send=(3, PARTS), gsib_recv=(3, PARTS), gsend=(3, PARTS, 6), grecv=(3, PARTS, 6),
     rep_send=(3,), rep_recv=(3,), gmate_send=(2, 3), gmate_recv=(2, 3), gvsend=(7,), gvrecv=(7,),
 )
 
@@ -442,8 +439,9 @@
     return (lane == 12 * row + c - 12 * ((c * 43691) >> 19)).astype(F32).astype(BF)
 
 
-def mega_kernel(lengths, vec_in, qkv_in, out_in, up_in, down_in, x_in, og_in,
-                enc_out, sgrad_out, oqkv, oout, oup, odown, ovec, *scratch):
+def mega_kernel(lengths, *refs):
+    vecs_in, (qkv_in, out_in, up_in, down_in, x_in, og_in,
+               enc_out, sgrad_out, oqkv, oout, oup, odown, ovec), scratch = refs[:9], refs[9:22], refs[22:]
     r = b = types.SimpleNamespace(**dict(zip([*SCRATCH, *BUFFERS, *SEMS], scratch)))
     here = position()
     me = member_of(here)
@@ -479,22 +477,45 @@
                 r.tall[which, 12 * i:12 * i + 12, :] = r.landed[which, i, 0:12, :]
         weights[which][own_at(which)] = r.tall[which].astype(BF)
 
+    def push(phase, part, found, slot, there):
+        w = weights[phase]
+        for box in found:
+            view = w.at[slices(phase, here.core, box, part)]
+            remote(view, view, r.send.at[phase, part, slot], r.recv.at[phase, part, slot], there).start()
+
+    def share(phase, part, found):
+        w = weights[phase]
+        for box in found:
+            view = w.at[slices(phase, here.core, box, part)]
+            remote(view, view, r.sib_send.at[phase, part], r.sib_recv.at[phase, part], sibling).start()
+
+    def gather_first(phase):
+        for part in range(PARTS):
+            for slot, there in enumerate(trio(here, ORDERS[part])):
+                push(phase, part, boxes(here, ()), slot, there)
+
     def gather(phase, step):
         w = weights[phase]
         for part in range(PARTS):
             order = ORDERS[part]
-            if step > 0:
-                wait_units(w, phase, 1 << (step - 1), part, r.recv.at[phase, part, step - 1])
-            if step < 5:
-                there = hop(here, order[step])
-                for box in boxes(here, order[:step]):
-                    view = w.at[slices(phase, here.core, box, part)]
-                    remote(view, view, r.send.at[phase, part, step], r.recv.at[phase, part, step], there).start()
-            if step >= 4:
-                new = boxes(here, order[:4]) if step == 4 else boxes(hop(here, order[4]), order[:4])
-                for box in new:
-                    view = w.at[slices(phase, here.core, box, part)]
-                    remote(view, view, r.sib_send.at[phase, part], r.sib_recv.at[phase, part], sibling).start()
+            if step == 2:
+                for slot in range(3):
+                    wait_units(w, phase, 1, part, r.recv.at[phase, part, slot])
+            else:
+                wait_units(w, phase, 1 << (step - 1), part, r.recv.at[phase, part, step])
+            there = hop(here, order[step])
+            if step < 4:
+                push(phase, part, boxes(here, order[:step]), step + 1, there)
+            else:
+                for half, found in enumerate(halves(boxes(here, order[:4]))):
+                    push(phase, part, found, 5 + half, there)
+                share(phase, part, boxes(here, order[:4]))
+
+    def gather_last(phase, half):
+        for part in range(PARTS):
+            order = ORDERS[part]
+            wait_units(weights[phase], phase, 8, part, r.recv.at[phase, part, 5 + half])
+            share(phase, part, halves(boxes(hop(here, order[4]), order[:4]))[half])
 
     def gathered(phase):
         for part in range(PARTS):
@@ -503,8 +524,8 @@
     def gather_sent(phase):
         for part in range(PARTS):
             wait_units(weights[phase], phase, 32, part, r.sib_send.at[phase, part])
-            for s in range(5):
-                wait_units(weights[phase], phase, 1 << s, part, r.send.at[phase, part, s])
+            for slot, n in enumerate((1, 1, 1, 4, 8, 8, 8)):
+                wait_units(weights[phase], phase, n, part, r.send.at[phase, part, slot])
 
     def vec_copy(k):
         n = 1 << k
@@ -527,68 +548,95 @@
         for j in range(4):
             r.vec[8 + j:9 + j, :] = jnp.sum(jnp.where(owner_masks(j), t, 0.0), 0, keepdims=True)
 
-    def sib_slices(phase, part):
-        cols = pl.ds(part * LANES, LANES)
-        if phase < 2:
-            return (slice(None), pl.ds(0, 1), slice(None), slice(None), slice(None), slice(None), cols)
-        return (slice(None), slice(None), slice(None), slice(None), pl.ds(0, 1), slice(None), cols)
-
-    def sib_copy(phase, part):
-        return remote(grads[phase].at[slices(phase, 1 - here.core, EVERY, part)], rds[phase].at[sib_slices(phase, part)],
-                      r.gsib_send.at[phase, part], r.gsib_recv.at[phase, part], sibling)
-
-    def sib_add(phase, part):
-        sib_copy(phase, part).wait()
-        for z in range(4):
-            box = ((0, 2), (z, 1), (0, 2), (0, 2))
-            at = slices(phase, here.core, box, part)
-            g = grads[phase]
-            g[at] = g[at] + rds[phase][slices(phase, 0, box, part)]
+    def sib_copy(phase, k):
+        g, rd = grads[phase], rds[phase]
+        if phase == 0:
+            cols = pl.ds(k * LANES, LANES)
+            src = g.at[:, pl.ds(sibling.core, 1), :, :, :, :, cols]
+            dst = rd.at[:, :, :, :, :, :, cols]
+        elif phase == 1:
+            src, dst = g.at[k, sibling.core], rd.at[k, 0]
+        else:
+            src, dst = g.at[k, :, :, :, pl.ds(sibling.core, 1)], rd.at[k]
+        return remote(src, dst, r.gsib_send.at[phase, k], r.gsib_recv.at[phase, k], sibling)
+
+    def sib_add(phase, k):
+        sib_copy(phase, k).wait()
+        g, rd = grads[phase], rds[phase]
+        for i in range(4):
+            if phase == 0:
+                at = slices(0, here.core, ((0, 2), (i, 1), (0, 2), (0, 2)), k)
+                g[at] = g[at] + rd[slices(0, 0, ((0, 2), (i, 1), (0, 2), (0, 2)), k)]
+            elif phase == 1:
+                g[k, here.core, i] = g[k, here.core, i] + rd[k, 0, i]
+            else:
+                at = (k, i // 2, i % 2, slice(None), pl.ds(here.core, 1))
+                g[at] = g[at] + rd[k, i // 2, i % 2]
 
     def hop_start(phase, part, step):
         order = ORDERS[part]
+        cols = pl.ds(part * LANES, LANES)
+        if step == 1:
+            for slot, there in enumerate(trio(here, order)):
+                src = grads[phase].at[slices(phase, here.core, boxes(there, ())[0], part)]
+                dst = r.rk.at[phase, pl.ds(28 + slot, 1)].reshape(src.shape[:5] + (UNIT, WIDTH)).at[:, :, :, :, :, :, cols]
+                remote(src, dst, r.gsend.at[phase, part, slot], r.grecv.at[phase, part, slot], there).start()
+            return
         there = hop(here, order[step])
         at = START[1 << step]
         for box in boxes(there, order[:step]):
             n = box_count(box)
             src = grads[phase].at[slices(phase, here.core, box, part)]
-            dst = r.rk.at[phase, pl.ds(at, n)].reshape(src.shape[:5] + (UNIT, WIDTH)).at[:, :, :, :, :, :, pl.ds(part * LANES, LANES)]
-            remote(src, dst, r.gsend.at[phase, part, step], r.grecv.at[phase, part, step], there).start()
+            dst = r.rk.at[phase, pl.ds(at, n)].reshape(src.shape[:5] + (UNIT, WIDTH)).at[:, :, :, :, :, :, cols]
+            remote(src, dst, r.gsend.at[phase, part, step + 1], r.grecv.at[phase, part, step + 1], there).start()
             at += n
 
     def hop_add(phase, part, step):
+        g = grads[phase]
+        cols = slice(part * LANES, part * LANES + LANES)
+        if step == 1:
+            where = slices(phase, here.core, boxes(here, ())[0], part)
+            total = g[where].astype(F32)
+            for slot in range(3):
+                view = r.rk.at[phase, 28 + slot, :, cols]
+                pltpu.make_async_copy(view, view, r.grecv.at[phase, part, slot]).wait()
+                total = total + view[...].astype(F32).reshape(total.shape)
+            g[where] = total.astype(BF)
+            return
         n = 1 << step
         at = START[n]
-        cols = pl.ds(part * LANES, LANES)
         view = r.rk.at[phase, pl.ds(at, n), :, cols]
-        pltpu.make_async_copy(view, view, r.grecv.at[phase, part, step]).wait()
+        pltpu.make_async_copy(view, view, r.grecv.at[phase, part, step + 1]).wait()
         for box in boxes(here, ORDERS[part][:step]):
             m = box_count(box)
-            g = grads[phase]
             where = slices(phase, here.core, box, part)
             old = g[where]
-            g[where] = old + r.rk[phase, at:at + m, :, part * LANES:(part + 1) * LANES].reshape(old.shape)
+            g[where] = old + r.rk[phase, at:at + m, :, cols].reshape(old.shape)
             at += m
 
     def rep_copy(phase):
         return remote(grads[phase].at[own_at(phase)], r.rx.at[phase], r.rep_send.at[phase], r.rep_recv.at[phase], twin)
 
-    def reduce_sib(phase):
+    def reduce_first(phase):
+        for k in range(2 if phase == 1 else 4):
+            sib_add(phase, k)
         for part in range(PARTS):
-            sib_copy(phase, part).start()
-
-    def reduce_first(phase, parts=range(PARTS)):
-        for part in parts:
-            sib_add(phase, part)
             hop_start(phase, part, 4)
+
+    def move(phase, part, step):
+        hop_add(phase, part, step)
+        if step > 1:
+            hop_start(phase, part, step - 1)
 
     def reduce(phase, step):
         for part in range(PARTS):
-            hop_add(phase, part, step)
-            if step > 0:
-                hop_start(phase, part, step - 1)
-        if step == 0:
+            move(phase, part, step)
+        if step == 1:
             rep_copy(phase).start()
+
+    def first_part(part):
+        sib_add(0, part)
+        hop_start(0, part, 4)
 
     def gmate_copy(which, k):
         mate = mates(here)[k]
@@ -624,10 +672,10 @@
 
     def reduce_sent(phase):
         for part in range(PARTS):
-            for step in range(5):
-                n = 1 << step
-                view = r.rk.at[phase, pl.ds(START[n], n), :, pl.ds(part * LANES, LANES)]
-                pltpu.make_async_copy(view, view, r.gsend.at[phase, part, step]).wait()
+            cols = pl.ds(part * LANES, LANES)
+            for slot, n in enumerate((1, 1, 1, 4, 8, 16)):
+                view = r.rk.at[phase, pl.ds(0, n), :, cols]
+                pltpu.make_async_copy(view, view, r.gsend.at[phase, part, slot]).wait()
 
     def pack_rows(rows):
         mask = owner_masks(None)
@@ -668,119 +716,178 @@
         if k < 6:
             gvec_copy(k + 1).start()
 
-    x_load = pltpu.make_async_copy(x_in, r.x, r.loads.at[0])
-    og_load = pltpu.make_async_copy(og_in, r.x, r.loads.at[1])
-    x_load.start()
-    near = [hop(here, link) for link in (Y1, Y3, Z1, Z3, X1, X3, CORE, X2)] + [mates(here)[2]]
+    near = [hop(here, link) for link in (Y1, Y3, Z1, Z3, X1, X3, CORE, X2, Y2, Z2)]
+    near += [mates(here)[2], hop(hop(here, Y3), Z1), hop(hop(here, Y1), Z3)]
     barrier = pltpu.get_barrier_semaphore()
     for place in near:
         pl.semaphore_signal(barrier, inc=1, device_id=device_of(place), device_id_type=MESH)
+    loads = [pltpu.make_async_copy(src, dst, r.loads.at[i]) for i, (src, dst) in enumerate((
+        (qkv_in, r.qkv_in), (out_in, r.out_in), (up_in, r.up_in), (down_in, weights[2].at[own_at(2)]), (x_in, r.x)))]
+    for load in loads:
+        load.start()
+    og_load = pltpu.make_async_copy(og_in, r.x, r.loads.at[5])
+    r.vt[dp] = jnp.zeros((2, LANES), F32)
+    for i in range(8):
+        r.vt[dp, 0:1, 12 * i:12 * i + 12] = vecs_in[i][...].astype(F32)
+    r.vt[dp, 1:2, 0:48] = vecs_in[8][...].astype(F32)
+    for load in loads[:4]:
+        load.wait()
     for i in range(4):
-        r.stage[0, i, 0:12, :] = (qkv_in[:, i * WIDTH:(i + 1) * WIDTH] if i < 3 else out_in[...]).astype(F32)
-        r.stage[1, i, 0:12, :] = up_in[:, i * WIDTH:(i + 1) * WIDTH].astype(F32)
-    r.vt[dp] = vec_in[...]
-    weights[2][own_at(2)] = down_in[...]
+        r.stage[0, i, 0:12, :] = (r.qkv_in[:, i * WIDTH:(i + 1) * WIDTH] if i < 3 else r.out_in[...]).astype(F32)
+        r.stage[1, i, 0:12, :] = r.up_in[:, i * WIDTH:(i + 1) * WIDTH].astype(F32)
     pl.semaphore_wait(barrier, len(near))
     for which in range(2):
         for k in range(3):
             mate_copy(which, k).start()
     vec_copy(0).start()
+    gather_first(2)
+    loads[4].wait()
+    b.xt[...] = r.x[...].T
     assemble(0)
-    gather(0, 0)
+    gather_first(0)
     assemble(1)
-    gather(1, 0)
     vec_next(1)
-    gather(2, 0)
-    gather(0, 1)
+    gather_first(1)
+    gather(0, 2)
     vec_next(2)
-    gather(1, 1)
-    gather(0, 2)
+    gather(2, 2)
+    gather(0, 3)
     vec_next(3)
-    gather(2, 1)
-    gather(0, 3)
+    gather(1, 2)
+    gather(0, 4)
     vec_next(4)
-    gather(1, 2)
-    gather(2, 2)
-    gather(0, 4)
+    gather(1, 3)
     vec_next(5)
-    x_load.wait()
-    b.xt[...] = r.x[...].T
-    gather(1, 3)
+    gather(2, 3)
     vec_next(6)
     expand()
-    gather(0, 5)
+    gather_last(0, 0)
+    gather_last(0, 1)
     gathered(0)
+    layer.project(0)
     gather(1, 4)
-    gather(2, 3)
-    layer.project()
+    layer.project(1)
+    layer.project(2)
     gather(2, 4)
     layer.attend()
-    gather(1, 5)
+    gather_last(1, 0)
+    gather_last(1, 1)
     layer.attn_out()
     og_load.start()
     b.nlt[...] = b.nl[...].T
-    gather(2, 5)
+    gather_last(2, 0)
+    gather_last(2, 1)
     gathered(1)
     layer.feed()
     og_load.wait()
     gathered(2)
     layer.feed_out()
-    enc_store = pltpu.make_async_copy(r.x, enc_out, r.loads.at[2])
+    enc_store = pltpu.make_async_copy(r.x, enc_out, r.loads.at[6])
     enc_store.start()
-    layer.feed_back()
     gather_sent(2)
-    layer.down_grads()
-    reduce_sib(2)
-    layer.norm1_back()
+
+    def down_body(j, _):
+        layer.feed_back(j)
+        layer.down_grads(j)
+        sib_copy(2, j).start()
+        return 0
+
+    lax.fori_loop(0, 4, down_body, 0)
+    for n in range(3):
+        layer.norm1_back(n)
     reduce_first(2)
+    gather_sent(1)
+
+    def up_body(i, _):
+        layer.up_grads(i * 2 + sibling.core)
+        sib_copy(1, i).start()
+        return 0
+
+    def up_own(i, _):
+        layer.up_grads(i * 2 + here.core)
+        return 0
+
+    lax.fori_loop(0, 2, up_body, 0)
+    lax.fori_loop(0, 2, up_own, 0)
     layer.norm1_rows()
-    gather_sent(1)
-    layer.up_grads()
-    reduce_sib(1)
+    reduce_first(1)
+    layer.out_grads()
     reduce(2, 4)
-    layer.out_grads()
-    reduce_first(1)
+    layer.out_back()
+    pack()
+    layer.attend_back(0)
+    sib_copy(0, 0).start()
+    layer.attend_back(1)
+    sib_copy(0, 1).start()
+    reduce(1, 4)
+    first_part(0)
+    layer.attend_back(2)
+    sib_copy(0, 2).start()
     reduce(2, 3)
-    pack()
-    for p in range(PARTS):
-        layer.attend_back(p)
-        sib_copy(0, p).start()
-        if p > 0:
-            reduce_first(0, (p - 1,))
-        if p < 3:
-            reduce(2, 2 - p)
-        elif p == 3:
-            reduce_last(2)
-        if p < 5:
-            reduce(1, 4 - p)
-        else:
-            reduce_last(1)
-    layer.qkv_totals()
+    first_part(1)
+    layer.attend_back(3)
+    sib_copy(0, 3).start()
+    reduce(1, 3)
+    first_part(2)
+    layer.attend_back(4)
+    sib_copy(0, 4).start()
+    reduce(2, 2)
+    first_part(3)
+    layer.attend_back(5)
+    sib_copy(0, 5).start()
+    first_part(4)
     r.gv[:, 0, :] = r.gv[:, 0, :] + pack_rows((VQ, VV))
     gvec_copy(0).start()
+    reduce(1, 2)
     layer.input_grad(0)
-    reduce_first(0, (5,))
+    first_part(5)
+    move(0, 0, 4)
     layer.input_grad(1)
+    move(0, 1, 4)
     gvec_next(0)
     layer.input_grad(2)
-    sgrad_store = pltpu.make_async_copy(b.second, sgrad_out, r.loads.at[3])
+    sgrad_store = pltpu.make_async_copy(b.second, sgrad_out, r.loads.at[7])
     sgrad_store.start()
-    for step in range(4, -1, -1):
-        reduce(0, step)
-        gvec_next(5 - step)
+    reduce(2, 1)
+    move(0, 2, 4)
+    move(0, 0, 3)
+    gvec_next(1)
+    move(0, 3, 4)
+    move(0, 1, 3)
+    reduce(1, 1)
+    gvec_next(2)
+    move(0, 4, 4)
+    move(0, 2, 3)
+    move(0, 0, 2)
+    reduce_last(2)
+    move(0, 5, 4)
+    move(0, 3, 3)
+    move(0, 1, 2)
+    gvec_next(3)
+    move(0, 4, 3)
+    move(0, 2, 2)
+    reduce_last(1)
+    move(0, 5, 3)
+    move(0, 3, 2)
+    move(0, 4, 2)
+    gvec_next(4)
+    move(0, 5, 2)
     deliver(1)
-    reduce_last(0)
+    gvec_next(5)
+    reduce(0, 1)
     gvec_next(6)
     ovec[...] = r.gv[dp]
-    deliver(0)
-    for phase in range(3):
+    reduce_last(0)
+    for phase in range(1, 3):
         reduce_sent(phase)
     gather_sent(0)
+    deliver(0)
+    reduce_sent(0)
     enc_store.wait()
     sgrad_store.wait()
 
 
-def run_layer(lengths, vec_in, qkv, out, up, down, x, og):
+def run_layer(lengths, vecs, qkv, out, up, down, x, og):
     vm = pl.BlockSpec(memory_space=pltpu.VMEM)
     hb = pl.BlockSpec(memory_space=pl.ANY)
     return pl.pallas_call(
@@ -788,27 +895,56 @@
         out_shape=[
             jax.ShapeDtypeStruct((TOKENS, WIDTH), BF), jax.ShapeDtypeStruct((TOKENS, WIDTH), F32),
             jax.ShapeDtypeStruct((12, 3 * WIDTH), F32), jax.ShapeDtypeStruct((12, WIDTH), F32),
-            jax.ShapeDtypeStruct((12, 4 * WIDTH), F32), jax.ShapeDtypeStruct((UNIT, WIDTH), F32), jax.ShapeDtypeStruct((8, LANES), F32),
+            jax.ShapeDtypeStruct((12, 4 * WIDTH), F32), jax.ShapeDtypeStruct((UNIT, WIDTH), F32), jax.ShapeDtypeStruct((2, LANES), F32),
         ],
-        in_specs=[pl.BlockSpec(memory_space=pltpu.SMEM)] + [vm] * 5 + [hb] * 2,
+        in_specs=[pl.BlockSpec(memory_space=pltpu.SMEM)] + [vm] * 9 + [hb] * 6,
         out_specs=[hb, hb] + [vm] * 5,
         scratch_shapes=[pltpu.VMEM(s, d) for s, d in SCRATCH.values()] + [pltpu.VMEM(s, d) for s, d in BUFFERS.values()]
         + [pltpu.SemaphoreType.DMA(s) for s in SEMS.values()],
         compiler_params=pltpu.CompilerParams(collective_id=1, has_side_effects=True, vmem_limit_bytes=63 * 2**20),
-    )(lengths, vec_in, qkv, out, up, down, x, og)
+    )(lengths, *vecs, qkv, out, up, down, x, og)
+
+
+def finish_kernel(*refs):
+    srcs, vec, dsts, vec_outs, held, sems = refs[:6], refs[6], refs[7:13], refs[13:22], refs[22:28], refs[28]
+    loads = [pltpu.make_async_copy(src, mid, sems.at[0, i]) for i, (src, mid) in enumerate(zip(srcs, held))]
+    stores = [pltpu.make_async_copy(mid, dst, sems.at[1, i]) for i, (mid, dst) in enumerate(zip(held, dsts))]
+    for load in loads:
+        load.start()
+    for i in range(8):
+        vec_outs[i][...] = vec[0:1, 12 * i:12 * i + 12]
+    vec_outs[8][...] = vec[1:2, 0:48]
+    for load, store in zip(loads, stores):
+        load.wait()
+        store.start()
+    for store in stores:
+        store.wait()
+
+
+def finish(results):
+    vm = pl.BlockSpec(memory_space=pltpu.VMEM)
+    hb = pl.BlockSpec(memory_space=pl.ANY)
+    return pl.pallas_call(
+        finish_kernel,
+        out_shape=[jax.ShapeDtypeStruct(a.shape, a.dtype) for a in results[:6]]
+        + [jax.ShapeDtypeStruct((1, n), F32) for n in [12] * 8 + [48]],
+        in_specs=[hb] * 6 + [vm],
+        out_specs=[hb] * 6 + [vm] * 9,
+        scratch_shapes=[pltpu.VMEM(a.shape, a.dtype) for a in results[:6]] + [pltpu.SemaphoreType.DMA((2, 6))],
+        compiler_params=pltpu.CompilerParams(vmem_limit_bytes=63 * 2**20),
+    )(*results)
 
 
 def local(states, qkv_weight, query_bias, value_bias, out_weight, out_bias, attn_gain, attn_shift, up_weight, up_bias,
           down_weight, down_bias, ffn_gain, ffn_shift, out_grad, lengths):
-    short = (query_bias, value_bias, out_bias, attn_gain, attn_shift, down_bias, ffn_gain, ffn_shift)
-    rows = jnp.stack([jnp.pad(jnp.concatenate(short), (0, 32)), jnp.pad(up_bias, (0, 80))])
-    vec_in = jnp.pad(rows, ((0, 6), (0, 0))).astype(F32)
-    enc, sgrad, oqkv, oout, oup, odown, ovec = run_layer(
-        lengths, vec_in, qkv_weight, out_weight, up_weight, down_weight,
+    vecs = [v.reshape(1, -1) for v in (query_bias, value_bias, out_bias, attn_gain, attn_shift, down_bias, ffn_gain, ffn_shift, up_bias)]
+    results = run_layer(
+        lengths.reshape(1, 2), vecs, qkv_weight, out_weight, up_weight, down_weight,
         states.reshape(TOKENS, WIDTH), out_grad.reshape(TOKENS, WIDTH))
-    o = [ovec[0, 12 * i:12 * i + 12] for i in range(8)]
+    enc, sgrad, oqkv, oout, oup, odown, *o = finish(results)
+    o = [v.reshape(-1) for v in o]
     return (enc.reshape(states.shape), sgrad.reshape(states.shape), oqkv, o[0], o[1], oout, o[2], o[3], o[4],
-            oup, ovec[1, :48], odown, o[5], o[6], o[7])
+            oup, o[8], odown, o[5], o[6], o[7])
 
 
 def solution(mesh):

time: 180 us -> 145 us (0.81)
  Pallas kernels: 163 us -> 144 us
  local copies, waits for them, and re-layouts: 16.1 us -> 0 us
    pallas_call x1, Pallas kernels: 163 us -> 140 us  [run_layer(): pl.pallas_call(mega_kernel, out_shape=[jax.ShapeDtypeStruct((TOKENS, WIDT...]
    unnamed x17 -> x0, local copies, waits for them, and re-layouts: 7.14 us -> none
    concatenate x1 -> x0, local copies, waits for them, and re-layouts: 5.43 us -> none  [local(): jnp.concatenate(short)]
    pallas_call x0 -> x1, Pallas kernels: none -> 4.29 us  [finish(): pl.pallas_call(finish_kernel, out_shape=[jax.ShapeDtypeStruct(a.shape, a....]
    squeeze x2 -> x0, local copies, waits for them, and re-layouts: 2.89 us -> none  [the longest x1 1.58 us: local(): o = [ovec[0, 12 * i:12 * i + 12] for i in range(8)]]
where the time goes in v3:
time: 145 us
  Pallas kernels  144 us (99%)
    pallas_call x1, Pallas kernels, run_layer(): pl.pallas_call(mega_kernel, out_shape=[jax.ShapeDtypeStruct((TOKENS, WIDT...  140 us
    pallas_call x1, Pallas kernels, finish(): pl.pallas_call(finish_kernel, out_shape=[jax.ShapeDtypeStruct(a.shape, a....  4.29 us

profile of v3, /device:TPU:1, one launch (start us, length us, event | category | flops | bytes accessed | tf_op | source)
XLA Modules:
  0.0 145.0 jit_solution(8685271794272863872)
XLA Ops:
  0.7 139.9 %shard_map.271 = (bf16[512,768]{1,0:T(8,128)(2,1)}, f32[512,768]{1,0:T(8,128)}, f32[12,2304]{1,0:T(8,128)}, f32[12,768]{1,0:T(8,128)}, f32[12,3072]{1,0:T(8,128)}, /*index=5*/f32[48,768]{1,0:T(8,128)}, f32[2,128]{1,0:T(2,128)}) custom-call(s32[1,2]{1,0:T(1,128)} %bitcast.29, bf16[1,12]{1,0:T(2,128)(2,1)} %bitcast.30, bf16[1,12]{1,0:T(2,128)(2,1)} %bitcast.31, ...), custom_call_target="tpu_custom_call" | custom-call | tf_op jit(solution)/shard_map/pallas_call | solution.py:893
  140.6 4.3 %shard_map.272 = (bf16[512,768]{1,0:T(8,128)(2,1)}, f32[512,768]{1,0:T(8,128)}, f32[12,2304]{1,0:T(8,128)}, f32[12,768]{1,0:T(8,128)}, f32[12,3072]{1,0:T(8,128)...) custom-call(bf16[512,768]{1,0:T(8,128)(2,1)} %get-tuple-element.37.r, ...), custom_call_target="tpu_custom_call" | custom-call | tf_op jit(solution)/shard_map/pallas_call | solution.py:927

commit v4 on v3

--- a/solution.py
+++ b/solution.py
@@ -137,6 +137,7 @@
 HALF = 256
 SEQ = 256
 TOKENS = 512
+ROWS = 64
 epsilon = 1e-05
 NT = (((1,), (1,)), ((), ()))
 TN = (((0,), (0,)), ((), ()))
@@ -200,27 +201,27 @@
     def attend(self):
         b = self.b
         masks = half_masks()
-
-        def body(i, _):
-            s, p = i // 6, i % 6
-            rows = pl.ds(pl.multiple_of(s * SEQ, SEQ), SEQ)
+        key = lax.broadcasted_iota(jnp.int32, (SEQ, SEQ), 0)
+
+        def body(p, _):
             cols = pl.ds(pl.multiple_of(p * LANES, LANES), LANES)
-            q, k, v = b.q[rows, cols], b.k[rows, cols], b.v[rows, cols]
-            length = self.lengths[0, s]
-            key = lax.broadcasted_iota(jnp.int32, (SEQ, SEQ), 0)
-            out = None
-            for a in range(2):
-                st = mm_nt(k * masks[a], q)
-                st = jnp.where(key < length, st, -1e9)
-                e = jnp.exp(st - jnp.max(st, 0, keepdims=True))
-                att = e * (1.0 / jnp.sum(e, 0, keepdims=True))
-                b.p[i * 2 + a] = att
-                o = mm_tn(v * masks[a], att.astype(BF))
-                out = o if out is None else out + o
-            b.mixed[rows, cols] = out.T.astype(BF)
+            for s in range(2):
+                rows = slice(s * SEQ, s * SEQ + SEQ)
+                q, k, v = b.q[rows, cols], b.k[rows, cols], b.v[rows, cols]
+                length = self.lengths[0, s]
+                out = None
+                for a in range(2):
+                    st = mm_nt(k * masks[a], q)
+                    st = jnp.where(key < length, st, -1e9)
+                    e = jnp.exp(st - jnp.max(st, 0, keepdims=True))
+                    att = e * (1.0 / jnp.sum(e, 0, keepdims=True))
+                    b.p[s * 12 + p * 2 + a] = att
+                    o = mm_tn(v * masks[a], att.astype(BF))
+                    out = o if out is None else out + o
+                b.mixed[rows, cols] = out.T.astype(BF)
             return 0
 
-        lax.fori_loop(0, 12, body, 0)
+        lax.fori_loop(0, 6, body, 0)
 
     def attn_out(self):
         b = self.b
@@ -230,14 +231,14 @@
             b.n1[:, cols] = self.x[:, cols].astype(F32) + acc
 
         def body(r, _):
-            rows = pl.ds(pl.multiple_of(r * 32, 32), 32)
+            rows = pl.ds(pl.multiple_of(r * ROWS, ROWS), ROWS)
             n, scale = normalise(b.n1[rows, :])
             b.n1[rows, :] = n
-            b.r1[rows, :] = jnp.broadcast_to(scale, (32, LANES))
+            b.r1[rows, :] = jnp.broadcast_to(scale, (ROWS, LANES))
             b.nl[rows, :] = (n * self.v(VAG) + self.v(VAS)).astype(BF)
             return 0
 
-        lax.fori_loop(0, TOKENS // 32, body, 0)
+        lax.fori_loop(0, TOKENS // ROWS, body, 0)
 
     def feed(self):
         b = self.b
@@ -268,7 +269,7 @@
             b.second[:, cols] = acc
 
         def body(r, sums):
-            rows = pl.ds(pl.multiple_of(r * 32, 32), 32)
+            rows = pl.ds(pl.multiple_of(r * ROWS, ROWS), ROWS)
             n, scale = normalise(b.second[rows, :])
             c = self.og[rows, :].astype(F32)
             self.enc[rows, :] = (n * self.v(VFG) + self.v(VFS)).astype(BF)
@@ -279,14 +280,15 @@
             return sums[0] + column_total(c * n), sums[1] + column_total(c), sums[2] + column_total(low)
 
         zero = jnp.zeros((1, WIDTH), F32)
-        sums = lax.fori_loop(0, TOKENS // 32, body, (zero, zero, zero))
+        sums = lax.fori_loop(0, TOKENS // ROWS, body, (zero, zero, zero))
         self.gvec[VFG:VFG + 1, :], self.gvec[VFS:VFS + 1, :], self.gvec[VD:VD + 1, :] = sums
 
     def down_grads(self, j):
         b = self.b
+        left = b.act[j].T
         for n in range(3):
             cols = slice(n * 256, n * 256 + 256)
-            self.grads[2][j, :, cols] = mm_tn(b.act[j], b.nl[:, cols]).astype(BF)
+            self.grads[2][j, :, cols] = mm(left, b.nl[:, cols]).astype(BF)
 
     def feed_back(self, j):
         b = self.b
@@ -320,7 +322,7 @@
         b = self.b
 
         def body(r, sums):
-            rows = pl.ds(pl.multiple_of(r * 32, 32), 32)
+            rows = pl.ds(pl.multiple_of(r * ROWS, ROWS), ROWS)
             c = b.second[rows, :]
             n = b.n1[rows, :]
             g = norm_back(c, self.v(VAG), n, b.r1[rows, 0:1])
@@ -330,14 +332,15 @@
             return sums[0] + column_total(c * n), sums[1] + column_total(c), sums[2] + column_total(low)
 
         zero = jnp.zeros((1, WIDTH), F32)
-        sums = lax.fori_loop(0, TOKENS // 32, body, (zero, zero, zero))
+        sums = lax.fori_loop(0, TOKENS // ROWS, body, (zero, zero, zero))
         self.gvec[VAG:VAG + 1, :], self.gvec[VAS:VAS + 1, :], self.gvec[VO:VO + 1, :] = sums
 
     def out_grads(self):
         b = self.b
+        left = b.mixed[...].T
         for n in range(3):
             cols = slice(n * 256, n * 256 + 256)
-            self.grads[0][3, :, cols] = mm_tn(b.mixed[...], b.nl[:, cols]).astype(BF)
+            self.grads[0][3, :, cols] = mm(left, b.nl[:, cols]).astype(BF)
 
     def out_back(self):
         b = self.b
@@ -350,8 +353,8 @@
         masks = half_masks()
         cols = slice(p * LANES, p * LANES + LANES)
 
-        def body(s, _):
-            rows = pl.ds(pl.multiple_of(s * SEQ, SEQ), SEQ)
+        for s in range(2):
+            rows = slice(s * SEQ, s * SEQ + SEQ)
             q, k, v, do = b.q[rows, cols], b.k[rows, cols], b.v[rows, cols], b.mixed[rows, cols]
             dq = dk = dv = 0.0
             for a in range(2):
@@ -365,9 +368,6 @@
             b.gpre[0, rows, cols] = (dq.T * 0.125).astype(BF)
             b.gpre[1, rows, cols] = dk.astype(BF)
             b.gpre[2, rows, cols] = dv.astype(BF)
-            return 0
-
-        lax.fori_loop(0, 2, body, 0)
         both = mm(b.xt[...], jnp.concatenate([b.gpre[0, :, cols], b.gpre[1, :, cols]], 1))
         self.grads[0][0, :, cols] = both[:, :LANES].astype(BF)
         self.grads[0][1, :, cols] = both[:, LANES:].astype(BF)
@@ -393,22 +393,25 @@
 
 
 START = {16: 0, 8: 16, 4: 24}
-VLINKS = (CORE, Y1, Y3, X1, Z1, Z3)
+WHOLE = tuple((part, 0, UNIT, ORDERS[part]) for part in range(PARTS))
+CUT = WHOLE[:4] + tuple((4 + i // 3, 16 * (i % 3), 16, ORDERS[i]) for i in range(6))
+CHAINS = (CUT, WHOLE, WHOLE)
 EVERY = ((0, 2), (0, 4), (0, 2), (0, 2))
 SCRATCH = dict(
     wa=(SHAPES[0], BF), wb=(SHAPES[1], BF), wc=(SHAPES[2], BF), ga=(SHAPES[0], BF),
     rdb=((2, 1, 4, 2, 2, UNIT, WIDTH), BF), rdc=((4, 2, 2, 2, 1, UNIT, WIDTH), BF),
-    rk=((3, 31, UNIT, WIDTH), BF), rx=((3, UNIT, WIDTH), BF), tall=((2, UNIT, WIDTH), F32),
-    stage=((2, 4, 16, WIDTH), F32), landed=((2, 4, 16, WIDTH), F32),
-    vt=((64, 2, LANES), F32), gv=((64, 2, LANES), F32), rv=((64, 2, LANES), F32),
+    rk=((3, 31, UNIT, WIDTH), BF), rx=((UNIT, WIDTH), BF), tall=((UNIT, WIDTH), F32),
+    stage=((2, 4, 16, WIDTH), BF), final=((2, 2, 4, 16, WIDTH), BF),
+    vt=((4, 2, 8, 2, LANES), F32), gv=((4, 2, 8, 2, LANES), F32),
+    rv2=((3, 2, 8, 2, LANES), F32), rv1=((3, 4, 2, LANES), F32), rv0=((7, 2, LANES), F32),
     vec=((16, WIDTH), F32), gvec=((16, WIDTH), F32),
     x=((TOKENS, WIDTH), BF), qkv_in=((12, 3 * WIDTH), BF), out_in=((12, WIDTH), BF), up_in=((12, 4 * WIDTH), BF),
 )
 SEMS = dict(
     loads=(8,), mate_send=(2, 3), mate_recv=(2, 3), send=(3, PARTS, 7), recv=(3, PARTS, 7),
-    sib_send=(3, PARTS), sib_recv=(3, PARTS), vsend=(6,), vrecv=(6,),
-    gsib_send=(3, PARTS), gsib_recv=(3, PARTS), gsend=(3, PARTS, 6), grecv=(3, PARTS, 6),
-    rep_send=(3,), rep_recv=(3,), gmate_send=(2, 3), gmate_recv=(2, 3), gvsend=(7,), gvrecv=(7,),
+    sib_send=(3, PARTS), sib_recv=(3, PARTS), vsend=(9,), vrecv=(9,),
+    gsib_send=(3, PARTS), gsib_recv=(3, PARTS), gsend=(3, 10, 6), grecv=(3, 10, 6),
+    rep_send=(1,), rep_recv=(1,), gmate_send=(2, 7), gmate_recv=(2, 7), gvsend=(13,), gvrecv=(13,),
 )
 
 
@@ -447,7 +450,6 @@
     me = member_of(here)
     sibling = hop(here, CORE)
     twin = hop(here, X2)
-    dp = device_of(here)[0]
     weights = (r.wa, r.wb, r.wc)
     grads = (r.ga, r.wb, r.wc)
     rds = (r.act.at[pl.ds(0, 3)].reshape((2, 1, 4, 2, 2, UNIT, WIDTH)), r.rdb, r.rdc)
@@ -461,21 +463,16 @@
 
     def mate_copy(which, k):
         mate = mates(here)[k]
-        return remote(r.stage.at[which, member_of(mate)], r.landed.at[which, me],
+        return remote(r.stage.at[which, member_of(mate)], r.final.at[which, 0, me],
                       r.mate_send.at[which, k], r.mate_recv.at[which, k], mate)
 
     def assemble(which):
         for k in range(3):
             mate_copy(which, k).wait()
+        r.final[which, 0, me] = r.stage[which, me]
         for i in range(4):
-            @pl.when(me == i)
-            def _():
-                r.tall[which, 12 * i:12 * i + 12, :] = r.stage[which, i, 0:12, :]
-
-            @pl.when(me != i)
-            def _():
-                r.tall[which, 12 * i:12 * i + 12, :] = r.landed[which, i, 0:12, :]
-        weights[which][own_at(which)] = r.tall[which].astype(BF)
+            r.tall[12 * i:12 * i + 12, :] = r.final[which, 0, i, 0:12, :].astype(F32)
+        weights[which][own_at(which)] = r.tall[...].astype(BF)
 
     def push(phase, part, found, slot, there):
         w = weights[phase]
@@ -527,19 +524,33 @@
             for slot, n in enumerate((1, 1, 1, 4, 8, 8, 8)):
                 wait_units(weights[phase], phase, n, part, r.send.at[phase, part, slot])
 
-    def vec_copy(k):
-        n = 1 << k
-        view = r.vt.at[pl.ds(dp // n * n, n)]
-        return remote(view, view, r.vsend.at[k], r.vrecv.at[k], hop(here, VLINKS[k]))
-
-    def vec_next(k):
-        vec_copy(k - 1).wait()
-        if k < 6:
-            vec_copy(k).start()
+    def vec_tile(place):
+        return (place.z, place.x % 2, place.y * 2 + place.core)
+
+    def vec_pair(place):
+        return (place.z, place.x % 2, pl.ds(place.y // 2 * 4, 4))
+
+    def vec_ring(place):
+        return (pl.ds(place.z // 2 * 2, 2), place.x % 2)
+
+    def vec_peers(k):
+        return (mates(here), trio(here, (Y3, Z1)), trio(here, (Z3, X1)))[k]
+
+    def vec_copies(k):
+        view = r.vt.at[(vec_tile, vec_pair, vec_ring)[k](here)]
+        return [remote(view, view, r.vsend.at[3 * k + i], r.vrecv.at[3 * k + i], there) for i, there in enumerate(vec_peers(k))]
+
+    def vec_start(k):
+        for copy in vec_copies(k):
+            copy.start()
+
+    def vec_wait(k):
+        for copy in vec_copies(k):
+            copy.wait()
 
     def expand():
-        first = r.vt[:, 0, :].astype(BF)
-        second = r.vt[:, 1, :].astype(BF)
+        first = r.vt[:, :, :, 0, :].reshape(64, LANES).astype(BF)
+        second = r.vt[:, :, :, 1, :].reshape(64, LANES).astype(BF)
         mask = owner_masks(None)
         for row in range(8):
             t = mm_nt(first, lane_picks(row))
@@ -573,49 +584,60 @@
                 at = (k, i // 2, i % 2, slice(None), pl.ds(here.core, 1))
                 g[at] = g[at] + rd[k, i // 2, i % 2]
 
-    def hop_start(phase, part, step):
-        order = ORDERS[part]
-        cols = pl.ds(part * LANES, LANES)
+    def unit_slices(phase, box, chain):
+        part, row, rows, _ = chain
+        return slices(phase, here.core, box, part)[:5] + (slice(row, row + rows), slice(part * LANES, part * LANES + LANES))
+
+    def hop_start(phase, c, step):
+        chain = CHAINS[phase][c]
+        order = chain[3]
+
+        def send(box, at, slot, there):
+            n = box_count(box)
+            src = grads[phase].at[slices(phase, here.core, box, chain[0])[:5]]
+            dst = r.rk.at[phase, pl.ds(at, n)].reshape(src.shape)
+            at5 = (slice(None),) * 5 + (pl.ds(chain[1], chain[2]), pl.ds(chain[0] * LANES, LANES))
+            remote(src.at[at5], dst.at[at5], r.gsend.at[phase, c, slot], r.grecv.at[phase, c, slot], there).start()
+            return at + n
+
         if step == 1:
             for slot, there in enumerate(trio(here, order)):
-                src = grads[phase].at[slices(phase, here.core, boxes(there, ())[0], part)]
-                dst = r.rk.at[phase, pl.ds(28 + slot, 1)].reshape(src.shape[:5] + (UNIT, WIDTH)).at[:, :, :, :, :, :, cols]
-                remote(src, dst, r.gsend.at[phase, part, slot], r.grecv.at[phase, part, slot], there).start()
+                send(boxes(there, ())[0], 28 + slot, slot, there)
             return
         there = hop(here, order[step])
         at = START[1 << step]
         for box in boxes(there, order[:step]):
-            n = box_count(box)
-            src = grads[phase].at[slices(phase, here.core, box, part)]
-            dst = r.rk.at[phase, pl.ds(at, n)].reshape(src.shape[:5] + (UNIT, WIDTH)).at[:, :, :, :, :, :, cols]
-            remote(src, dst, r.gsend.at[phase, part, step + 1], r.grecv.at[phase, part, step + 1], there).start()
-            at += n
-
-    def hop_add(phase, part, step):
+            at = send(box, at, step + 1, there)
+
+    def landing(phase, c, at, n):
+        part, row, rows, _ = CHAINS[phase][c]
+        return r.rk.at[phase, pl.ds(at, n), pl.ds(row, rows), pl.ds(part * LANES, LANES)]
+
+    def hop_add(phase, c, step):
         g = grads[phase]
-        cols = slice(part * LANES, part * LANES + LANES)
+        chain = CHAINS[phase][c]
         if step == 1:
-            where = slices(phase, here.core, boxes(here, ())[0], part)
+            where = unit_slices(phase, boxes(here, ())[0], chain)
             total = g[where].astype(F32)
             for slot in range(3):
-                view = r.rk.at[phase, 28 + slot, :, cols]
-                pltpu.make_async_copy(view, view, r.grecv.at[phase, part, slot]).wait()
+                view = landing(phase, c, 28 + slot, 1)
+                pltpu.make_async_copy(view, view, r.grecv.at[phase, c, slot]).wait()
                 total = total + view[...].astype(F32).reshape(total.shape)
             g[where] = total.astype(BF)
             return
         n = 1 << step
         at = START[n]
-        view = r.rk.at[phase, pl.ds(at, n), :, cols]
-        pltpu.make_async_copy(view, view, r.grecv.at[phase, part, step + 1]).wait()
-        for box in boxes(here, ORDERS[part][:step]):
+        view = landing(phase, c, at, n)
+        pltpu.make_async_copy(view, view, r.grecv.at[phase, c, step + 1]).wait()
+        for box in boxes(here, chain[3][:step]):
             m = box_count(box)
-            where = slices(phase, here.core, box, part)
+            where = unit_slices(phase, box, chain)
             old = g[where]
-            g[where] = old + r.rk[phase, at:at + m, :, cols].reshape(old.shape)
+            g[where] = old + landing(phase, c, at, m)[...].reshape(old.shape)
             at += m
 
-    def rep_copy(phase):
-        return remote(grads[phase].at[own_at(phase)], r.rx.at[phase], r.rep_send.at[phase], r.rep_recv.at[phase], twin)
+    def rep_copy():
+        return remote(grads[2].at[own_at(2)], r.rx, r.rep_send.at[0], r.rep_recv.at[0], twin)
 
     def reduce_first(phase):
         for k in range(2 if phase == 1 else 4):
@@ -623,59 +645,57 @@
         for part in range(PARTS):
             hop_start(phase, part, 4)
 
-    def move(phase, part, step):
-        hop_add(phase, part, step)
+    def move(phase, c, step):
+        hop_add(phase, c, step)
         if step > 1:
-            hop_start(phase, part, step - 1)
+            hop_start(phase, c, step - 1)
 
     def reduce(phase, step):
         for part in range(PARTS):
             move(phase, part, step)
-        if step == 1:
-            rep_copy(phase).start()
 
     def first_part(part):
         sib_add(0, part)
-        hop_start(0, part, 4)
+        for c, chain in enumerate(CUT):
+            if chain[0] == part:
+                hop_start(0, c, 4)
+
+    def move_part(part, step):
+        for c, chain in enumerate(CUT):
+            if chain[0] == part:
+                move(0, c, step)
 
     def gmate_copy(which, k):
-        mate = mates(here)[k]
-        return remote(r.stage.at[which, member_of(mate)], r.landed.at[which, me],
-                      r.gmate_send.at[which, k], r.gmate_recv.at[which, k], mate)
-
-    def reduce_last(phase):
-        rep_copy(phase).wait()
-        total = grads[phase][own_at(phase)].astype(F32) + r.rx[phase].astype(F32)
-        if phase == 2:
-            odown[...] = total
-            return
-        r.tall[phase] = total
+        others = mates(here)
+        there = (others + [twin] + [hop(mate, X2) for mate in others])[k]
+        return remote(r.stage.at[which, member_of(there)], r.final.at[which, k // 3 if k < 6 else 1, me],
+                      r.gmate_send.at[which, k], r.gmate_recv.at[which, k], there)
+
+    def hand_over(phase):
+        r.tall[...] = grads[phase][own_at(phase)].astype(F32)
         for i in range(4):
-            r.stage[phase, i, 0:12, :] = r.tall[phase, 12 * i:12 * i + 12, :]
-        for k in range(3):
+            r.stage[phase, i, 0:12, :] = r.tall[12 * i:12 * i + 12, :].astype(BF)
+        for k in range(7):
             gmate_copy(phase, k).start()
 
     def deliver(phase):
-        for k in range(3):
+        for k in range(7):
             gmate_copy(phase, k).wait()
+        r.final[phase, 0, me] = r.stage[phase, me]
         for i in range(4):
             cols = pl.ds(i * WIDTH, WIDTH)
             dst = oup.at[:, cols] if phase else (oqkv.at[:, cols] if i < 3 else oout)
-
-            @pl.when(me == i)
-            def _():
-                dst[...] = r.stage[phase, i, 0:12, :]
-
-            @pl.when(me != i)
-            def _():
-                dst[...] = r.landed[phase, i, 0:12, :]
+            dst[...] = r.final[phase, 0, i, 0:12, :].astype(F32) + r.final[phase, 1, i, 0:12, :].astype(F32)
+
+    def deliver_down():
+        rep_copy().wait()
+        odown[...] = grads[2][own_at(2)].astype(F32) + r.rx[...].astype(F32)
 
     def reduce_sent(phase):
-        for part in range(PARTS):
-            cols = pl.ds(part * LANES, LANES)
+        for c in range(len(CHAINS[phase])):
             for slot, n in enumerate((1, 1, 1, 4, 8, 16)):
-                view = r.rk.at[phase, pl.ds(0, n), :, cols]
-                pltpu.make_async_copy(view, view, r.gsend.at[phase, part, slot]).wait()
+                view = landing(phase, c, 0, n)
+                pltpu.make_async_copy(view, view, r.gsend.at[phase, c, slot]).wait()
 
     def pack_rows(rows):
         mask = owner_masks(None)
@@ -685,7 +705,7 @@
             picks = lane_picks(row)
             for piece in split3(value):
                 first = first + mm(piece, picks)
-        return first
+        return first.reshape(4, 2, 8, LANES)
 
     def pack():
         second = jnp.zeros((64, LANES), F32)
@@ -694,73 +714,79 @@
             value = jnp.where(owner_masks(j), jnp.broadcast_to(r.gvec[8 + j:9 + j, :], (64, WIDTH)), 0.0)
             for piece in split3(value):
                 second = second + mm(piece, picks)
-        r.gv[:, 0, :] = pack_rows((VO, VAG, VAS, VD, VFG, VFS))
-        r.gv[:, 1, :] = second
-
-    def gvec_copy(k):
-        if k < 6:
-            n = 32 >> k
-            there = hop(here, VLINKS[5 - k])
-            to = device_of(there)[0]
-            src, dst = r.gv.at[pl.ds(to // n * n, n)], r.rv.at[pl.ds(64 - 2 * n, n)]
+        r.gv[:, :, :, 0, :] = pack_rows((VO, VAG, VAS, VD, VFG, VFS))
+        r.gv[:, :, :, 1, :] = second.reshape(4, 2, 8, LANES)
+
+    def gvec_copies(k):
+        if k == 0:
+            peers = mates(here) + [twin] + [hop(mate, X2) for mate in mates(here)]
         else:
-            there, src, dst = twin, r.gv.at[pl.ds(dp, 1)], r.rv.at[pl.ds(63, 1)]
-        return remote(src, dst, r.gvsend.at[k], r.gvrecv.at[k], there)
-
-    def gvec_next(k):
-        gvec_copy(k).wait()
-        n = 32 >> k if k < 6 else 1
-        lo = 64 - 2 * n if k < 6 else 63
-        mine = pl.ds(dp // n * n, n)
-        r.gv[mine] = r.gv[mine] + r.rv[lo:lo + n]
-        if k < 6:
-            gvec_copy(k + 1).start()
+            peers = vec_peers(k)
+        part, landing_ref = ((vec_tile, r.rv0), (vec_pair, r.rv1), (vec_ring, r.rv2))[k]
+        base = (6, 3, 0)[k]
+        return [remote(r.gv.at[part(there)], landing_ref.at[i], r.gvsend.at[base + i], r.gvrecv.at[base + i], there)
+                for i, there in enumerate(peers)]
+
+    def gvec_start(k):
+        for copy in gvec_copies(k):
+            copy.start()
+
+    def gvec_add(k):
+        part, landing_ref = ((vec_tile, r.rv0), (vec_pair, r.rv1), (vec_ring, r.rv2))[k]
+        at = part(here)
+        total = r.gv[at]
+        for i, copy in enumerate(gvec_copies(k)):
+            copy.wait()
+            total = total + landing_ref[i].reshape(total.shape)
+        r.gv[at] = total
 
     near = [hop(here, link) for link in (Y1, Y3, Z1, Z3, X1, X3, CORE, X2, Y2, Z2)]
     near += [mates(here)[2], hop(hop(here, Y3), Z1), hop(hop(here, Y1), Z3)]
-    barrier = pltpu.get_barrier_semaphore()
-    for place in near:
-        pl.semaphore_signal(barrier, inc=1, device_id=device_of(place), device_id_type=MESH)
+    near += [hop(mate, X2) for mate in mates(here)] + [hop(hop(here, Z3), X1)]
     loads = [pltpu.make_async_copy(src, dst, r.loads.at[i]) for i, (src, dst) in enumerate((
         (qkv_in, r.qkv_in), (out_in, r.out_in), (up_in, r.up_in), (down_in, weights[2].at[own_at(2)]), (x_in, r.x)))]
     for load in loads:
         load.start()
+    barrier = pltpu.get_barrier_semaphore()
+    for place in near:
+        pl.semaphore_signal(barrier, inc=1, device_id=device_of(place), device_id_type=MESH)
     og_load = pltpu.make_async_copy(og_in, r.x, r.loads.at[5])
-    r.vt[dp] = jnp.zeros((2, LANES), F32)
+    own = vec_tile(here)
+    r.vt[own] = jnp.zeros((2, LANES), F32)
     for i in range(8):
-        r.vt[dp, 0:1, 12 * i:12 * i + 12] = vecs_in[i][...].astype(F32)
-    r.vt[dp, 1:2, 0:48] = vecs_in[8][...].astype(F32)
+        r.vt[own + (slice(0, 1), slice(12 * i, 12 * i + 12))] = vecs_in[i][...].astype(F32)
+    r.vt[own + (slice(1, 2), slice(0, 48))] = vecs_in[8][...].astype(F32)
     for load in loads[:4]:
         load.wait()
     for i in range(4):
-        r.stage[0, i, 0:12, :] = (r.qkv_in[:, i * WIDTH:(i + 1) * WIDTH] if i < 3 else r.out_in[...]).astype(F32)
-        r.stage[1, i, 0:12, :] = r.up_in[:, i * WIDTH:(i + 1) * WIDTH].astype(F32)
+        r.stage[0, i, 0:12, :] = r.qkv_in[:, i * WIDTH:(i + 1) * WIDTH] if i < 3 else r.out_in[...]
+        r.stage[1, i, 0:12, :] = r.up_in[:, i * WIDTH:(i + 1) * WIDTH]
     pl.semaphore_wait(barrier, len(near))
-    for which in range(2):
-        for k in range(3):
-            mate_copy(which, k).start()
-    vec_copy(0).start()
+    for k in range(3):
+        mate_copy(0, k).start()
+    vec_start(0)
+    for k in range(3):
+        mate_copy(1, k).start()
     gather_first(2)
     loads[4].wait()
     b.xt[...] = r.x[...].T
     assemble(0)
+    vec_wait(0)
+    vec_start(1)
     gather_first(0)
     assemble(1)
-    vec_next(1)
     gather_first(1)
+    vec_wait(1)
+    vec_start(2)
     gather(0, 2)
-    vec_next(2)
     gather(2, 2)
+    gather(1, 2)
     gather(0, 3)
-    vec_next(3)
-    gather(1, 2)
+    vec_wait(2)
+    expand()
     gather(0, 4)
-    vec_next(4)
     gather(1, 3)
-    vec_next(5)
     gather(2, 3)
-    vec_next(6)
-    expand()
     gather_last(0, 0)
     gather_last(0, 1)
     gathered(0)
@@ -833,58 +859,58 @@
     sib_copy(0, 4).start()
     reduce(2, 2)
     first_part(3)
+    move_part(0, 4)
     layer.attend_back(5)
     sib_copy(0, 5).start()
     first_part(4)
-    r.gv[:, 0, :] = r.gv[:, 0, :] + pack_rows((VQ, VV))
-    gvec_copy(0).start()
-    reduce(1, 2)
+    r.gv[:, :, :, 0, :] = r.gv[:, :, :, 0, :] + pack_rows((VQ, VV))
+    gvec_start(2)
+    move_part(1, 4)
     layer.input_grad(0)
     first_part(5)
-    move(0, 0, 4)
+    reduce(1, 2)
     layer.input_grad(1)
-    move(0, 1, 4)
-    gvec_next(0)
+    move_part(2, 4)
+    move_part(0, 3)
     layer.input_grad(2)
     sgrad_store = pltpu.make_async_copy(b.second, sgrad_out, r.loads.at[7])
     sgrad_store.start()
     reduce(2, 1)
-    move(0, 2, 4)
-    move(0, 0, 3)
-    gvec_next(1)
-    move(0, 3, 4)
-    move(0, 1, 3)
+    rep_copy().start()
+    move_part(4, 4)
+    gvec_add(2)
+    gvec_start(1)
+    move_part(3, 4)
+    move_part(5, 4)
+    move_part(1, 3)
+    move_part(0, 2)
+    move_part(2, 3)
+    move_part(4, 3)
     reduce(1, 1)
-    gvec_next(2)
-    move(0, 4, 4)
-    move(0, 2, 3)
-    move(0, 0, 2)
-    reduce_last(2)
-    move(0, 5, 4)
-    move(0, 3, 3)
-    move(0, 1, 2)
-    gvec_next(3)
-    move(0, 4, 3)
-    move(0, 2, 2)
-    reduce_last(1)
-    move(0, 5, 3)
-    move(0, 3, 2)
-    move(0, 4, 2)
-    gvec_next(4)
-    move(0, 5, 2)
+    hand_over(1)
+    move_part(5, 3)
+    move_part(3, 3)
+    move_part(1, 2)
+    move_part(2, 2)
+    move_part(4, 2)
+    gvec_add(1)
+    gvec_start(0)
+    move_part(3, 2)
+    move_part(5, 2)
+    deliver_down()
+    for part in range(PARTS):
+        move_part(part, 1)
+    hand_over(0)
     deliver(1)
-    gvec_next(5)
-    reduce(0, 1)
-    gvec_next(6)
-    ovec[...] = r.gv[dp]
-    reduce_last(0)
+    gvec_add(0)
+    ovec[...] = r.gv[vec_tile(here)]
     for phase in range(1, 3):
         reduce_sent(phase)
     gather_sent(0)
-    deliver(0)
     reduce_sent(0)
     enc_store.wait()
     sgrad_store.wait()
+    deliver(0)
 
 
 def run_layer(lengths, vecs, qkv, out, up, down, x, og):

time: 145 us -> 135 us (0.931)
  Pallas kernels: 144 us -> 134 us
    pallas_call x1, Pallas kernels: 140 us -> 129 us  [run_layer(): pl.pallas_call(mega_kernel, out_shape=[jax.ShapeDtypeStruct((TOKENS, WIDT...]
where the time goes in v4:
time: 135 us; the launch traced here: 134 us
  Pallas kernels  134 us (99%)
    pallas_call x1, Pallas kernels, run_layer(): pl.pallas_call(mega_kernel, out_shape=[jax.ShapeDtypeStruct((TOKENS, WIDT...  129 us
    pallas_call x1, Pallas kernels, finish(): pl.pallas_call(finish_kernel, out_shape=[jax.ShapeDtypeStruct(a.shape, a....  4.29 us

profile of v4, /device:TPU:1, one launch (start us, length us, event | category | flops | bytes accessed | tf_op | source)
XLA Modules:
  0.0 134.4 jit_solution(6336624177299071766)
XLA Ops:
  0.7 129.3 %shard_map.271 = (bf16[512,768]{1,0:T(8,128)(2,1)}, f32[512,768]{1,0:T(8,128)}, f32[12,2304]{1,0:T(8,128)}, f32[12,768]{1,0:T(8,128)}, f32[12,3072]{1,0:T(8,128)}, /*index=5*/f32[48,768]{1,0:T(8,128)}, f32[2,128]{1,0:T(2,128)}) custom-call(s32[1,2]{1,0:T(1,128)} %bitcast.29, bf16[1,12]{1,0:T(2,128)(2,1)} %bitcast.30, bf16[1,12]{1,0:T(2,128)(2,1)} %bitcast.31, ...), custom_call_target="tpu_custom_call" | custom-call | tf_op jit(solution)/shard_map/pallas_call | solution.py:919
  129.9 4.3 %shard_map.272 = (bf16[512,768]{1,0:T(8,128)(2,1)}, f32[512,768]{1,0:T(8,128)}, f32[12,2304]{1,0:T(8,128)}, f32[12,768]{1,0:T(8,128)}, f32[12,3072]{1,0:T(8,128)...) custom-call(bf16[512,768]{1,0:T(8,128)(2,1)} %get-tuple-element.37.r, ...), custom_call_target="tpu_custom_call" | custom-call | tf_op jit(solution)/shard_map/pallas_call | solution.py:953

commit v5 on v4

--- a/solution.py
+++ b/solution.py
@@ -173,6 +173,12 @@
     return low, (1.0 - low.astype(F32)).astype(BF)
 
 
+def row_masks():
+    row = lax.broadcasted_iota(jnp.int32, (LANES, SEQ), 0)
+    low = (row < 64).astype(F32).astype(BF)
+    return low, (1.0 - low.astype(F32)).astype(BF)
+
+
 def column_total(ref_rows):
     return jnp.sum(ref_rows.astype(F32), 0, keepdims=True)
 
@@ -200,25 +206,26 @@
 
     def attend(self):
         b = self.b
-        masks = half_masks()
+        masks, tall = half_masks(), row_masks()
         key = lax.broadcasted_iota(jnp.int32, (SEQ, SEQ), 0)
 
         def body(p, _):
             cols = pl.ds(pl.multiple_of(p * LANES, LANES), LANES)
+            rows = [slice(s * SEQ, s * SEQ + SEQ) for s in range(2)]
+            scores = [[mm_nt(b.k[rows[s], cols] * masks[a], b.q[rows[s], cols]) for a in range(2)] for s in range(2)]
+            low = [[None, None], [None, None]]
             for s in range(2):
-                rows = slice(s * SEQ, s * SEQ + SEQ)
-                q, k, v = b.q[rows, cols], b.k[rows, cols], b.v[rows, cols]
                 length = self.lengths[0, s]
-                out = None
                 for a in range(2):
-                    st = mm_nt(k * masks[a], q)
-                    st = jnp.where(key < length, st, -1e9)
+                    st = jnp.where(key < length, scores[s][a], -1e9)
                     e = jnp.exp(st - jnp.max(st, 0, keepdims=True))
                     att = e * (1.0 / jnp.sum(e, 0, keepdims=True))
                     b.p[s * 12 + p * 2 + a] = att
-                    o = mm_tn(v * masks[a], att.astype(BF))
-                    out = o if out is None else out + o
-                b.mixed[rows, cols] = out.T.astype(BF)
+                    low[s][a] = att.astype(BF)
+            for s in range(2):
+                vt = b.v[rows[s], cols].T
+                out = mm(jnp.concatenate([vt * tall[0], vt * tall[1]], 1), jnp.concatenate(low[s], 0))
+                b.mixed[rows[s], cols] = out.T.astype(BF)
             return 0
 
         lax.fori_loop(0, 6, body, 0)
@@ -350,24 +357,26 @@
 
     def attend_back(self, p):
         b = self.b
-        masks = half_masks()
+        masks, tall = half_masks(), row_masks()
         cols = slice(p * LANES, p * LANES + LANES)
-
+        rows = [slice(s * SEQ, s * SEQ + SEQ) for s in range(2)]
+        dos = [[b.mixed[rows[s], cols] * masks[a] for a in range(2)] for s in range(2)]
+        dps = [[mm_nt(b.v[rows[s], cols], dos[s][a]) for a in range(2)] for s in range(2)]
+        low = [[None, None], [None, None]]
         for s in range(2):
-            rows = slice(s * SEQ, s * SEQ + SEQ)
-            q, k, v, do = b.q[rows, cols], b.k[rows, cols], b.v[rows, cols], b.mixed[rows, cols]
-            dq = dk = dv = 0.0
+            atts = []
             for a in range(2):
                 att = b.p[s * 12 + p * 2 + a]
-                do_a = do * masks[a]
-                dv = dv + mm(att.astype(BF), do_a)
-                dp = mm_nt(v, do_a)
-                ds = (att * (dp - jnp.sum(att * dp, 0, keepdims=True))).astype(BF)
-                dk = dk + mm(ds, q * masks[a])
-                dq = dq + mm_tn(k * masks[a], ds)
-            b.gpre[0, rows, cols] = (dq.T * 0.125).astype(BF)
-            b.gpre[1, rows, cols] = dk.astype(BF)
-            b.gpre[2, rows, cols] = dv.astype(BF)
+                atts.append(att.astype(BF))
+                dp = dps[s][a]
+                low[s][a] = (att * (dp - jnp.sum(att * dp, 0, keepdims=True))).astype(BF)
+            b.gpre[2, rows[s], cols] = mm(jnp.concatenate(atts, 1), jnp.concatenate(dos[s], 0)).astype(BF)
+        for s in range(2):
+            q, kt = b.q[rows[s], cols], b.k[rows[s], cols].T
+            dk = mm(jnp.concatenate(low[s], 1), jnp.concatenate([q * masks[0], q * masks[1]], 0))
+            b.gpre[1, rows[s], cols] = dk.astype(BF)
+            dq = mm(jnp.concatenate([kt * tall[0], kt * tall[1]], 1), jnp.concatenate(low[s], 0))
+            b.gpre[0, rows[s], cols] = (dq.T * 0.125).astype(BF)
         both = mm(b.xt[...], jnp.concatenate([b.gpre[0, :, cols], b.gpre[1, :, cols]], 1))
         self.grads[0][0, :, cols] = both[:, :LANES].astype(BF)
         self.grads[0][1, :, cols] = both[:, LANES:].astype(BF)
@@ -394,9 +403,11 @@
 
 START = {16: 0, 8: 16, 4: 24}
 WHOLE = tuple((part, 0, UNIT, ORDERS[part]) for part in range(PARTS))
-CUT = WHOLE[:4] + tuple((4 + i // 3, 16 * (i % 3), 16, ORDERS[i]) for i in range(6))
+CUT = tuple((i // 3, 16 * (i % 3), 16, ORDERS[i % 6]) for i in range(3 * PARTS))
 CHAINS = (CUT, WHOLE, WHOLE)
+FIRST = (0, 18, 24)
 EVERY = ((0, 2), (0, 4), (0, 2), (0, 2))
+VECTORS = "v0 v1 v2 v3".split() + "v4 v5 v6 v7".split()
 SCRATCH = dict(
     wa=(SHAPES[0], BF), wb=(SHAPES[1], BF), wc=(SHAPES[2], BF), ga=(SHAPES[0], BF),
     rdb=((2, 1, 4, 2, 2, UNIT, WIDTH), BF), rdc=((4, 2, 2, 2, 1, UNIT, WIDTH), BF),
@@ -406,12 +417,13 @@
     rv2=((3, 2, 8, 2, LANES), F32), rv1=((3, 4, 2, LANES), F32), rv0=((7, 2, LANES), F32),
     vec=((16, WIDTH), F32), gvec=((16, WIDTH), F32),
     x=((TOKENS, WIDTH), BF), qkv_in=((12, 3 * WIDTH), BF), out_in=((12, WIDTH), BF), up_in=((12, 4 * WIDTH), BF),
+    **{name: ((1, 12), BF) for name in VECTORS}, v8=((1, 48), BF),
 )
 SEMS = dict(
-    loads=(8,), mate_send=(2, 3), mate_recv=(2, 3), send=(3, PARTS, 7), recv=(3, PARTS, 7),
+    loads=(17,), mate_send=(2, 3), mate_recv=(2, 3), send=(3, PARTS, 7), recv=(3, PARTS, 7),
     sib_send=(3, PARTS), sib_recv=(3, PARTS), vsend=(9,), vrecv=(9,),
-    gsib_send=(3, PARTS), gsib_recv=(3, PARTS), gsend=(3, 10, 6), grecv=(3, 10, 6),
-    rep_send=(1,), rep_recv=(1,), gmate_send=(2, 7), gmate_recv=(2, 7), gvsend=(13,), gvrecv=(13,),
+    gsib_send=(3, PARTS), gsib_recv=(3, PARTS), gsend=(30, 7), grecv=(30, 7),
+    rep_send=(1,), rep_recv=(1,), gmate_send=(3, 7), gmate_recv=(3, 7), gvsend=(13,), gvrecv=(13,),
 )
 
 
@@ -549,12 +561,13 @@
             copy.wait()
 
     def expand():
-        first = r.vt[:, :, :, 0, :].reshape(64, LANES).astype(BF)
+        first = r.vt[:, :, :, 0, :].reshape(64, LANES)
         second = r.vt[:, :, :, 1, :].reshape(64, LANES).astype(BF)
         mask = owner_masks(None)
+        turned = [first] + [pltpu.roll(first, LANES - 12 * row, 1) for row in range(1, 8)]
+        t = mm_nt(jnp.concatenate(turned, 0).astype(BF), lane_picks(0)).reshape(8, 64, WIDTH)
         for row in range(8):
-            t = mm_nt(first, lane_picks(row))
-            r.vec[row:row + 1, :] = jnp.sum(jnp.where(mask, t, 0.0), 0, keepdims=True)
+            r.vec[row:row + 1, :] = jnp.sum(jnp.where(mask, t[row], 0.0), 0, keepdims=True)
         t = mm_nt(second, lane_picks(None))
         for j in range(4):
             r.vec[8 + j:9 + j, :] = jnp.sum(jnp.where(owner_masks(j), t, 0.0), 0, keepdims=True)
@@ -597,17 +610,23 @@
             src = grads[phase].at[slices(phase, here.core, box, chain[0])[:5]]
             dst = r.rk.at[phase, pl.ds(at, n)].reshape(src.shape)
             at5 = (slice(None),) * 5 + (pl.ds(chain[1], chain[2]), pl.ds(chain[0] * LANES, LANES))
-            remote(src.at[at5], dst.at[at5], r.gsend.at[phase, c, slot], r.grecv.at[phase, c, slot], there).start()
+            remote(src.at[at5], dst.at[at5], r.gsend.at[FIRST[phase] + c, slot], r.grecv.at[FIRST[phase] + c, slot], there).start()
             return at + n
 
         if step == 1:
             for slot, there in enumerate(trio(here, order)):
                 send(boxes(there, ())[0], 28 + slot, slot, there)
             return
+        if phase == 0 and step == 3:
+            for i, there in enumerate(trio(here, order[2:])):
+                at = 16 + 4 * i
+                for box in boxes(there, order[:2]):
+                    at = send(box, at, 3 + i, there)
+            return
         there = hop(here, order[step])
         at = START[1 << step]
         for box in boxes(there, order[:step]):
-            at = send(box, at, step + 1, there)
+            at = send(box, at, step + 2, there)
 
     def landing(phase, c, at, n):
         part, row, rows, _ = CHAINS[phase][c]
@@ -621,14 +640,28 @@
             total = g[where].astype(F32)
             for slot in range(3):
                 view = landing(phase, c, 28 + slot, 1)
-                pltpu.make_async_copy(view, view, r.grecv.at[phase, c, slot]).wait()
+                pltpu.make_async_copy(view, view, r.grecv.at[FIRST[phase] + c, slot]).wait()
                 total = total + view[...].astype(F32).reshape(total.shape)
             g[where] = total.astype(BF)
+            return
+        if phase == 0 and step == 3:
+            for i in range(3):
+                view = landing(phase, c, 16 + 4 * i, 4)
+                pltpu.make_async_copy(view, view, r.grecv.at[FIRST[phase] + c, 3 + i]).wait()
+            at = 16
+            for box in boxes(here, chain[3][:2]):
+                m = box_count(box)
+                where = unit_slices(phase, box, chain)
+                total = g[where].astype(F32)
+                for i in range(3):
+                    total = total + landing(phase, c, at + 4 * i, m)[...].astype(F32).reshape(total.shape)
+                g[where] = total.astype(BF)
+                at += m
             return
         n = 1 << step
         at = START[n]
         view = landing(phase, c, at, n)
-        pltpu.make_async_copy(view, view, r.grecv.at[phase, c, step + 1]).wait()
+        pltpu.make_async_copy(view, view, r.grecv.at[FIRST[phase] + c, step + 2]).wait()
         for box in boxes(here, chain[3][:step]):
             m = box_count(box)
             where = unit_slices(phase, box, chain)
@@ -648,7 +681,7 @@
     def move(phase, c, step):
         hop_add(phase, c, step)
         if step > 1:
-            hop_start(phase, c, step - 1)
+            hop_start(phase, c, 1 if phase == 0 and step == 3 else step - 1)
 
     def reduce(phase, step):
         for part in range(PARTS):
@@ -668,24 +701,30 @@
     def gmate_copy(which, k):
         others = mates(here)
         there = (others + [twin] + [hop(mate, X2) for mate in others])[k]
-        return remote(r.stage.at[which, member_of(there)], r.final.at[which, k // 3 if k < 6 else 1, me],
+        cols = (pl.ds(0, 512), pl.ds(0, WIDTH), pl.ds(512, 256))[which]
+        phase = which % 2
+        return remote(r.stage.at[phase, member_of(there), :, cols], r.final.at[phase, k // 3 if k < 6 else 1, me, :, cols],
                       r.gmate_send.at[which, k], r.gmate_recv.at[which, k], there)
 
-    def hand_over(phase):
-        r.tall[...] = grads[phase][own_at(phase)].astype(F32)
+    def hand_over(which):
+        phase = which % 2
+        cols = (slice(0, 512), slice(0, WIDTH), slice(512, WIDTH))[which]
+        r.tall[:, cols] = grads[phase][own_at(phase) + (slice(None), cols)].astype(F32)
         for i in range(4):
-            r.stage[phase, i, 0:12, :] = r.tall[12 * i:12 * i + 12, :].astype(BF)
+            r.stage[phase, i, 0:12, cols] = r.tall[12 * i:12 * i + 12, cols].astype(BF)
         for k in range(7):
-            gmate_copy(phase, k).start()
-
-    def deliver(phase):
+            gmate_copy(which, k).start()
+
+    def deliver(which):
+        phase = which % 2
+        cols = (slice(0, 512), slice(0, WIDTH), slice(512, WIDTH))[which]
         for k in range(7):
-            gmate_copy(phase, k).wait()
-        r.final[phase, 0, me] = r.stage[phase, me]
+            gmate_copy(which, k).wait()
+        r.final[phase, 0, me, :, cols] = r.stage[phase, me, :, cols]
         for i in range(4):
-            cols = pl.ds(i * WIDTH, WIDTH)
-            dst = oup.at[:, cols] if phase else (oqkv.at[:, cols] if i < 3 else oout)
-            dst[...] = r.final[phase, 0, i, 0:12, :].astype(F32) + r.final[phase, 1, i, 0:12, :].astype(F32)
+            at = slice(i * WIDTH + cols.start, i * WIDTH + cols.stop)
+            dst = oup.at[:, at] if phase else (oqkv.at[:, at] if i < 3 else oout.at[:, cols])
+            dst[...] = r.final[phase, 0, i, 0:12, cols].astype(F32) + r.final[phase, 1, i, 0:12, cols].astype(F32)
 
     def deliver_down():
         rep_copy().wait()
@@ -693,29 +732,30 @@
 
     def reduce_sent(phase):
         for c in range(len(CHAINS[phase])):
-            for slot, n in enumerate((1, 1, 1, 4, 8, 16)):
+            for slot, n in enumerate((1, 1, 1, 4, 4, 4, 16) if phase == 0 else (1, 1, 1, 0, 4, 8, 16)):
+                if n == 0:
+                    continue
                 view = landing(phase, c, 0, n)
-                pltpu.make_async_copy(view, view, r.gsend.at[phase, c, slot]).wait()
-
-    def pack_rows(rows):
-        mask = owner_masks(None)
-        first = jnp.zeros((64, LANES), F32)
-        for row in rows:
-            value = jnp.where(mask, jnp.broadcast_to(r.gvec[row:row + 1, :], (64, WIDTH)), 0.0)
-            picks = lane_picks(row)
-            for piece in split3(value):
-                first = first + mm(piece, picks)
-        return first.reshape(4, 2, 8, LANES)
+                pltpu.make_async_copy(view, view, r.gsend.at[FIRST[phase] + c, slot]).wait()
+
+    def pack_rows(first, count):
+        mask = owner_masks(None).astype(F32).astype(BF)
+        pieces = split3(r.gvec[first:first + count, :])
+        spread = [piece[i:i + 1, :] * mask for piece in pieces for i in range(count)]
+        out = mm(jnp.concatenate(spread, 0), lane_picks(0)).reshape(3, count, 64, LANES)
+        out = out[0] + out[1] + out[2]
+        total = out[0] if first == 0 else pltpu.roll(out[0], 12 * first, 1)
+        for i in range(1, count):
+            total = total + pltpu.roll(out[i], 12 * (first + i), 1)
+        return total.reshape(4, 2, 8, LANES)
 
     def pack():
-        second = jnp.zeros((64, LANES), F32)
-        picks = lane_picks(None)
-        for j in range(4):
-            value = jnp.where(owner_masks(j), jnp.broadcast_to(r.gvec[8 + j:9 + j, :], (64, WIDTH)), 0.0)
-            for piece in split3(value):
-                second = second + mm(piece, picks)
-        r.gv[:, :, :, 0, :] = pack_rows((VO, VAG, VAS, VD, VFG, VFS))
-        r.gv[:, :, :, 1, :] = second.reshape(4, 2, 8, LANES)
+        pieces = split3(r.gvec[8:12, :])
+        masks = [owner_masks(j).astype(F32).astype(BF) for j in range(4)]
+        spread = [piece[j:j + 1, :] * masks[j] for piece in pieces for j in range(4)]
+        out = mm(jnp.concatenate(spread, 0), lane_picks(None)).reshape(12, 64, LANES)
+        r.gv[:, :, :, 0, :] = pack_rows(2, 6)
+        r.gv[:, :, :, 1, :] = jnp.sum(out, 0).reshape(4, 2, 8, LANES)
 
     def gvec_copies(k):
         if k == 0:
@@ -742,10 +782,13 @@
 
     near = [hop(here, link) for link in (Y1, Y3, Z1, Z3, X1, X3, CORE, X2, Y2, Z2)]
     near += [mates(here)[2], hop(hop(here, Y3), Z1), hop(hop(here, Y1), Z3)]
-    near += [hop(mate, X2) for mate in mates(here)] + [hop(hop(here, Z3), X1)]
+    near += [hop(mate, X2) for mate in mates(here)]
+    near += [hop(hop(here, a), c) for a, c in ((Z3, X1), (X1, Z1), (X3, Y3), (X3, Y1))]
     loads = [pltpu.make_async_copy(src, dst, r.loads.at[i]) for i, (src, dst) in enumerate((
         (qkv_in, r.qkv_in), (out_in, r.out_in), (up_in, r.up_in), (down_in, weights[2].at[own_at(2)]), (x_in, r.x)))]
-    for load in loads:
+    held = [getattr(r, name) for name in VECTORS] + [r.v8]
+    vec_loads = [pltpu.make_async_copy(src, dst, r.loads.at[8 + i]) for i, (src, dst) in enumerate(zip(vecs_in, held))]
+    for load in loads[:4] + vec_loads + loads[4:]:
         load.start()
     barrier = pltpu.get_barrier_semaphore()
     for place in near:
@@ -753,11 +796,11 @@
     og_load = pltpu.make_async_copy(og_in, r.x, r.loads.at[5])
     own = vec_tile(here)
     r.vt[own] = jnp.zeros((2, LANES), F32)
+    for load in loads[:4] + vec_loads:
+        load.wait()
     for i in range(8):
-        r.vt[own + (slice(0, 1), slice(12 * i, 12 * i + 12))] = vecs_in[i][...].astype(F32)
-    r.vt[own + (slice(1, 2), slice(0, 48))] = vecs_in[8][...].astype(F32)
-    for load in loads[:4]:
-        load.wait()
+        r.vt[own + (slice(0, 1), slice(12 * i, 12 * i + 12))] = held[i][...].astype(F32)
+    r.vt[own + (slice(1, 2), slice(0, 48))] = held[8][...].astype(F32)
     for i in range(4):
         r.stage[0, i, 0:12, :] = r.qkv_in[:, i * WIDTH:(i + 1) * WIDTH] if i < 3 else r.out_in[...]
         r.stage[1, i, 0:12, :] = r.up_in[:, i * WIDTH:(i + 1) * WIDTH]
@@ -768,14 +811,14 @@
     for k in range(3):
         mate_copy(1, k).start()
     gather_first(2)
-    loads[4].wait()
-    b.xt[...] = r.x[...].T
     assemble(0)
     vec_wait(0)
     vec_start(1)
     gather_first(0)
     assemble(1)
     gather_first(1)
+    loads[4].wait()
+    b.xt[...] = r.x[...].T
     vec_wait(1)
     vec_start(2)
     gather(0, 2)
@@ -836,72 +879,71 @@
     lax.fori_loop(0, 2, up_body, 0)
     lax.fori_loop(0, 2, up_own, 0)
     layer.norm1_rows()
-    reduce_first(1)
     layer.out_grads()
     reduce(2, 4)
+    reduce_first(1)
     layer.out_back()
     pack()
     layer.attend_back(0)
     sib_copy(0, 0).start()
+    reduce(2, 3)
     layer.attend_back(1)
     sib_copy(0, 1).start()
-    reduce(1, 4)
     first_part(0)
     layer.attend_back(2)
     sib_copy(0, 2).start()
-    reduce(2, 3)
+    reduce(1, 4)
     first_part(1)
     layer.attend_back(3)
     sib_copy(0, 3).start()
-    reduce(1, 3)
+    reduce(2, 2)
     first_part(2)
+    move_part(0, 4)
     layer.attend_back(4)
     sib_copy(0, 4).start()
-    reduce(2, 2)
+    reduce(1, 3)
     first_part(3)
-    move_part(0, 4)
+    move_part(1, 4)
     layer.attend_back(5)
     sib_copy(0, 5).start()
     first_part(4)
-    r.gv[:, :, :, 0, :] = r.gv[:, :, :, 0, :] + pack_rows((VQ, VV))
+    r.gv[:, :, :, 0, :] = r.gv[:, :, :, 0, :] + pack_rows(VQ, 2)
     gvec_start(2)
-    move_part(1, 4)
+    reduce(2, 1)
+    rep_copy().start()
+    move_part(0, 3)
+    move_part(2, 4)
     layer.input_grad(0)
     first_part(5)
+    layer.input_grad(1)
     reduce(1, 2)
-    layer.input_grad(1)
-    move_part(2, 4)
-    move_part(0, 3)
+    move_part(3, 4)
     layer.input_grad(2)
     sgrad_store = pltpu.make_async_copy(b.second, sgrad_out, r.loads.at[7])
     sgrad_store.start()
-    reduce(2, 1)
-    rep_copy().start()
+    move_part(1, 3)
     move_part(4, 4)
     gvec_add(2)
     gvec_start(1)
-    move_part(3, 4)
+    move_part(2, 3)
     move_part(5, 4)
-    move_part(1, 3)
-    move_part(0, 2)
-    move_part(2, 3)
-    move_part(4, 3)
     reduce(1, 1)
     hand_over(1)
-    move_part(5, 3)
+    move_part(0, 1)
     move_part(3, 3)
-    move_part(1, 2)
-    move_part(2, 2)
-    move_part(4, 2)
+    move_part(4, 3)
     gvec_add(1)
     gvec_start(0)
-    move_part(3, 2)
-    move_part(5, 2)
+    move_part(1, 1)
     deliver_down()
-    for part in range(PARTS):
-        move_part(part, 1)
+    move_part(5, 3)
+    move_part(2, 1)
+    move_part(3, 1)
     hand_over(0)
+    move_part(4, 1)
     deliver(1)
+    move_part(5, 1)
+    hand_over(2)
     gvec_add(0)
     ovec[...] = r.gv[vec_tile(here)]
     for phase in range(1, 3):
@@ -911,6 +953,7 @@
     enc_store.wait()
     sgrad_store.wait()
     deliver(0)
+    deliver(2)
 
 
 def run_layer(lengths, vecs, qkv, out, up, down, x, og):
@@ -923,7 +966,7 @@
             jax.ShapeDtypeStruct((12, 3 * WIDTH), F32), jax.ShapeDtypeStruct((12, WIDTH), F32),
             jax.ShapeDtypeStruct((12, 4 * WIDTH), F32), jax.ShapeDtypeStruct((UNIT, WIDTH), F32), jax.ShapeDtypeStruct((2, LANES), F32),
         ],
-        in_specs=[pl.BlockSpec(memory_space=pltpu.SMEM)] + [vm] * 9 + [hb] * 6,
+        in_specs=[pl.BlockSpec(memory_space=pltpu.SMEM)] + [hb] * 15,
         out_specs=[hb, hb] + [vm] * 5,
         scratch_shapes=[pltpu.VMEM(s, d) for s, d in SCRATCH.values()] + [pltpu.VMEM(s, d) for s, d in BUFFERS.values()]
         + [pltpu.SemaphoreType.DMA(s) for s in SEMS.values()],
@@ -932,31 +975,36 @@
 
 
 def finish_kernel(*refs):
-    srcs, vec, dsts, vec_outs, held, sems = refs[:6], refs[6], refs[7:13], refs[13:22], refs[22:28], refs[28]
+    srcs, dsts, vec_outs, held, parts, sems = refs[:7], refs[7:13], refs[13:22], refs[22:29], refs[29:38], refs[38]
     loads = [pltpu.make_async_copy(src, mid, sems.at[0, i]) for i, (src, mid) in enumerate(zip(srcs, held))]
     stores = [pltpu.make_async_copy(mid, dst, sems.at[1, i]) for i, (mid, dst) in enumerate(zip(held, dsts))]
-    for load in loads:
+    vec_stores = [pltpu.make_async_copy(mid, dst, sems.at[1, 6 + i]) for i, (mid, dst) in enumerate(zip(parts, vec_outs))]
+    for load in loads[::-1]:
         load.start()
+    loads[6].wait()
+    vec = held[6]
     for i in range(8):
-        vec_outs[i][...] = vec[0:1, 12 * i:12 * i + 12]
-    vec_outs[8][...] = vec[1:2, 0:48]
-    for load, store in zip(loads, stores):
+        parts[i][...] = vec[0:1, 12 * i:12 * i + 12]
+    parts[8][...] = vec[1:2, 0:48]
+    for store in vec_stores:
+        store.start()
+    for load, store in list(zip(loads, stores))[::-1]:
         load.wait()
         store.start()
-    for store in stores:
+    for store in vec_stores + stores:
         store.wait()
 
 
 def finish(results):
-    vm = pl.BlockSpec(memory_space=pltpu.VMEM)
     hb = pl.BlockSpec(memory_space=pl.ANY)
+    small = [(1, n) for n in [12] * 8 + [48]]
     return pl.pallas_call(
         finish_kernel,
-        out_shape=[jax.ShapeDtypeStruct(a.shape, a.dtype) for a in results[:6]]
-        + [jax.ShapeDtypeStruct((1, n), F32) for n in [12] * 8 + [48]],
-        in_specs=[hb] * 6 + [vm],
-        out_specs=[hb] * 6 + [vm] * 9,
-        scratch_shapes=[pltpu.VMEM(a.shape, a.dtype) for a in results[:6]] + [pltpu.SemaphoreType.DMA((2, 6))],
+        out_shape=[jax.ShapeDtypeStruct(a.shape, a.dtype) for a in results[:6]] + [jax.ShapeDtypeStruct(n, F32) for n in small],
+        in_specs=[hb] * 7,
+        out_specs=[hb] * 15,
+        scratch_shapes=[pltpu.VMEM(a.shape, a.dtype) for a in results] + [pltpu.VMEM(n, F32) for n in small]
+        + [pltpu.SemaphoreType.DMA((2, 15))],
         compiler_params=pltpu.CompilerParams(vmem_limit_bytes=63 * 2**20),
     )(*results)
 

time: 135 us -> 127 us (0.941)
  Pallas kernels: 134 us -> 126 us
    pallas_call x1, Pallas kernels: 129 us -> 122 us  [run_layer(): pl.pallas_call(mega_kernel, out_shape=[jax.ShapeDtypeStruct((TOKENS, WIDT...]
where the time goes in v5:
time: 127 us
  Pallas kernels  126 us (99%)
    pallas_call x1, Pallas kernels, run_layer(): pl.pallas_call(mega_kernel, out_shape=[jax.ShapeDtypeStruct((TOKENS, WIDT...  122 us
    pallas_call x1, Pallas kernels, finish(): pl.pallas_call(finish_kernel, out_shape=[jax.ShapeDtypeStruct(a.shape, a....  3.38 us

profile of v5, /device:TPU:1, one launch (start us, length us, event | category | flops | bytes accessed | tf_op | source)
XLA Modules:
  0.0 126.5 jit_solution(8532130135925111963)
XLA Ops:
  0.7 122.3 %shard_map.271 = (bf16[512,768]{1,0:T(8,128)(2,1)}, f32[512,768]{1,0:T(8,128)}, f32[12,2304]{1,0:T(8,128)}, f32[12,768]{1,0:T(8,128)}, f32[12,3072]{1,0:T(8,128)}, /*index=5*/f32[48,768]{1,0:T(8,128)}, f32[2,128]{1,0:T(2,128)}) custom-call(s32[1,2]{1,0:T(1,128)} %bitcast.29, bf16[1,12]{1,0:T(2,128)(2,1)} %bitcast.30, bf16[1,12]{1,0:T(2,128)(2,1)} %bitcast.31, ...), custom_call_target="tpu_custom_call" | custom-call | tf_op jit(solution)/shard_map/pallas_call | solution.py:962
  123.0 3.4 %shard_map.272 = (bf16[512,768]{1,0:T(8,128)(2,1)}, f32[512,768]{1,0:T(8,128)}, f32[12,2304]{1,0:T(8,128)}, f32[12,768]{1,0:T(8,128)}, f32[12,3072]{1,0:T(8,128)...) custom-call(bf16[512,768]{1,0:T(8,128)(2,1)} %get-tuple-element.37.r, ...), custom_call_target="tpu_custom_call" | custom-call | tf_op jit(solution)/shard_map/pallas_call | solution.py:1001

commit v6 on v5

--- a/solution.py
+++ b/solution.py
@@ -137,7 +137,7 @@
 HALF = 256
 SEQ = 256
 TOKENS = 512
-ROWS = 64
+ROWS = 128
 epsilon = 1e-05
 NT = (((1,), (1,)), ((), ()))
 TN = (((0,), (0,)), ((), ()))
@@ -191,18 +191,13 @@
     def v(self, row):
         return self.vec[row:row + 1, :]
 
-    def project(self, j):
-        b = self.b
-        dst, row = ((b.q, VQ), (b.k, None), (b.v, VV))[j]
-        for n in range(3):
-            cols = slice(n * 256, n * 256 + 256)
-            acc = mm(self.x[...], self.slabs[0].at[j][:, cols])
-            if row is not None:
-                acc = acc + self.vec[row:row + 1, cols]
-            low = acc.astype(BF)
-            if j == 0:
-                low = (low.astype(F32) * 0.125).astype(BF)
-            dst[:, cols] = low
+    def project(self, n):
+        b = self.b
+        cols = slice(n * 256, n * 256 + 256)
+        x = self.x[...]
+        b.q[:, cols] = ((mm(x, self.slabs[0].at[0][:, cols]) + self.vec[VQ:VQ + 1, cols]).astype(BF).astype(F32) * 0.125).astype(BF)
+        b.k[:, cols] = mm(x, self.slabs[0].at[1][:, cols]).astype(BF)
+        b.v[:, cols] = (mm(x, self.slabs[0].at[2][:, cols]) + self.vec[VV:VV + 1, cols]).astype(BF)
 
     def attend(self):
         b = self.b
@@ -377,9 +372,17 @@
             b.gpre[1, rows[s], cols] = dk.astype(BF)
             dq = mm(jnp.concatenate([kt * tall[0], kt * tall[1]], 1), jnp.concatenate(low[s], 0))
             b.gpre[0, rows[s], cols] = (dq.T * 0.125).astype(BF)
-        both = mm(b.xt[...], jnp.concatenate([b.gpre[0, :, cols], b.gpre[1, :, cols]], 1))
-        self.grads[0][0, :, cols] = both[:, :LANES].astype(BF)
-        self.grads[0][1, :, cols] = both[:, LANES:].astype(BF)
+
+    def qkv_grads(self, start, count):
+        b = self.b
+        cols = slice(start, start + count)
+        if count == LANES:
+            both = mm(b.xt[...], jnp.concatenate([b.gpre[0, :, cols], b.gpre[1, :, cols]], 1))
+            self.grads[0][0, :, cols] = both[:, :LANES].astype(BF)
+            self.grads[0][1, :, cols] = both[:, LANES:].astype(BF)
+        else:
+            self.grads[0][0, :, cols] = mm(b.xt[...], b.gpre[0, :, cols]).astype(BF)
+            self.grads[0][1, :, cols] = mm(b.xt[...], b.gpre[1, :, cols]).astype(BF)
         self.grads[0][2, :, cols] = mm(b.xt[...], b.gpre[2, :, cols]).astype(BF)
         self.gvec[VQ:VQ + 1, cols] = column_total(b.gpre[0, :, cols])
         self.gvec[VV:VV + 1, cols] = column_total(b.gpre[2, :, cols])
@@ -402,10 +405,15 @@
 
 
 START = {16: 0, 8: 16, 4: 24}
-WHOLE = tuple((part, 0, UNIT, ORDERS[part]) for part in range(PARTS))
-CUT = tuple((i // 3, 16 * (i % 3), 16, ORDERS[i % 6]) for i in range(3 * PARTS))
+WHOLE = tuple((part, part * LANES, LANES, 0, UNIT, ORDERS[part]) for part in range(PARTS))
+STRIPS = (
+    ((Z1, Z3, Y1, Y3, X1), (Z1, Z3, X1, Y1, Y3), (Y1, Y3, X3, Z3, Z1)),
+    ((Y1, Y3, Z1, Z3, X3), (Z1, Z3, X1, Y3, Y1), (Y1, Y3, X3, Z1, Z3)),
+)
+COLUMNS = ((0, 256), (256, 256), (512, LANES), (640, LANES))
+CUT = tuple((part,) + COLUMNS[part] + (16 * i, 16, STRIPS[part % 2][i]) for part in range(4) for i in range(3))
 CHAINS = (CUT, WHOLE, WHOLE)
-FIRST = (0, 18, 24)
+FIRST = (0, 12, 18)
 EVERY = ((0, 2), (0, 4), (0, 2), (0, 2))
 VECTORS = "v0 v1 v2 v3".split() + "v4 v5 v6 v7".split()
 SCRATCH = dict(
@@ -422,7 +430,7 @@
 SEMS = dict(
     loads=(17,), mate_send=(2, 3), mate_recv=(2, 3), send=(3, PARTS, 7), recv=(3, PARTS, 7),
     sib_send=(3, PARTS), sib_recv=(3, PARTS), vsend=(9,), vrecv=(9,),
-    gsib_send=(3, PARTS), gsib_recv=(3, PARTS), gsend=(30, 7), grecv=(30, 7),
+    gsib_send=(3, PARTS), gsib_recv=(3, PARTS), gsend=(24, 7), grecv=(24, 7),
     rep_send=(1,), rep_recv=(1,), gmate_send=(3, 7), gmate_recv=(3, 7), gvsend=(13,), gvrecv=(13,),
 )
 
@@ -526,8 +534,8 @@
             wait_units(weights[phase], phase, 8, part, r.recv.at[phase, part, 5 + half])
             share(phase, part, halves(boxes(hop(here, order[4]), order[:4]))[half])
 
-    def gathered(phase):
-        for part in range(PARTS):
+    def gathered(phase, parts=range(PARTS)):
+        for part in parts:
             wait_units(weights[phase], phase, 32, part, r.sib_recv.at[phase, part])
 
     def gather_sent(phase):
@@ -575,7 +583,7 @@
     def sib_copy(phase, k):
         g, rd = grads[phase], rds[phase]
         if phase == 0:
-            cols = pl.ds(k * LANES, LANES)
+            cols = pl.ds(*COLUMNS[k])
             src = g.at[:, pl.ds(sibling.core, 1), :, :, :, :, cols]
             dst = rd.at[:, :, :, :, :, :, cols]
         elif phase == 1:
@@ -589,8 +597,9 @@
         g, rd = grads[phase], rds[phase]
         for i in range(4):
             if phase == 0:
-                at = slices(0, here.core, ((0, 2), (i, 1), (0, 2), (0, 2)), k)
-                g[at] = g[at] + rd[slices(0, 0, ((0, 2), (i, 1), (0, 2), (0, 2)), k)]
+                cols = slice(COLUMNS[k][0], sum(COLUMNS[k]))
+                at = (slice(None), pl.ds(here.core, 1), i, slice(None), slice(None), slice(None), cols)
+                g[at] = g[at] + rd[:, :, i, :, :, :, cols]
             elif phase == 1:
                 g[k, here.core, i] = g[k, here.core, i] + rd[k, 0, i]
             else:
@@ -598,18 +607,18 @@
                 g[at] = g[at] + rd[k, i // 2, i % 2]
 
     def unit_slices(phase, box, chain):
-        part, row, rows, _ = chain
-        return slices(phase, here.core, box, part)[:5] + (slice(row, row + rows), slice(part * LANES, part * LANES + LANES))
+        _, col, cols, row, rows, _ = chain
+        return slices(phase, here.core, box, 0)[:5] + (slice(row, row + rows), slice(col, col + cols))
 
     def hop_start(phase, c, step):
         chain = CHAINS[phase][c]
-        order = chain[3]
+        _, col, cols, row, rows, order = chain
 
         def send(box, at, slot, there):
             n = box_count(box)
-            src = grads[phase].at[slices(phase, here.core, box, chain[0])[:5]]
+            src = grads[phase].at[slices(phase, here.core, box, 0)[:5]]
             dst = r.rk.at[phase, pl.ds(at, n)].reshape(src.shape)
-            at5 = (slice(None),) * 5 + (pl.ds(chain[1], chain[2]), pl.ds(chain[0] * LANES, LANES))
+            at5 = (slice(None),) * 5 + (pl.ds(row, rows), pl.ds(col, cols))
             remote(src.at[at5], dst.at[at5], r.gsend.at[FIRST[phase] + c, slot], r.grecv.at[FIRST[phase] + c, slot], there).start()
             return at + n
 
@@ -629,8 +638,8 @@
             at = send(box, at, step + 2, there)
 
     def landing(phase, c, at, n):
-        part, row, rows, _ = CHAINS[phase][c]
-        return r.rk.at[phase, pl.ds(at, n), pl.ds(row, rows), pl.ds(part * LANES, LANES)]
+        _, col, cols, row, rows, _ = CHAINS[phase][c]
+        return r.rk.at[phase, pl.ds(at, n), pl.ds(row, rows), pl.ds(col, cols)]
 
     def hop_add(phase, c, step):
         g = grads[phase]
@@ -649,7 +658,7 @@
                 view = landing(phase, c, 16 + 4 * i, 4)
                 pltpu.make_async_copy(view, view, r.grecv.at[FIRST[phase] + c, 3 + i]).wait()
             at = 16
-            for box in boxes(here, chain[3][:2]):
+            for box in boxes(here, chain[5][:2]):
                 m = box_count(box)
                 where = unit_slices(phase, box, chain)
                 total = g[where].astype(F32)
@@ -662,7 +671,7 @@
         at = START[n]
         view = landing(phase, c, at, n)
         pltpu.make_async_copy(view, view, r.grecv.at[FIRST[phase] + c, step + 2]).wait()
-        for box in boxes(here, chain[3][:step]):
+        for box in boxes(here, chain[5][:step]):
             m = box_count(box)
             where = unit_slices(phase, box, chain)
             old = g[where]
@@ -783,7 +792,7 @@
     near = [hop(here, link) for link in (Y1, Y3, Z1, Z3, X1, X3, CORE, X2, Y2, Z2)]
     near += [mates(here)[2], hop(hop(here, Y3), Z1), hop(hop(here, Y1), Z3)]
     near += [hop(mate, X2) for mate in mates(here)]
-    near += [hop(hop(here, a), c) for a, c in ((Z3, X1), (X1, Z1), (X3, Y3), (X3, Y1))]
+    near += [hop(hop(here, a), c) for a, c in ((Z3, X1), (X1, Y1), (X1, Y3), (X3, Z1), (X3, Z3))]
     loads = [pltpu.make_async_copy(src, dst, r.loads.at[i]) for i, (src, dst) in enumerate((
         (qkv_in, r.qkv_in), (out_in, r.out_in), (up_in, r.up_in), (down_in, weights[2].at[own_at(2)]), (x_in, r.x)))]
     held = [getattr(r, name) for name in VECTORS] + [r.v8]
@@ -832,11 +841,11 @@
     gather(2, 3)
     gather_last(0, 0)
     gather_last(0, 1)
-    gathered(0)
-    layer.project(0)
-    gather(1, 4)
-    layer.project(1)
-    layer.project(2)
+    for n in range(3):
+        gathered(0, (2 * n, 2 * n + 1))
+        layer.project(n)
+        if n == 0:
+            gather(1, 4)
     gather(2, 4)
     layer.attend()
     gather_last(1, 0)
@@ -885,65 +894,59 @@
     layer.out_back()
     pack()
     layer.attend_back(0)
+    layer.attend_back(1)
+    layer.qkv_grads(*COLUMNS[0])
     sib_copy(0, 0).start()
     reduce(2, 3)
-    layer.attend_back(1)
+    layer.attend_back(2)
+    first_part(0)
+    layer.attend_back(3)
+    layer.qkv_grads(*COLUMNS[1])
     sib_copy(0, 1).start()
-    first_part(0)
-    layer.attend_back(2)
+    reduce(1, 4)
+    layer.attend_back(4)
+    layer.qkv_grads(*COLUMNS[2])
     sib_copy(0, 2).start()
-    reduce(1, 4)
     first_part(1)
-    layer.attend_back(3)
+    move_part(0, 4)
+    reduce(2, 2)
+    layer.attend_back(5)
+    layer.qkv_grads(*COLUMNS[3])
     sib_copy(0, 3).start()
-    reduce(2, 2)
     first_part(2)
-    move_part(0, 4)
-    layer.attend_back(4)
-    sib_copy(0, 4).start()
     reduce(1, 3)
+    layer.input_grad(0)
+    layer.input_grad(1)
     first_part(3)
-    move_part(1, 4)
-    layer.attend_back(5)
-    sib_copy(0, 5).start()
-    first_part(4)
     r.gv[:, :, :, 0, :] = r.gv[:, :, :, 0, :] + pack_rows(VQ, 2)
     gvec_start(2)
-    reduce(2, 1)
-    rep_copy().start()
+    move_part(1, 4)
     move_part(0, 3)
-    move_part(2, 4)
-    layer.input_grad(0)
-    first_part(5)
-    layer.input_grad(1)
-    reduce(1, 2)
-    move_part(3, 4)
     layer.input_grad(2)
     sgrad_store = pltpu.make_async_copy(b.second, sgrad_out, r.loads.at[7])
     sgrad_store.start()
-    move_part(1, 3)
-    move_part(4, 4)
+    reduce(1, 2)
+    move_part(2, 4)
     gvec_add(2)
     gvec_start(1)
-    move_part(2, 3)
-    move_part(5, 4)
+    reduce(2, 1)
+    rep_copy().start()
+    move_part(3, 4)
     reduce(1, 1)
     hand_over(1)
     move_part(0, 1)
-    move_part(3, 3)
-    move_part(4, 3)
+    move_part(1, 3)
+    move_part(2, 3)
     gvec_add(1)
     gvec_start(0)
+    move_part(3, 3)
+    deliver_down()
     move_part(1, 1)
-    deliver_down()
-    move_part(5, 3)
+    hand_over(0)
     move_part(2, 1)
     move_part(3, 1)
-    hand_over(0)
-    move_part(4, 1)
+    hand_over(2)
     deliver(1)
-    move_part(5, 1)
-    hand_over(2)
     gvec_add(0)
     ovec[...] = r.gv[vec_tile(here)]
     for phase in range(1, 3):

time: 127 us -> 124 us (0.976)
  Pallas kernels: 126 us -> 123 us
    pallas_call x1, Pallas kernels: 122 us -> 120 us  [run_layer(): pl.pallas_call(mega_kernel, out_shape=[jax.ShapeDtypeStruct((TOKENS, WIDT...]
where the time goes in v6:
time: 124 us
  Pallas kernels  123 us (99%)
    pallas_call x1, Pallas kernels, run_layer(): pl.pallas_call(mega_kernel, out_shape=[jax.ShapeDtypeStruct((TOKENS, WIDT...  120 us
    pallas_call x1, Pallas kernels, finish(): pl.pallas_call(finish_kernel, out_shape=[jax.ShapeDtypeStruct(a.shape, a....  3.38 us

profile of v6, /device:TPU:1, one launch (start us, length us, event | category | flops | bytes accessed | tf_op | source)
XLA Modules:
  0.0 124.2 jit_solution(5229715352554994617)
XLA Ops:
  0.7 119.9 %shard_map.271 = (bf16[512,768]{1,0:T(8,128)(2,1)}, f32[512,768]{1,0:T(8,128)}, f32[12,2304]{1,0:T(8,128)}, f32[12,768]{1,0:T(8,128)}, f32[12,3072]{1,0:T(8,128)}, /*index=5*/f32[48,768]{1,0:T(8,128)}, f32[2,128]{1,0:T(2,128)}) custom-call(s32[1,2]{1,0:T(1,128)} %bitcast.29, bf16[1,12]{1,0:T(2,128)(2,1)} %bitcast.30, bf16[1,12]{1,0:T(2,128)(2,1)} %bitcast.31, ...), custom_call_target="tpu_custom_call" | custom-call | tf_op jit(solution)/shard_map/pallas_call | solution.py:965
  120.6 3.4 %shard_map.272 = (bf16[512,768]{1,0:T(8,128)(2,1)}, f32[512,768]{1,0:T(8,128)}, f32[12,2304]{1,0:T(8,128)}, f32[12,768]{1,0:T(8,128)}, f32[12,3072]{1,0:T(8,128)...) custom-call(bf16[512,768]{1,0:T(8,128)(2,1)} %get-tuple-element.37.r, ...), custom_call_target="tpu_custom_call" | custom-call | tf_op jit(solution)/shard_map/pallas_call | solution.py:1004

commit v7 on v6

--- a/solution.py
+++ b/solution.py
@@ -428,9 +428,9 @@
     **{name: ((1, 12), BF) for name in VECTORS}, v8=((1, 48), BF),
 )
 SEMS = dict(
-    loads=(17,), mate_send=(2, 3), mate_recv=(2, 3), send=(3, PARTS, 7), recv=(3, PARTS, 7),
-    sib_send=(3, PARTS), sib_recv=(3, PARTS), vsend=(9,), vrecv=(9,),
-    gsib_send=(3, PARTS), gsib_recv=(3, PARTS), gsend=(24, 7), grecv=(24, 7),
+    loads=(17,), mate_send=(2, 3), mate_recv=(2, 3), send=(3,), recv=(3, PARTS, 7),
+    sib_send=(3,), sib_recv=(3, PARTS), vsend=(9,), vrecv=(9,),
+    gsib_send=(3, PARTS), gsib_recv=(3, PARTS), gsend=(3,), grecv=(24, 7),
     rep_send=(1,), rep_recv=(1,), gmate_send=(3, 7), gmate_recv=(3, 7), gvsend=(13,), gvrecv=(13,),
 )
 
@@ -498,13 +498,13 @@
         w = weights[phase]
         for box in found:
             view = w.at[slices(phase, here.core, box, part)]
-            remote(view, view, r.send.at[phase, part, slot], r.recv.at[phase, part, slot], there).start()
+            remote(view, view, r.send.at[phase], r.recv.at[phase, part, slot], there).start()
 
     def share(phase, part, found):
         w = weights[phase]
         for box in found:
             view = w.at[slices(phase, here.core, box, part)]
-            remote(view, view, r.sib_send.at[phase, part], r.sib_recv.at[phase, part], sibling).start()
+            remote(view, view, r.sib_send.at[phase], r.sib_recv.at[phase, part], sibling).start()
 
     def gather_first(phase):
         for part in range(PARTS):
@@ -538,11 +538,13 @@
         for part in parts:
             wait_units(weights[phase], phase, 32, part, r.sib_recv.at[phase, part])
 
+    def wait_bytes(phase, units, sem):
+        view = weights[phase].reshape((64, UNIT, WIDTH)).at[pl.ds(0, units)]
+        pltpu.make_async_copy(view, view, sem).wait()
+
     def gather_sent(phase):
-        for part in range(PARTS):
-            wait_units(weights[phase], phase, 32, part, r.sib_send.at[phase, part])
-            for slot, n in enumerate((1, 1, 1, 4, 8, 8, 8)):
-                wait_units(weights[phase], phase, n, part, r.send.at[phase, part, slot])
+        wait_bytes(phase, 32, r.sib_send.at[phase])
+        wait_bytes(phase, 31, r.send.at[phase])
 
     def vec_tile(place):
         return (place.z, place.x % 2, place.y * 2 + place.core)
@@ -619,7 +621,7 @@
             src = grads[phase].at[slices(phase, here.core, box, 0)[:5]]
             dst = r.rk.at[phase, pl.ds(at, n)].reshape(src.shape)
             at5 = (slice(None),) * 5 + (pl.ds(row, rows), pl.ds(col, cols))
-            remote(src.at[at5], dst.at[at5], r.gsend.at[FIRST[phase] + c, slot], r.grecv.at[FIRST[phase] + c, slot], there).start()
+            remote(src.at[at5], dst.at[at5], r.gsend.at[phase], r.grecv.at[FIRST[phase] + c, slot], there).start()
             return at + n
 
         if step == 1:
@@ -740,12 +742,7 @@
         odown[...] = grads[2][own_at(2)].astype(F32) + r.rx[...].astype(F32)
 
     def reduce_sent(phase):
-        for c in range(len(CHAINS[phase])):
-            for slot, n in enumerate((1, 1, 1, 4, 4, 4, 16) if phase == 0 else (1, 1, 1, 0, 4, 8, 16)):
-                if n == 0:
-                    continue
-                view = landing(phase, c, 0, n)
-                pltpu.make_async_copy(view, view, r.gsend.at[FIRST[phase] + c, slot]).wait()
+        wait_bytes(phase, 31, r.gsend.at[phase])
 
     def pack_rows(first, count):
         mask = owner_masks(None).astype(F32).astype(BF)

time: 124 us -> 122 us (0.984)
  Pallas kernels: 123 us -> 121 us
    pallas_call x1, Pallas kernels: 120 us -> 117 us  [run_layer(): pl.pallas_call(mega_kernel, out_shape=[jax.ShapeDtypeStruct((TOKENS, WIDT...]
where the time goes in v7:
time: 122 us; the launch traced here: 121 us
  Pallas kernels  121 us (99%)
    pallas_call x1, Pallas kernels, run_layer(): pl.pallas_call(mega_kernel, out_shape=[jax.ShapeDtypeStruct((TOKENS, WIDT...  117 us
    pallas_call x1, Pallas kernels, finish(): pl.pallas_call(finish_kernel, out_shape=[jax.ShapeDtypeStruct(a.shape, a....  3.38 us

profile of v7, /device:TPU:1, one launch (start us, length us, event | category | flops | bytes accessed | tf_op | source)
XLA Modules:
  0.0 121.4 jit_solution(4770019828462013367)
XLA Ops:
  0.7 117.1 %shard_map.271 = (bf16[512,768]{1,0:T(8,128)(2,1)}, f32[512,768]{1,0:T(8,128)}, f32[12,2304]{1,0:T(8,128)}, f32[12,768]{1,0:T(8,128)}, f32[12,3072]{1,0:T(8,128)}, /*index=5*/f32[48,768]{1,0:T(8,128)}, f32[2,128]{1,0:T(2,128)}) custom-call(s32[1,2]{1,0:T(1,128)} %bitcast.29, bf16[1,12]{1,0:T(2,128)(2,1)} %bitcast.30, bf16[1,12]{1,0:T(2,128)(2,1)} %bitcast.31, ...), custom_call_target="tpu_custom_call" | custom-call | tf_op jit(solution)/shard_map/pallas_call | solution.py:962
  117.8 3.4 %shard_map.272 = (bf16[512,768]{1,0:T(8,128)(2,1)}, f32[512,768]{1,0:T(8,128)}, f32[12,2304]{1,0:T(8,128)}, f32[12,768]{1,0:T(8,128)}, f32[12,3072]{1,0:T(8,128)...) custom-call(bf16[512,768]{1,0:T(8,128)(2,1)} %get-tuple-element.37.r, ...), custom_call_target="tpu_custom_call" | custom-call | tf_op jit(solution)/shard_map/pallas_call | solution.py:1001

commit v8 on v7

--- a/solution.py
+++ b/solution.py
@@ -911,10 +911,10 @@
     layer.qkv_grads(*COLUMNS[3])
     sib_copy(0, 3).start()
     first_part(2)
-    reduce(1, 3)
     layer.input_grad(0)
     layer.input_grad(1)
     first_part(3)
+    reduce(1, 3)
     r.gv[:, :, :, 0, :] = r.gv[:, :, :, 0, :] + pack_rows(VQ, 2)
     gvec_start(2)
     move_part(1, 4)

time: 122 us -> 121 us (level)
  no operation moved by 1% of the time
where the time goes in v8:
time: 121 us
  Pallas kernels  120 us (99%)
    pallas_call x1, Pallas kernels, run_layer(): pl.pallas_call(mega_kernel, out_shape=[jax.ShapeDtypeStruct((TOKENS, WIDT...  117 us
    pallas_call x1, Pallas kernels, finish(): pl.pallas_call(finish_kernel, out_shape=[jax.ShapeDtypeStruct(a.shape, a....  3.38 us

profile of v8, /device:TPU:1, one launch (start us, length us, event | category | flops | bytes accessed | tf_op | source)
XLA Modules:
  0.0 120.9 jit_solution(14475188464310671824)
XLA Ops:
  0.7 116.6 %shard_map.271 = (bf16[512,768]{1,0:T(8,128)(2,1)}, f32[512,768]{1,0:T(8,128)}, f32[12,2304]{1,0:T(8,128)}, f32[12,768]{1,0:T(8,128)}, f32[12,3072]{1,0:T(8,128)}, /*index=5*/f32[48,768]{1,0:T(8,128)}, f32[2,128]{1,0:T(2,128)}) custom-call(s32[1,2]{1,0:T(1,128)} %bitcast.29, bf16[1,12]{1,0:T(2,128)(2,1)} %bitcast.30, bf16[1,12]{1,0:T(2,128)(2,1)} %bitcast.31, ...), custom_call_target="tpu_custom_call" | custom-call | tf_op jit(solution)/shard_map/pallas_call | solution.py:962
  117.3 3.4 %shard_map.272 = (bf16[512,768]{1,0:T(8,128)(2,1)}, f32[512,768]{1,0:T(8,128)}, f32[12,2304]{1,0:T(8,128)}, f32[12,768]{1,0:T(8,128)}, f32[12,3072]{1,0:T(8,128)...) custom-call(bf16[512,768]{1,0:T(8,128)(2,1)} %get-tuple-element.37.r, ...), custom_call_target="tpu_custom_call" | custom-call | tf_op jit(solution)/shard_map/pallas_call | solution.py:1001
